TPU v7x, 32 devices: a whole 2x2x4 slice. The times are simulated.
32 devices in a mesh: scen: 2 (over y), row: 4 (over x, core), col: 4 (over z).
Axes of the slice: x: 2, y: 2, z: 4, core: 2. Of those that a mesh axis runs over, the one named last changes fastest.
Arguments:
- tokens: bfloat16 [10240, 4096], P(('scen', 'row'), 'col'), parts along dimension 0, may hold values from -60 to 60
- norm_gain: float32 [4096], replicated, may hold values from 0.1 to 1.9
- w_in: bfloat16 [4096, 16384], P('row', 'col'), may hold values from -0.09375 to 0.09375
- conv_kernel: float32 [9, 16384], P(None, 'col'), may hold values from -2 to 2
- w_out: bfloat16 [16384, 4096], P('col', 'row'), may hold values from -0.0625 to 0.0625
Outputs:
- block_out: bfloat16 [10240, 4096], P(('scen', 'row'), 'col'), parts along dimension 0
There are 2 independent parts, one for each index of `scen`. A program takes and returns all parts, laid end to end along the dimension named above; an argument that names none is the same for every part. Nothing has to cross between parts.
All inputs are finite; a program needn't handle non-finite values.
Results may differ from a plain program's by a relative error of at most 0.0038.
Values may be sent and summed in bfloat16 or wider, within the bound.
No kernel may reach another device: no remote copies, remote signals or barrier semaphores. Data moves between devices by JAX's collectives and lax.ppermute only.
A program may use at most 192 MiB of HBM per device.

v0:
```python
import jax
import jax.numpy as jnp
from jax import lax
from jax.sharding import PartitionSpec as P

LAT = 40


eps = 1e-05


def extended(cells, sides, width):
    for axis, dim in sides:
        count = lax.axis_size(axis)
        head = lax.slice_in_dim(cells, 0, width, axis=dim)
        tail = lax.slice_in_dim(cells, cells.shape[dim] - width, cells.shape[dim], axis=dim)
        cells = jnp.concatenate(
            [
                lax.ppermute(tail, axis, [(i, (i + 1) % count) for i in range(count)]),
                cells,
                lax.ppermute(head, axis, [((i + 1) % count, i) for i in range(count)]),
            ],
            axis=dim,
        )
    return cells


def per_device(tokens, norm_gain, w_in, conv_kernel, w_out):
    rows, local_cols = tokens.shape
    values = tokens.astype(jnp.float32)
    whole = lax.all_gather(tokens, "col", axis=1, tiled=True).astype(jnp.float32)
    mean = jnp.mean(whole, axis=1, keepdims=True)
    var = jnp.mean(whole * whole, axis=1, keepdims=True) - mean * mean
    normed = ((whole - mean) * lax.rsqrt(var + eps) * norm_gain).astype(jnp.bfloat16)
    units = w_in.shape[1]
    pre_hidden = jnp.dot(
        normed, lax.all_gather(w_in, "row", axis=0, tiled=True), preferred_element_type=jnp.float32
    )
    hidden = pre_hidden.astype(jnp.bfloat16)
    lon_local = rows // LAT
    grid = hidden.reshape(lon_local, LAT, units)
    padded = extended(grid, (("row", 0),), 1)
    padded = jnp.pad(padded.astype(jnp.float32), ((0, 0), (1, 1), (0, 0)))
    conv = jnp.zeros((lon_local, LAT, units), jnp.float32)
    for shift_lon in range(3):
        for shift_lat in range(3):
            conv = (
                conv
                + conv_kernel[shift_lon * 3 + shift_lat]
                * padded[shift_lon : shift_lon + lon_local, shift_lat : shift_lat + LAT]
            )
    act = jax.nn.gelu(conv, approximate=True).astype(jnp.bfloat16).reshape(rows, units)
    partial_value = jnp.dot(
        act, lax.all_gather(w_out, "row", axis=1, tiled=True), preferred_element_type=jnp.float32
    )
    mixed = lax.psum_scatter(partial_value, "col", scatter_dimension=1, tiled=True)
    return (values + mixed).astype(jnp.bfloat16)


def solution(mesh):
    placed = (P(("scen", "row"), "col"), P(), P("row", "col"), P(None, "col"), P("col", "row"))
    return jax.shard_map(
        per_device, mesh=mesh, in_specs=placed, out_specs=P(("scen", "row"), "col"), check_vma=False
    )
```

profile of v0, /device:TPU:0, one launch (start us, length us, event | category | flops | bytes accessed | tf_op | source)
XLA Modules:
  0.0 1018.8 jit_solution(6760261650245805252)
XLA Ops:
  6.5 0.0 copy-start.2
  6.5 0.0 all-gather.4.cloned.1.call-start
  6.5 0.7 all-gather.4.cloned.1.call-update
  7.3 0.0 all-gather.6.cloned.1.call-start
  7.3 0.7 all-gather.6.cloned.1.call-update
  8.0 0.0 all-gather.8.cloned.1.call-start
  8.1 0.7 all-gather.8.cloned.1.call-update
  8.7 0.0 reduce-scatter.2.cloned.1.call-start
  8.8 186.8 %all-gather.4.cloned.1.call-done = bf16[1280,4096]{1,0:T(8,128)(2,1)} async-done(((bf16[1280,1024]{1,0:T(8,128)(2,1)}), bf16[1280,4096]{1,0:T(8,128)(2,1)}) %all-gather.4.cloned.1.call-update) | async-done | bytes 10485776 | tf_op jit(solution)/shard_map/all_gather | solution.py:31
  195.6 7.1 convert_reduce_fusion
  202.7 194.2 %all-gather.6.cloned.1.call-done = bf16[4096,4096]{1,0:T(8,128)(2,1)} async-done(((bf16[1024,4096]{1,0:T(8,128)(2,1)}), bf16[4096,4096]{1,0:T(8,128)(2,1)}) %all-gather.6.cloned.1.call-update) | async-done | bytes 33554448 | tf_op jit(solution)/shard_map/all_gather | solution.py:37
  396.9 0.0 copy-done.2
  396.9 0.0 copy-start.1
  396.9 51.2 %convolution_convert_fusion = bf16[1280,4096]{1,0:T(8,128)(2,1)S(1)} fusion(bf16[4096,4096]{1,0:T(8,128)(2,1)} %all-gather.6.cloned.1.call-done, bf16[1280,4096]{1,0:T(8,128)(2,1)} %all-gather.4.cloned.1.call-done, f32[4096]{0:T(1024)S(1)} %copy-done.2, f32[1280]{0:T(1024)S(1)} %get-tuple-element.19, f32[1280]{0:T(1024)S(1)} %get-tuple-element.18), kind=kOutput, calls=%fused_computation.39 | convolution fusion | flops 42981130240 | bytes 54552576 | tf_op jit(solution)/shard_map/dot_general | solution.py:36
  448.1 0.3 collective-permute-start
  448.4 1.5 collective-permute-start.1
  449.9 0.0 copy-done.1
  449.9 0.1 fusion.30
  450.0 14.9 %collective-permute-done = bf16[1,40,4096]{2,1,0:T(8,128)(2,1)S(1)} collective-permute-done((bf16[1,40,4096]{2,1,0:T(8,128)(2,1)S(1)}, bf16[1,40,4096]{2,1,0:T(8,128)(2,1)S(1)}, u32[]{:S(2)}, u32[]{:S(2)}) %collective-permute-start) | collective-permute-done | bytes 327712 | tf_op jit(solution)/shard_map/ppermute | solution.py:19
  464.9 0.0 collective-permute-done.1
  464.9 7.9 maximum_convert_fusion
  472.9 65.4 %fusion.25 = bf16[32,40,4096]{2,1,0:T(8,128)(2,1)} fusion(f32[34,40,4096]{2,1,0:T(8,128)} %maximum_convert_fusion, f32[4096]{0:T(1024)S(1)} %bitcast.28, f32[4096]{0:T(1024)S(1)} %bitcast.29, f32[4096]{0:T(1024)S(1)} %bitcast.22, f32[4096]{0:T(1024)S(1)} %bitcast.23, f32[4096]{0:T(1024)S(1)} %bitcast.24, f32[4096]{0:T(1024)S(1)} %bitcast.25, ...), kind=kLoop, calls=%fused_computation.35 | loop fusion | flops 136314880 | bytes 95830016 | tf_op jit(solution)/shard_map/convert_element_type | solution.py:52
  538.3 68.8 %all-gather.8.cloned.1.call-done = bf16[4096,4096]{1,0:T(8,128)(2,1)} async-done(((bf16[4096,1024]{1,0:T(8,128)(2,1)}), bf16[4096,4096]{1,0:T(8,128)(2,1)}) %all-gather.8.cloned.1.call-update) | async-done | bytes 33554448 | tf_op jit(solution)/shard_map/all_gather | solution.py:54
  607.1 52.9 %fusion.31 = f32[1280,4096]{1,0:T(8,128)} fusion(bf16[1280,4096]{1,0:T(8,128)(2,1)} %bitcast.20, bf16[4096,4096]{1,0:T(8,128)(2,1)} %all-gather.8.cloned.1.call-done), kind=kOutput, calls=%fused_computation.50 | convolution fusion | flops 42949672960 | bytes 65011712 | tf_op jit(solution)/shard_map/dot_general | solution.py:53
  659.9 0.0 copy-start
  659.9 0.0 reduce-scatter.2.cloned.1.call-update
  660.0 347.4 %reduce-scatter.2.cloned.1.call-done = f32[1280,1024]{1,0:T(8,128)} async-done(((f32[1280,4096]{1,0:T(8,128)}), f32[1280,1024]{1,0:T(8,128)}) %reduce-scatter.2.cloned.1.call-update) | async-done | bytes 5242896 | tf_op jit(solution)/shard_map/reduce_scatter | solution.py:56
  1007.3 0.0 copy-done
  1007.3 5.0 add_convert_fusion
  (2 shorter events, 0.1 us)
Async XLA Ops:
  6.5 390.4 %copy-start.2 = (f32[4096]{0:T(1024)S(1)}, f32[4096]{0:T(1024)}, u32[]{:S(2)}) copy-start(f32[4096]{0:T(1024)} %param.6) | copy-start | bytes 49156
  6.5 189.0 %all-gather.4.cloned.1.call-start = ((), (), s32[]{:S(2)}) async-start(), calls=%async_computation.1 | async-start | bytes 13107200 | tf_op jit(solution)/shard_map/all_gather | solution.py:31
  7.3 389.6 %all-gather.6.cloned.1.call-start = ((), (), s32[]{:S(2)}) async-start(), calls=%async_computation.2 | async-start | bytes 41943040 | tf_op jit(solution)/shard_map/all_gather | solution.py:37
  8.0 599.0 %all-gather.8.cloned.1.call-start = ((), (), s32[]{:S(2)}) async-start(), calls=%async_computation.3 | async-start | bytes 41943040 | tf_op jit(solution)/shard_map/all_gather | solution.py:54
  8.7 998.6 %reduce-scatter.2.cloned.1.call-start = ((), (), s32[]{:S(2)}) async-start(), calls=%async_computation.4 | async-start | bytes 26214400 | tf_op jit(solution)/shard_map/reduce_scatter | solution.py:56
  396.9 53.0 %copy-start.1 = (f32[9,4096]{1,0:T(8,128)S(1)}, f32[9,4096]{1,0:T(8,128)}, u32[]{:S(2)}) copy-start(f32[9,4096]{1,0:T(8,128)} %param.8) | copy-start | bytes 442372
  448.1 16.8 %collective-permute-start = (bf16[1,40,4096]{2,1,0:T(8,128)(2,1)S(1)}, bf16[1,40,4096]{2,1,0:T(8,128)(2,1)S(1)}, u32[]{:S(2)}, u32[]{:S(2)}) collective-permute-start(bf16[1,40,4096]{2,1,0:T(8,128)(2,1)S(1)} %get-tuple-element.7), channel_id=1, source_target_pairs={{0,4},{4,8},{8,12},{12,0},{1,5},{5,9},{9,13},{13,1},{2,6},{6,10},{... | collective-permute-start | bytes 983048 | tf_op jit(solution)/shard_map/ppermute | solution.py:19
  448.4 16.5 %collective-permute-start.1 = (bf16[1,40,4096]{2,1,0:T(8,128)(2,1)S(1)}, bf16[1,40,4096]{2,1,0:T(8,128)(2,1)S(1)}, u32[]{:S(2)}, u32[]{:S(2)}) collective-permute-start(bf16[1,40,4096]{2,1,0:T(8,128)(2,1)S(1)} %get-tuple-element.8), channel_id=1, source_target_pairs={{4,0},{8,4},{12,8},{0,12},{5,1},{9,5},{13,9},{1,13},{6,2},{10,6},{... | collective-permute-start | bytes 983048 | tf_op jit(solution)/shard_map/ppermute | solution.py:21
  659.9 347.4 %copy-start = (bf16[1280,1024]{1,0:T(8,128)(2,1)S(1)}, bf16[1280,1024]{1,0:T(8,128)(2,1)}, u32[]{:S(2)}) copy-start(bf16[1280,1024]{1,0:T(8,128)(2,1)} %param.5) | copy-start | bytes 7864324
Sparse Core Ops, SparseCore 0:
  8.9 186.6 all-gather.3
  197.1 199.7 all-gather.5
  398.5 208.5 all-gather.7
  660.1 347.2 reduce-scatter.1
where the time goes:
time: 1020 us
  waiting for transfers between devices  814 us (80%)
  matrix products  104 us (10%)
  other arithmetic  85.4 us (8%)
  between operations  13.2 us (1%)
    reduce_scatter x1, waiting for transfers between devices, per_device(): lax.psum_scatter(partial_value, 'col', scatter_dimension=1, tiled=True)  347 us
    all_gather x1, waiting for transfers between devices, per_device(): lax.all_gather(w_in, 'row', axis=0, tiled=True)  194 us
    all_gather x1, waiting for transfers between devices, per_device(): lax.all_gather(tokens, 'col', axis=1, tiled=True).astype(jnp.float32)  187 us
    all_gather x1, waiting for transfers between devices, per_device(): lax.all_gather(w_out, 'row', axis=1, tiled=True)  68.8 us
    convert_element_type x1, other arithmetic, per_device(): jax.nn.gelu(conv, approximate=True).astype(jnp.bfloat16)  65.4 us
    dot_general x1, matrix products, per_device(): jnp.dot(act, lax.all_gather(w_out, 'row', axis=1, tiled=True), preferred_...  52.9 us
    dot_general x1, matrix products, per_device(): jnp.dot(normed, lax.all_gather(w_in, 'row', axis=0, tiled=True), preferre...  51.2 us
  transfers between devices with their start and end apart: 6, of which 5 were waited for; matrix products, arithmetic and copies ran while one was open for 13% of the time, Pallas kernels for 0%

commit v1 on v0

--- a/solution.py
+++ b/solution.py
@@ -1,12 +1,16 @@
+import functools
+
 import jax
 import jax.numpy as jnp
 from jax import lax
+from jax.experimental import pallas as pl
+from jax.experimental.pallas import tpu as pltpu
 from jax.sharding import PartitionSpec as P
 
 LAT = 40
-
-
 eps = 1e-05
+TILE = 512
+VMEM_LIMIT = 44 * 1024 * 1024
 
 
 def extended(cells, sides, width):
@@ -25,7 +29,7 @@
     return cells
 
 
-def per_device(tokens, norm_gain, w_in, conv_kernel, w_out):
+def any_mesh(tokens, norm_gain, w_in, conv_kernel, w_out):
     rows, local_cols = tokens.shape
     values = tokens.astype(jnp.float32)
     whole = lax.all_gather(tokens, "col", axis=1, tiled=True).astype(jnp.float32)
@@ -57,8 +61,246 @@
     return (values + mixed).astype(jnp.bfloat16)
 
 
+def after(value, *others):
+    return lax.optimization_barrier((value, *others))[0]
+
+
+def swap_x(v):
+    return lax.ppermute(v, "row", [(i, i ^ 2) for i in range(4)])
+
+
+def swap_core(v):
+    return lax.ppermute(v, "row", [(i, i ^ 1) for i in range(4)])
+
+
+def swap_scen(v):
+    return lax.ppermute(v, "scen", [(0, 1), (1, 0)])
+
+
+def down(v, hop):
+    return lax.ppermute(v, "col", [(i, i - 1) for i in range(1, 5 - hop)])
+
+
+def up(v, hop):
+    return lax.ppermute(v, "col", [(i, i + 1) for i in range(hop - 1, 3)])
+
+
+def spread(own, first):
+    own_ = after(own, *first)
+    d, u = [], []
+    dv, uv = own_, own_
+    for hop in (1, 2, 3):
+        dv, uv = down(dv, hop), up(uv, hop)
+        d.append(dv)
+        u.append(uv)
+        dv, uv = lax.optimization_barrier((dv, uv))
+    return [own, *d, *u]
+
+
+def conv_gelu(hid_ref, k_ref, o_ref, lons):
+    width = hid_ref.shape[1]
+    lanes = 256
+    for c in range(0, width, lanes):
+        cols = pl.ds(c, lanes)
+        taps = [k_ref[pl.ds(i, 1), cols] for i in range(9)]
+        at = lax.broadcasted_iota(jnp.int32, (LAT, lanes), 0)
+
+        def one_lon(lon):
+            base = pl.multiple_of(lon * LAT, 8)
+            left = hid_ref[pl.ds(base, LAT), cols]
+            here = hid_ref[pl.ds(pl.multiple_of(base + LAT, 8), LAT), cols]
+            right = hid_ref[pl.ds(pl.multiple_of(base + 2 * LAT, 8), LAT), cols]
+            s = [taps[b] * left + taps[3 + b] * here + taps[6 + b] * right for b in range(3)]
+            below = jnp.where(at == 0, 0.0, pltpu.roll(s[0], 1, 0))
+            above = jnp.where(at == LAT - 1, 0.0, pltpu.roll(s[2], LAT - 1, 0))
+            v = s[1] + below + above
+            inner = 0.7978845608028654 * (v + 0.044715 * (v * v * v))
+            return 0.5 * v * (1.0 + jnp.tanh(inner))
+
+        def one(pair, _):
+            both = jnp.concatenate([one_lon(2 * pair), one_lon(2 * pair + 1)], axis=0)
+            o_ref[pl.ds(pl.multiple_of(pair * 2 * LAT, 16), 2 * LAT), cols] = both.astype(o_ref.dtype)
+            return 0
+
+        lax.fori_loop(0, lons // 2, one, 0)
+
+
+def first_kernel(has_tail, n_w, place_ref, *refs):
+    toks, refs = refs[:7], refs[7:]
+    ws, refs = refs[:n_w], refs[n_w:]
+    if has_tail:
+        tail_ref, k_ref, act_ref, tok, wbuf, hid, tsem, wsem = refs
+    else:
+        k_ref, act_ref, tail_out, tok, wbuf, hid, tsem, wsem = refs
+    scen, row, col = place_ref[0], place_ref[1], place_ref[2]
+    n, count = pl.program_id(0), pl.num_programs(0)
+    d = toks[0].shape[1]
+
+    def w_copies(tile, slot):
+        cols = pl.ds(pl.multiple_of(tile * TILE, TILE), TILE)
+        for ref, base, step, flip in ws_places(ws):
+            off = base + step * (scen if not flip else 1 - scen)
+            off = pl.multiple_of(jnp.int32(off), 16)
+            pltpu.make_async_copy(
+                ref.at[:, cols], wbuf.at[slot, pl.ds(off, ref.shape[0]), :], wsem.at[slot]
+            ).start()
+
+    @pl.when(n == 0)
+    def _():
+        w_copies(0, 0)
+
+        def tok_copy(ref, f):
+            at = pl.multiple_of((row ^ f) * d, d)
+            pltpu.make_async_copy(ref, tok.at[:, pl.ds(at, d)], tsem).start()
+
+        tok_copy(toks[0], col)
+        for hop in (1, 2, 3):
+
+            @pl.when(col + hop <= 3)
+            def _():
+                tok_copy(toks[hop], col + hop)
+
+            @pl.when(col - hop >= 0)
+            def _():
+                tok_copy(toks[3 + hop], col - hop)
+
+        pltpu.make_async_copy(tok, tok, tsem).wait()
+
+    slot = lax.rem(n, 2)
+
+    @pl.when(n + 1 < count)
+    def _():
+        w_copies(n + 1, 1 - slot)
+
+    pltpu.make_async_copy(wbuf.at[slot], wbuf.at[slot], wsem.at[slot]).wait()
+    lead = hid.shape[0] - tok.shape[0]
+    if has_tail:
+        hid[pl.ds(0, lead), :] = tail_ref[...].astype(jnp.float32)
+    product = jnp.dot(tok[...], wbuf[slot], preferred_element_type=jnp.float32)
+    hidden = product.astype(jnp.bfloat16)
+    if not has_tail:
+        tail_out[...] = hidden[hidden.shape[0] - 2 * LAT :]
+    hid[pl.ds(lead, tok.shape[0]), :] = hidden.astype(jnp.float32)
+    conv_gelu(hid, k_ref, act_ref, act_ref.shape[0] // LAT)
+
+
+def ws_places(ws):
+    d = ws[0].shape[0]
+    own, sib = ws[:2]
+    out = [(own, 0, 0, False), (sib, d, 0, False)]
+    pieces = (len(ws) - 2) // 2
+    for which in range(2):
+        mine = ws[2 + which * pieces : 2 + (which + 1) * pieces]
+        base = (2 + which) * d
+        x0, y0, x1, y1 = mine[:4]
+        h = x0.shape[0]
+        out += [(x0, base, 2 * h, False), (y0, base, 2 * h, True)]
+        out += [(x1, base + h, 2 * h, False), (y1, base + h, 2 * h, True)]
+        if len(mine) > 4:
+            out += [(mine[4], base + 4 * h, 0, False)]
+    return out
+
+
+def first(place, toks, ws, conv_kernel, tail, lons):
+    rows, d = toks[0].shape
+    units = conv_kernel.shape[1]
+    has_tail = tail is not None
+    hid_rows = rows + (2 * LAT if has_tail else 0)
+    out_rows = lons * LAT
+    any_spec = pl.BlockSpec(memory_space=pl.ANY)
+    wide = lambda r: pl.BlockSpec((r, TILE), lambda n: (0, n))
+    act_shape = jax.ShapeDtypeStruct((out_rows, units), jnp.bfloat16)
+    tail_shape = jax.ShapeDtypeStruct((2 * LAT, units), jnp.bfloat16)
+    return pl.pallas_call(
+        functools.partial(first_kernel, has_tail, len(ws)),
+        grid=(units // TILE,),
+        in_specs=[pl.BlockSpec(memory_space=pltpu.SMEM)]
+        + [any_spec] * (7 + len(ws))
+        + ([wide(2 * LAT)] if has_tail else [])
+        + [wide(9)],
+        out_specs=wide(out_rows) if has_tail else [wide(out_rows), wide(2 * LAT)],
+        out_shape=act_shape if has_tail else [act_shape, tail_shape],
+        scratch_shapes=[
+            pltpu.VMEM((rows, 4 * d), jnp.bfloat16),
+            pltpu.VMEM((2, 4 * d, TILE), jnp.bfloat16),
+            pltpu.VMEM((hid_rows, TILE), jnp.float32),
+            pltpu.SemaphoreType.DMA,
+            pltpu.SemaphoreType.DMA((2,)),
+        ],
+        compiler_params=pltpu.CompilerParams(vmem_limit_bytes=VMEM_LIMIT),
+        cost_estimate=pl.CostEstimate(
+            flops=2 * rows * 4 * d * units, bytes_accessed=8 * d * units, transcendentals=0
+        ),
+        name="first",
+    )(place, *toks, *ws, *([tail] if has_tail else []), conv_kernel)
+
+
+def w_in_parts(w, scen, start):
+    d, units = w.shape
+    h = (d * 13 // 64) // 16 * 16
+    x_in = [lax.dynamic_slice(w, (scen * 2 * h + i * h, 0), (h, units)) for i in range(2)]
+    sib = swap_core(w)
+    x0 = swap_x(x_in[0])
+    x1 = swap_x(after(x_in[1], x0))
+    y0 = swap_scen(x0)
+    xd = swap_x(after(w[4 * h :], x1))
+    y1 = swap_scen(after(x1, y0))
+    mine = [x0, y0, x1, y1, xd]
+    return [w, sib, *mine, *[swap_core(v) for v in mine]], (x1, xd, y1)
+
+
+def per_device(tokens, norm_gain, w_in, conv_kernel, w_out):
+    rows, d = tokens.shape
+    scen, row, col = (lax.axis_index(a) for a in ("scen", "row", "col"))
+    place = jnp.stack([scen, row, col]).astype(jnp.int32)
+    wide = extended(tokens, (("row", 0),), LAT)
+    v = wide.astype(jnp.float32)
+    sums = jnp.stack([jnp.sum(v, axis=1), jnp.sum(v * v, axis=1)])
+    sums = jnp.sum(lax.all_gather(sums, "col"), axis=0) / (4 * d)
+    mean = sums[0][:, None]
+    var = sums[1][:, None] - mean * mean
+    gain = lax.dynamic_slice(norm_gain, (col * d,), (d,))
+    normed = ((v - mean) * lax.rsqrt(var + eps) * gain).astype(jnp.bfloat16)
+
+    lons = rows // LAT
+    cut = (lons // 2 + 2) * LAT
+    toks_a = spread(normed[:cut], ())
+    toks_b = spread(normed[cut:], toks_a[1:])
+
+    ws, (x1, xd, y1) = w_in_parts(w_in, scen, ())
+    act_a, tail = first(place, toks_a, ws, conv_kernel, None, lons // 2)
+    act_b = first(place, toks_b, ws, conv_kernel, tail, lons - lons // 2)
+
+    q = d // 4
+    out_in = [lax.dynamic_slice(w_out, (0, i * 2 * q + scen * q), (w_out.shape[0], q)) for i in range(2)]
+    o_sib = swap_core(after(w_out, ws[1]))
+    ox0 = swap_x(after(out_in[0], xd))
+    oy0 = swap_scen(after(ox0, y1))
+    ox1 = swap_x(after(out_in[1], ox0))
+    oy1 = swap_scen(after(ox1, oy0))
+
+    def join(a, b):
+        return jnp.concatenate([jnp.where(scen == 0, a, b), jnp.where(scen == 0, b, a)], axis=1)
+
+    far = jnp.concatenate([join(ox0, oy0), join(ox1, oy1)], axis=1)
+    far_sib = swap_core(far)
+    shards = jnp.stack([w_out, o_sib, far, far_sib])
+    full = jnp.concatenate([lax.dynamic_index_in_dim(shards, row ^ f, 0, False) for f in range(4)], axis=1)
+    outs = []
+    for act in (act_a, act_b):
+        part = jnp.dot(act, full, preferred_element_type=jnp.float32).astype(jnp.bfloat16)
+        outs.append(lax.psum_scatter(part, "col", scatter_dimension=1, tiled=True))
+    mixed = jnp.concatenate(outs, axis=0).astype(jnp.float32)
+    return (tokens.astype(jnp.float32) + mixed).astype(jnp.bfloat16)
+
+
 def solution(mesh):
     placed = (P(("scen", "row"), "col"), P(), P("row", "col"), P(None, "col"), P("col", "row"))
+    sizes = tuple(mesh.shape[a] for a in ("scen", "row", "col"))
     return jax.shard_map(
-        per_device, mesh=mesh, in_specs=placed, out_specs=P(("scen", "row"), "col"), check_vma=False
+        per_device if sizes == (2, 4, 4) else any_mesh,
+        mesh=mesh,
+        in_specs=placed,
+        out_specs=P(("scen", "row"), "col"),
+        check_vma=False,
     )

time: 1020 us -> 841 us (0.82)
  waiting for transfers between devices: 814 us -> 520 us
  Pallas kernels: 0 us -> 83.8 us
  local copies, waits for them, and re-layouts: 0.15 us -> 52.6 us
  other arithmetic: 85.4 us -> 41.1 us
  starting transfers between devices: 1.91 us -> 35.2 us
  matrix products: 104 us -> 80.3 us
  blocking collectives: 0 us -> 13.4 us
    all_gather x3 -> x0, waiting for transfers between devices: 450 us -> none  [the longest x1 194 us: per_device(): lax.all_gather(w_in, 'row', axis=0, tiled=True)]
    ppermute x0 -> x29, waiting for transfers between devices: none -> 383 us  [the longest x6 206 us: down(): return lax.ppermute(v, 'col', [(i, i - 1) for i in range(1, 5 - hop)])]
    reduce_scatter x1 -> x2, waiting for transfers between devices: 347 us -> 97.5 us  [per_device(): outs.append(lax.psum_scatter(part, 'col', scatter_dimension=1, tiled=True))]
    pallas_call x0 -> x2, Pallas kernels: none -> 83.8 us  [first(): pl.pallas_call(functools.partial(first_kernel, has_tail, len(ws)), grid=(...]
    convert_element_type x3 -> x2, other arithmetic: 78.3 us -> 6.38 us  [the longest x1 4.48 us: per_device(): return (tokens.astype(jnp.float32) + mixed).astype(jnp.bfloat16)]
    ppermute x0 -> x29, starting transfers between devices: none -> 33.3 us  [the longest x5 9.39 us: swap_x(): return lax.ppermute(v, 'row', [(i, i ^ 2) for i in range(4)])]
    another operation x0 -> x3, other arithmetic: none -> 29.3 us  [the longest x2 29.3 us: per_device(): shards = jnp.stack([w_out, o_sib, far, far_sib])]
    dot_general x2, matrix products: 104 us -> 80.3 us  [per_device(): jnp.dot(act, full, preferred_element_type=jnp.float32).astype(jnp.bfloat16)]
  transfers between devices with their start and end apart: 6 -> 33, of which waited for: 5 -> 14; matrix products, arithmetic and copies ran while one was open for 13% -> 17% of each run, Pallas kernels for 0% -> 10%
where the time goes in v1:
time: 841 us; the launch traced here: 840 us
  waiting for transfers between devices  520 us (62%)
  Pallas kernels  83.8 us (10%)
  matrix products  80.3 us (10%)
  local copies, waits for them, and re-layouts  52.6 us (6%)
  other arithmetic  41.1 us (5%)
  starting transfers between devices  35.2 us (4%)
  between operations  13.8 us (2%)
  blocking collectives  13.4 us (2%)
    ppermute x6, waiting for transfers between devices, down(): return lax.ppermute(v, 'col', [(i, i - 1) for i in range(1, 5 - hop)])  206 us
    ppermute x5, waiting for transfers between devices, swap_x(): return lax.ppermute(v, 'row', [(i, i ^ 2) for i in range(4)])  139 us
    reduce_scatter x2, waiting for transfers between devices, per_device(): outs.append(lax.psum_scatter(part, 'col', scatter_dimension=1, tiled=True))  97.5 us
    pallas_call x2, Pallas kernels, first(): pl.pallas_call(functools.partial(first_kernel, has_tail, len(ws)), grid=(...  83.8 us
    dot_general x2, matrix products, per_device(): jnp.dot(act, full, preferred_element_type=jnp.float32).astype(jnp.bfloat16)  80.3 us
    ppermute x4, waiting for transfers between devices, swap_scen(): return lax.ppermute(v, 'scen', [(0, 1), (1, 0)])  36.6 us
    ppermute x1, waiting for transfers between devices, extended(): lax.ppermute(tail, axis, [(i, (i + 1) % count) for i in range(count)])  36.1 us
    another operation x2, other arithmetic, per_device(): shards = jnp.stack([w_out, o_sib, far, far_sib])  29.3 us
  transfers between devices with their start and end apart: 33, of which 14 were waited for; matrix products, arithmetic and copies ran while one was open for 17% of the time, Pallas kernels for 10%

profile of v1, /device:TPU:0, one launch (start us, length us, event | category | flops | bytes accessed | tf_op | source)
XLA Modules:
  0.0 840.5 jit_solution(15613182037739578144)
XLA Ops:
  6.5 2.2 constant_dynamic-slice_fusion.2
  8.7 3.0 collective-permute-start.9
  11.7 37.3 %collective-permute-done.9.refs_9_ = bf16[208,4096]{1,0:T(8,128)(2,1)} collective-permute-done((bf16[208,4096]{1,0:T(8,128)(2,1)S(1)}, bf16[208,4096]{1,0:T(8,128)(2,1)}, u32[]{:S(2)}, u32[]{:S(2)}) %collective-permute-start.9) | collective-permute-done | bytes 1703968 | tf_op jit(solution)/shard_map/ppermute | solution.py:69
  49.0 1.7 collective-permute-start.11
  50.8 2.8 slice.26
  53.6 33.9 %collective-permute-done.11.refs_11_ = bf16[208,4096]{1,0:T(8,128)(2,1)S(1)} collective-permute-done((bf16[208,4096]{1,0:T(8,128)(2,1)S(1)}, bf16[208,4096]{1,0:T(8,128)(2,1)S(1)}, u32[]{:S(2)}, u32[]{:S(2)}) %collective-permute-start.11) | collective-permute-done | bytes 1703968 | tf_op jit(solution)/shard_map/ppermute | solution.py:69
  88.6 1.4 collective-permute-start.13
  90.0 1.5 collective-permute-start.10
  91.6 4.0 constant_dynamic-slice_fusion.1
  95.5 28.1 %collective-permute-done.13.refs_13_ = bf16[192,4096]{1,0:T(8,128)(2,1)} collective-permute-done((bf16[192,4096]{1,0:T(8,128)(2,1)}, bf16[192,4096]{1,0:T(8,128)(2,1)}, u32[]{:S(2)}, u32[]{:S(2)}) %collective-permute-start.13) | collective-permute-done | bytes 1572896 | tf_op jit(solution)/shard_map/ppermute | solution.py:69
  124.8 2.8 collective-permute-done.10.refs_10_
  127.6 1.5 collective-permute-start.12
  129.1 39.6 %collective-permute-done.20 = bf16[4096,256]{1,0:T(8,128)(2,1)} collective-permute-done((bf16[4096,256]{1,0:T(8,128)(2,1)S(1)}, bf16[4096,256]{1,0:T(8,128)(2,1)}, u32[]{:S(2)}, u32[]{:S(2)}) %collective-permute-start.20) | collective-permute-done | bytes 2097184 | tf_op jit(solution)/shard_map/ppermute | solution.py:69
  169.7 2.0 collective-permute-start.22
  171.8 1.7 collective-permute-start.1
  174.2 36.1 %collective-permute-done = bf16[40,1024]{1,0:T(8,128)(2,1)S(1)} collective-permute-done((bf16[40,1024]{1,0:T(8,128)(2,1)S(1)}, bf16[40,1024]{1,0:T(8,128)(2,1)S(1)}, u32[]{:S(2)}, u32[]{:S(2)}) %collective-permute-start) | collective-permute-done | bytes 81952 | tf_op jit(solution)/shard_map/ppermute | solution.py:23
  210.3 3.9 collective-permute-done.1
  215.2 13.4 %all-gather.1 = f32[4,2,1360]{2,1,0:T(2,128)S(1)} all-gather(f32[1,2,1360]{2,1,0:T(2,128)S(1)} %maximum_bitcast_fusion), channel_id=2, replica_groups=mesh['scen'=2,'row'=4,'col'=4] {'col'}, dimensions={0}, use_global_device_ids=true | all-gather | bytes 54400 | tf_op jit(solution)/shard_map/all_gather | solution.py:259
  229.8 1.9 fusion.3
  231.9 1.4 copy-done.15
  233.3 3.5 collective-permute-start.3
  238.2 2.5 broadcast_select_fusion.3
  240.7 33.8 %collective-permute-done.23 = bf16[4096,256]{1,0:T(8,128)(2,1)S(1)} collective-permute-done((bf16[4096,256]{1,0:T(8,128)(2,1)}, bf16[4096,256]{1,0:T(8,128)(2,1)S(1)}, u32[]{:S(2)}, u32[]{:S(2)}) %collective-permute-start.23) | collective-permute-done | bytes 2097184 | tf_op jit(solution)/shard_map/ppermute | solution.py:77
  274.5 1.9 broadcast_select_fusion.1
  276.4 6.6 fusion.6
  287.8 31.8 %collective-permute-done.4.refs_2_ = bf16[720,1024]{1,0:T(8,128)(2,1)S(1)} collective-permute-done((bf16[720,1024]{1,0:T(8,128)(2,1)S(1)}, bf16[720,1024]{1,0:T(8,128)(2,1)S(1)}, u32[]{:S(2)}, u32[]{:S(2)}) %collective-permute-start.4) | collective-permute-done | bytes 1474592 | tf_op jit(solution)/shard_map/ppermute | solution.py:81
  324.0 32.2 %collective-permute-done.6.refs_3_ = bf16[720,1024]{1,0:T(8,128)(2,1)S(1)} collective-permute-done((bf16[720,1024]{1,0:T(8,128)(2,1)S(1)}, bf16[720,1024]{1,0:T(8,128)(2,1)S(1)}, u32[]{:S(2)}, u32[]{:S(2)}) %collective-permute-start.6) | collective-permute-done | bytes 1474592 | tf_op jit(solution)/shard_map/ppermute | solution.py:81
  360.2 1.4 slice.31.refs_0_
  361.6 2.5 collective-permute-start.26
  364.2 1.8 collective-permute-done.18.refs_18_
  366.0 1.5 collective-permute-start.25
  367.5 1.4 copy-done.1
  368.8 1.4 copy-done.3
  370.2 1.4 copy-done.5
  371.6 1.4 copy-done.7
  373.0 1.4 copy-done.9
  374.3 42.8 %first.2 = (bf16[640,4096]{1,0:T(8,128)(2,1)}, bf16[80,4096]{1,0:T(8,128)(2,1)S(1)}) custom-call(s32[3]{0:T(128)S(1)} %pad_add_fusion.place_ref, bf16[720,1024]{1,0:T(8,128)(2,1)S(1)} %slice.30.refs_0_, bf16[720,1024]{1,0:T(8,128)(2,1)S(1)} %copy-done.3, bf16[720,1024]{1,0:T(8,128)(2,1)S(1)} %copy-done.5, bf16[720,1024]{1,0:T(8,128)(2,1)S(1)} %copy-done.9, ...), custom_call_target="tpu_custom_call" | custom-call | flops 24159191040 | bytes 33554432 | tf_op jit(solution)/shard_map/first/pallas_call | solution.py:214
  418.0 22.7 %pad_maximum_fusion = bf16[4,4096,1024]{2,1,0:T(8,128)(2,1)} fusion(bf16[1,4096,1024]{2,1,0:T(8,128)(2,1)} %bitcast.7, bf16[1,4096,1024]{2,1,0:T(8,128)(2,1)} %get-tuple-element.51, bf16[1,4096,1024]{2,1,0:T(8,128)(2,1)} %bitcast.5, bf16[1,4096,1024]{2,1,0:T(8,128)(2,1)} %bitcast.21), kind=kLoop, calls=%fused_computation | loop fusion | flops 50331648 | bytes 67108864 | tf_op jit(solution)/shard_map/stack | solution.py:287
  440.7 20.3 %dynamic-slice_bitcast_fusion.3 = (bf16[4096,1024]{1,0:T(8,128)(2,1)S(1)}, bf16[4096,1024]{1,0:T(8,128)(2,1)}, bf16[4096,1024]{1,0:T(8,128)(2,1)}, bf16[4096,1024]{1,0:T(8,128)(2,1)}) fusion(bf16[4,4096,1024]{2,1,0:T(8,128)(2,1)} %pad_maximum_fusion, s32[]{:T(128)S(6)} %select_n.58, s32[]{:T(128)S(6)} %select_n.61, s32[]{:T(128)S(6)} %select_n.60, ...), kind=kLoop, calls=%fused_computation.6 | loop fusion | bytes 67108880 | tf_op jit(solution)/shard_map/jit(dynamic_index_in_dim)/squeeze | solution.py:288
  461.0 3.3 copy-done.16
  464.3 40.1 %convolution_convert_fusion.1 = bf16[640,4096]{1,0:T(8,128)(2,1)} fusion(bf16[640,4096]{1,0:T(8,128)(2,1)} %get-tuple-element.31, bf16[4096,1024]{1,0:T(8,128)(2,1)} %get-tuple-element.48, bf16[4096,1024]{1,0:T(8,128)(2,1)} %get-tuple-element.49, bf16[4096,1024]{1,0:T(8,128)(2,1)} %get-tuple-element.50, bf16[4096,1024]{1,0:T(8,128)(2,1)S(1)} %get-tuple-element.47), kind=kOutput, calls=%fused_computation.11 | convolution fusion | flops 21611675648 | bytes 44040192 | tf_op jit(solution)/shard_map/dot_general | solution.py:291
  504.5 1.3 collective-permute-start.27
  506.5 85.5 %collective-permute-done.27.refs_2_ = bf16[640,1024]{1,0:T(8,128)(2,1)S(1)} collective-permute-done((bf16[640,1024]{1,0:T(8,128)(2,1)}, bf16[640,1024]{1,0:T(8,128)(2,1)S(1)}, u32[]{:S(2)}, u32[]{:S(2)}) %collective-permute-start.27) | collective-permute-done | bytes 1310752 | tf_op jit(solution)/shard_map/ppermute | solution.py:81
  594.3 56.1 %collective-permute-done.29.refs_3_ = bf16[640,1024]{1,0:T(8,128)(2,1)S(1)} collective-permute-done((bf16[640,1024]{1,0:T(8,128)(2,1)S(1)}, bf16[640,1024]{1,0:T(8,128)(2,1)S(1)}, u32[]{:S(2)}, u32[]{:S(2)}) %collective-permute-start.29) | collective-permute-done | bytes 1310752 | tf_op jit(solution)/shard_map/ppermute | solution.py:81
  650.4 41.0 %first.3 = bf16[640,4096]{1,0:T(8,128)(2,1)} custom-call(s32[3]{0:T(128)S(1)} %pad_add_fusion.place_ref, bf16[640,1024]{1,0:T(8,128)(2,1)S(1)} %slice.31.refs_0_, bf16[640,1024]{1,0:T(8,128)(2,1)} %collective-permute-done.25.refs_1_, bf16[640,1024]{1,0:T(8,128)(2,1)S(1)} %collective-permute-done.27.refs_2_, ...), custom_call_target="tpu_custom_call" | custom-call | flops 21474836480 | bytes 33554432 | tf_op jit(solution)/shard_map/first/pallas_call | solution.py:214
  691.4 40.1 %convolution_convert_fusion = bf16[640,4096]{1,0:T(8,128)(2,1)} fusion(bf16[640,4096]{1,0:T(8,128)(2,1)} %first.3, bf16[4096,1024]{1,0:T(8,128)(2,1)} %get-tuple-element.48, bf16[4096,1024]{1,0:T(8,128)(2,1)} %get-tuple-element.49, bf16[4096,1024]{1,0:T(8,128)(2,1)} %get-tuple-element.50, bf16[4096,1024]{1,0:T(8,128)(2,1)S(1)} %copy-done.17), kind=kOutput, calls=%fused_computation.10 | convolution fusion | flops 21611675648 | bytes 44040192 | tf_op jit(solution)/shard_map/dot_general | solution.py:291
  731.6 97.5 %reduce-scatter.5.cloned.1.call-done = bf16[640,1024]{1,0:T(8,128)(2,1)} async-done(((bf16[640,4096]{1,0:T(8,128)(2,1)}), bf16[640,1024]{1,0:T(8,128)(2,1)}) %reduce-scatter.5.cloned.1.call-update) | async-done | bytes 1310736 | tf_op jit(solution)/shard_map/reduce_scatter | solution.py:292
  829.2 4.5 add_convert_fusion
  (96 shorter events, 25.0 us)
Async XLA Ops:
  6.5 725.1 %reduce-scatter.3.cloned.1.call-start = ((), (), s32[]{:S(2)}) async-start(), calls=%async_computation.2 | async-start | bytes 6553600 | tf_op jit(solution)/shard_map/reduce_scatter | solution.py:292
  8.7 40.3 %collective-permute-start.9 = (bf16[208,4096]{1,0:T(8,128)(2,1)S(1)}, bf16[208,4096]{1,0:T(8,128)(2,1)}, u32[]{:S(2)}, u32[]{:S(2)}) collective-permute-start(bf16[208,4096]{1,0:T(8,128)(2,1)S(1)} %get-tuple-element.56), channel_id=1, source_target_pairs={{0,8},{4,12},{8,0},{12,4},{1,9},{5,13},{9,1},{13,5},{2,10},{6,14},... | collective-permute-start | bytes 5111816 | tf_op jit(solution)/shard_map/ppermute | solution.py:69
  49.0 122.6 %copy-start.13 = (bf16[1280,1024]{1,0:T(8,128)(2,1)S(1)}, bf16[1280,1024]{1,0:T(8,128)(2,1)}, u32[]{:S(2)}) copy-start(bf16[1280,1024]{1,0:T(8,128)(2,1)} %param.5) | copy-start | bytes 7864324
  49.0 38.4 %collective-permute-start.11 = (bf16[208,4096]{1,0:T(8,128)(2,1)S(1)}, bf16[208,4096]{1,0:T(8,128)(2,1)S(1)}, u32[]{:S(2)}, u32[]{:S(2)}) collective-permute-start(bf16[208,4096]{1,0:T(8,128)(2,1)S(1)} %get-tuple-element.28), channel_id=1, source_target_pairs={{0,8},{4,12},{8,0},{12,4},{1,9},{5,13},{9,1},{13,5},{2,10},{6,14},... | collective-permute-start | bytes 5111816 | tf_op jit(solution)/shard_map/ppermute | solution.py:69
  50.8 187.3 %collective-permute-start.8 = (bf16[1024,4096]{1,0:T(8,128)(2,1)}, bf16[1024,4096]{1,0:T(8,128)(2,1)}, u32[]{:S(2)}, u32[]{:S(2)}) collective-permute-start(bf16[1024,4096]{1,0:T(8,128)(2,1)} %refs_7_.3), channel_id=1, source_target_pairs={{0,4},{4,0},{8,12},{12,8},{1,5},{5,1},{9,13},{13,9},{2,6},{6,2},{1... | collective-permute-start | bytes 25165832 | tf_op jit(solution)/shard_map/ppermute | solution.py:73
  88.6 35.0 %collective-permute-start.13 = (bf16[192,4096]{1,0:T(8,128)(2,1)}, bf16[192,4096]{1,0:T(8,128)(2,1)}, u32[]{:S(2)}, u32[]{:S(2)}) collective-permute-start(bf16[192,4096]{1,0:T(8,128)(2,1)} %slice.26), channel_id=1, source_target_pairs={{0,8},{4,12},{8,0},{12,4},{1,9},{5,13},{9,1},{13,5},{2,10},{6,14},... | collective-permute-start | bytes 4718600 | tf_op jit(solution)/shard_map/ppermute | solution.py:69
  90.0 37.6 %collective-permute-start.10 = (bf16[208,4096]{1,0:T(8,128)(2,1)}, bf16[208,4096]{1,0:T(8,128)(2,1)}, u32[]{:S(2)}, u32[]{:S(2)}) collective-permute-start(bf16[208,4096]{1,0:T(8,128)(2,1)} %collective-permute-done.9.refs_9_), channel_id=1, source_target_pairs={{0,16},{16,0},{1,17},{17,1},{2,18},{18,2},{3,19},{19,3},{4,20},{20... | collective-permute-start | bytes 5111816 | tf_op jit(solution)/shard_map/ppermute | solution.py:77
  91.6 36.1 %copy-start.19 = (bf16[208,4096]{1,0:T(8,128)(2,1)S(1)}, bf16[208,4096]{1,0:T(8,128)(2,1)}, u32[]{:S(2)}) copy-start(bf16[208,4096]{1,0:T(8,128)(2,1)} %copy-done.18) | copy-start | bytes 5111812
  123.6 45.1 %collective-permute-start.20 = (bf16[4096,256]{1,0:T(8,128)(2,1)S(1)}, bf16[4096,256]{1,0:T(8,128)(2,1)}, u32[]{:S(2)}, u32[]{:S(2)}) collective-permute-start(bf16[4096,256]{1,0:T(8,128)(2,1)S(1)} %get-tuple-element.33), channel_id=1, source_target_pairs={{0,8},{4,12},{8,0},{12,4},{1,9},{5,13},{9,1},{13,5},{2,10},{6,14},... | collective-permute-start | bytes 6291464 | tf_op jit(solution)/shard_map/ppermute | solution.py:69
  127.6 41.1 %collective-permute-start.12 = (bf16[208,4096]{1,0:T(8,128)(2,1)S(1)}, bf16[208,4096]{1,0:T(8,128)(2,1)}, u32[]{:S(2)}, u32[]{:S(2)}) collective-permute-start(bf16[208,4096]{1,0:T(8,128)(2,1)S(1)} %copy-done.19), channel_id=1, source_target_pairs={{0,16},{16,0},{1,17},{17,1},{2,18},{18,2},{3,19},{19,3},{4,20},{20... | collective-permute-start | bytes 5111816 | tf_op jit(solution)/shard_map/ppermute | solution.py:77
  168.7 59.9 %collective-permute-start.21 = (bf16[4096,256]{1,0:T(8,128)(2,1)}, bf16[4096,256]{1,0:T(8,128)(2,1)}, u32[]{:S(2)}, u32[]{:S(2)}) collective-permute-start(bf16[4096,256]{1,0:T(8,128)(2,1)} %collective-permute-done.20), channel_id=1, source_target_pairs={{0,16},{16,0},{1,17},{17,1},{2,18},{18,2},{3,19},{19,3},{4,20},{20... | collective-permute-start | bytes 6291464 | tf_op jit(solution)/shard_map/ppermute | solution.py:77
  169.7 58.9 %collective-permute-start.22 = (bf16[4096,256]{1,0:T(8,128)(2,1)}, bf16[4096,256]{1,0:T(8,128)(2,1)}, u32[]{:S(2)}, u32[]{:S(2)}) collective-permute-start(bf16[4096,256]{1,0:T(8,128)(2,1)} %get-tuple-element.35), channel_id=1, source_target_pairs={{0,8},{4,12},{8,0},{12,4},{1,9},{5,13},{9,1},{13,5},{2,10},{6,14},... | collective-permute-start | bytes 6291464 | tf_op jit(solution)/shard_map/ppermute | solution.py:69
  171.7 38.6 %collective-permute-start = (bf16[40,1024]{1,0:T(8,128)(2,1)S(1)}, bf16[40,1024]{1,0:T(8,128)(2,1)S(1)}, u32[]{:S(2)}, u32[]{:S(2)}) collective-permute-start(bf16[40,1024]{1,0:T(8,128)(2,1)S(1)} %get-tuple-element.61), channel_id=1, source_target_pairs={{0,4},{4,8},{8,12},{12,0},{1,5},{5,9},{9,13},{13,1},{2,6},{6,10},{... | collective-permute-start | bytes 245768 | tf_op jit(solution)/shard_map/ppermute | solution.py:23
  171.8 42.4 %collective-permute-start.1 = (bf16[40,1024]{1,0:T(8,128)(2,1)S(1)}, bf16[40,1024]{1,0:T(8,128)(2,1)S(1)}, u32[]{:S(2)}, u32[]{:S(2)}) collective-permute-start(bf16[40,1024]{1,0:T(8,128)(2,1)S(1)} %get-tuple-element.62), channel_id=1, source_target_pairs={{4,0},{8,4},{12,8},{0,12},{5,1},{9,5},{13,9},{1,13},{6,2},{10,6},{... | collective-permute-start | bytes 245768 | tf_op jit(solution)/shard_map/ppermute | solution.py:25
  228.6 45.9 %collective-permute-start.23 = (bf16[4096,256]{1,0:T(8,128)(2,1)}, bf16[4096,256]{1,0:T(8,128)(2,1)S(1)}, u32[]{:S(2)}, u32[]{:S(2)}) collective-permute-start(bf16[4096,256]{1,0:T(8,128)(2,1)} %collective-permute-done.22), channel_id=1, source_target_pairs={{0,16},{16,0},{1,17},{17,1},{2,18},{18,2},{3,19},{19,3},{4,20},{20... | collective-permute-start | bytes 6291464 | tf_op jit(solution)/shard_map/ppermute | solution.py:77
  231.7 1.5 copy-start.15
  233.3 50.2 %collective-permute-start.3 = (bf16[720,1024]{1,0:T(8,128)(2,1)S(1)}, bf16[720,1024]{1,0:T(8,128)(2,1)S(1)}, u32[]{:S(2)}, u32[]{:S(2)}) collective-permute-start(bf16[720,1024]{1,0:T(8,128)(2,1)S(1)} %slice.30.refs_0_), channel_id=1, source_target_pairs={{0,1},{1,2},{2,3},{4,5},{5,6},{6,7},{8,9},{9,10},{10,11},{12,13},{... | collective-permute-start | bytes 4423688 | tf_op jit(solution)/shard_map/ppermute | solution.py:85
  236.8 46.7 %collective-permute-start.2 = (bf16[720,1024]{1,0:T(8,128)(2,1)S(1)}, bf16[720,1024]{1,0:T(8,128)(2,1)S(1)}, u32[]{:S(2)}, u32[]{:S(2)}) collective-permute-start(bf16[720,1024]{1,0:T(8,128)(2,1)S(1)} %slice.30.refs_0_), channel_id=1, source_target_pairs={{1,0},{2,1},{3,2},{5,4},{6,5},{7,6},{9,8},{10,9},{11,10},{13,12},{... | collective-permute-start | bytes 4423688 | tf_op jit(solution)/shard_map/ppermute | solution.py:81
  238.1 179.9 %collective-permute-start.19 = (bf16[4096,1024]{1,0:T(8,128)(2,1)}, bf16[4096,1024]{1,0:T(8,128)(2,1)}, u32[]{:S(2)}, u32[]{:S(2)}) collective-permute-start(bf16[4096,1024]{1,0:T(8,128)(2,1)} %param.9), channel_id=1, source_target_pairs={{0,4},{4,0},{8,12},{12,8},{1,5},{5,1},{9,13},{13,9},{2,6},{6,2},{1... | collective-permute-start | bytes 25165832 | tf_op jit(solution)/shard_map/ppermute | solution.py:73
  276.4 43.2 %copy-start.20 = (bf16[208,4096]{1,0:T(8,128)(2,1)S(1)}, bf16[208,4096]{1,0:T(8,128)(2,1)}, u32[]{:S(2)}) copy-start(bf16[208,4096]{1,0:T(8,128)(2,1)} %copy-done.18) | copy-start | bytes 5111812
  276.4 91.0 %copy-start.10 = (f32[9,4096]{1,0:T(8,128)S(1)}, f32[9,4096]{1,0:T(8,128)}, u32[]{:S(2)}) copy-start(f32[9,4096]{1,0:T(8,128)} %refs_20_.1) | copy-start | bytes 442372
  283.0 135.0 %collective-permute-start.24 = (bf16[4096,1024]{1,0:T(8,128)(2,1)}, bf16[4096,1024]{1,0:T(8,128)(2,1)}, u32[]{:S(2)}, u32[]{:S(2)}) collective-permute-start(bf16[4096,1024]{1,0:T(8,128)(2,1)} %get-tuple-element.52), channel_id=1, source_target_pairs={{0,4},{4,0},{8,12},{12,8},{1,5},{5,1},{9,13},{13,9},{2,6},{6,2},{1... | collective-permute-start | bytes 25165832 | tf_op jit(solution)/shard_map/ppermute | solution.py:73
  283.0 39.0 %collective-permute-start.14 = (bf16[208,4096]{1,0:T(8,128)(2,1)}, bf16[208,4096]{1,0:T(8,128)(2,1)S(1)}, u32[]{:S(2)}, u32[]{:S(2)}) collective-permute-start(bf16[208,4096]{1,0:T(8,128)(2,1)} %collective-permute-done.9.refs_9_), channel_id=1, source_target_pairs={{0,4},{4,0},{8,12},{12,8},{1,5},{5,1},{9,13},{13,9},{2,6},{6,2},{1... | collective-permute-start | bytes 5111816 | tf_op jit(solution)/shard_map/ppermute | solution.py:73
  283.5 36.1 %collective-permute-start.4 = (bf16[720,1024]{1,0:T(8,128)(2,1)S(1)}, bf16[720,1024]{1,0:T(8,128)(2,1)S(1)}, u32[]{:S(2)}, u32[]{:S(2)}) collective-permute-start(bf16[720,1024]{1,0:T(8,128)(2,1)S(1)} %collective-permute-done.2.refs_1_), channel_id=1, source_target_pairs={{1,0},{2,1},{5,4},{6,5},{9,8},{10,9},{13,12},{14,13},{17,16},{18,1... | collective-permute-start | bytes 4423688 | tf_op jit(solution)/shard_map/ppermute | solution.py:81
  285.9 33.7 %collective-permute-start.5 = (bf16[720,1024]{1,0:T(8,128)(2,1)S(1)}, bf16[720,1024]{1,0:T(8,128)(2,1)S(1)}, u32[]{:S(2)}, u32[]{:S(2)}) collective-permute-start(bf16[720,1024]{1,0:T(8,128)(2,1)S(1)} %collective-permute-done.3.refs_4_), channel_id=1, source_target_pairs={{1,2},{2,3},{5,6},{6,7},{9,10},{10,11},{13,14},{14,15},{17,18},{18... | collective-permute-start | bytes 4423688 | tf_op jit(solution)/shard_map/ppermute | solution.py:85
  319.6 38.3 %collective-permute-start.16 = (bf16[208,4096]{1,0:T(8,128)(2,1)S(1)}, bf16[208,4096]{1,0:T(8,128)(2,1)S(1)}, u32[]{:S(2)}, u32[]{:S(2)}) collective-permute-start(bf16[208,4096]{1,0:T(8,128)(2,1)S(1)} %copy-done.20), channel_id=1, source_target_pairs={{0,4},{4,0},{8,12},{12,8},{1,5},{5,1},{9,13},{13,9},{2,6},{6,2},{1... | collective-permute-start | bytes 5111816 | tf_op jit(solution)/shard_map/ppermute | solution.py:73
  319.6 36.6 %collective-permute-start.6 = (bf16[720,1024]{1,0:T(8,128)(2,1)S(1)}, bf16[720,1024]{1,0:T(8,128)(2,1)S(1)}, u32[]{:S(2)}, u32[]{:S(2)}) collective-permute-start(bf16[720,1024]{1,0:T(8,128)(2,1)S(1)} %collective-permute-done.4.refs_2_), channel_id=1, source_target_pairs={{1,0},{5,4},{9,8},{13,12},{17,16},{21,20},{25,24},{29,28}} | collective-permute-start | bytes 4423688 | tf_op jit(solution)/shard_map/ppermute | solution.py:81
  322.0 35.8 %copy-start.21 = (bf16[208,4096]{1,0:T(8,128)(2,1)}, bf16[208,4096]{1,0:T(8,128)(2,1)S(1)}, u32[]{:S(2)}) copy-start(bf16[208,4096]{1,0:T(8,128)(2,1)S(1)} %collective-permute-done.14.refs_14_) | copy-start | bytes 5111812
  322.0 35.3 %collective-permute-start.7 = (bf16[720,1024]{1,0:T(8,128)(2,1)S(1)}, bf16[720,1024]{1,0:T(8,128)(2,1)S(1)}, u32[]{:S(2)}, u32[]{:S(2)}) collective-permute-start(bf16[720,1024]{1,0:T(8,128)(2,1)S(1)} %collective-permute-done.5.refs_5_), channel_id=1, source_target_pairs={{2,3},{6,7},{10,11},{14,15},{18,19},{22,23},{26,27},{30,31}} | collective-permute-start | bytes 4423688 | tf_op jit(solution)/shard_map/ppermute | solution.py:85
  357.3 4.3 collective-permute-start.15
  357.4 10.1 %collective-permute-start.17 = (bf16[208,4096]{1,0:T(8,128)(2,1)}, bf16[208,4096]{1,0:T(8,128)(2,1)}, u32[]{:S(2)}, u32[]{:S(2)}) collective-permute-start(bf16[208,4096]{1,0:T(8,128)(2,1)} %collective-permute-done.12.refs_12_), channel_id=1, source_target_pairs={{0,4},{4,0},{8,12},{12,8},{1,5},{5,1},{9,13},{13,9},{2,6},{6,2},{1... | collective-permute-start | bytes 5111816 | tf_op jit(solution)/shard_map/ppermute | solution.py:73
  359.6 6.3 collective-permute-start.18
  361.6 142.8 %collective-permute-start.26 = (bf16[640,1024]{1,0:T(8,128)(2,1)S(1)}, bf16[640,1024]{1,0:T(8,128)(2,1)}, u32[]{:S(2)}, u32[]{:S(2)}) collective-permute-start(bf16[640,1024]{1,0:T(8,128)(2,1)S(1)} %slice.31.refs_0_), channel_id=1, source_target_pairs={{0,1},{1,2},{2,3},{4,5},{5,6},{6,7},{8,9},{9,10},{10,11},{12,13},{... | collective-permute-start | bytes 3932168 | tf_op jit(solution)/shard_map/ppermute | solution.py:85
  366.0 138.5 %collective-permute-start.25 = (bf16[640,1024]{1,0:T(8,128)(2,1)S(1)}, bf16[640,1024]{1,0:T(8,128)(2,1)}, u32[]{:S(2)}, u32[]{:S(2)}) collective-permute-start(bf16[640,1024]{1,0:T(8,128)(2,1)S(1)} %slice.31.refs_0_), channel_id=1, source_target_pairs={{1,0},{2,1},{3,2},{5,4},{6,5},{7,6},{9,8},{10,9},{11,10},{13,12},{... | collective-permute-start | bytes 3932168 | tf_op jit(solution)/shard_map/ppermute | solution.py:81
  367.5 1.4 copy-start.1
  368.8 1.4 copy-start.3
  370.2 1.4 copy-start.5
  371.6 1.4 copy-start.7
  373.0 1.4 copy-start.9
  461.0 3.3 copy-start.16
  464.3 186.1 %copy-start.12 = (bf16[80,4096]{1,0:T(8,128)(2,1)S(1)}, bf16[80,4096]{1,0:T(8,128)(2,1)}, u32[]{:S(2)}) copy-start(bf16[80,4096]{1,0:T(8,128)(2,1)} %copy-done.11) | copy-start | bytes 1966084
  504.4 324.8 %reduce-scatter.5.cloned.1.call-start = ((), (), s32[]{:S(2)}) async-start(), calls=%async_computation.3 | async-start | bytes 6553600 | tf_op jit(solution)/shard_map/reduce_scatter | solution.py:292
  504.5 87.6 %collective-permute-start.27 = (bf16[640,1024]{1,0:T(8,128)(2,1)}, bf16[640,1024]{1,0:T(8,128)(2,1)S(1)}, u32[]{:S(2)}, u32[]{:S(2)}) collective-permute-start(bf16[640,1024]{1,0:T(8,128)(2,1)} %collective-permute-done.25.refs_1_), channel_id=1, source_target_pairs={{1,0},{2,1},{5,4},{6,5},{9,8},{10,9},{13,12},{14,13},{17,16},{18,1... | collective-permute-start | bytes 3932168 | tf_op jit(solution)/shard_map/ppermute | solution.py:81
  505.8 86.3 %collective-permute-start.28 = (bf16[640,1024]{1,0:T(8,128)(2,1)}, bf16[640,1024]{1,0:T(8,128)(2,1)S(1)}, u32[]{:S(2)}, u32[]{:S(2)}) collective-permute-start(bf16[640,1024]{1,0:T(8,128)(2,1)} %collective-permute-done.26.refs_4_), channel_id=1, source_target_pairs={{1,2},{2,3},{5,6},{6,7},{9,10},{10,11},{13,14},{14,15},{17,18},{18... | collective-permute-start | bytes 3932168 | tf_op jit(solution)/shard_map/ppermute | solution.py:85
  592.0 58.3 %collective-permute-start.29 = (bf16[640,1024]{1,0:T(8,128)(2,1)S(1)}, bf16[640,1024]{1,0:T(8,128)(2,1)S(1)}, u32[]{:S(2)}, u32[]{:S(2)}) collective-permute-start(bf16[640,1024]{1,0:T(8,128)(2,1)S(1)} %collective-permute-done.27.refs_2_), channel_id=1, source_target_pairs={{1,0},{5,4},{9,8},{13,12},{17,16},{21,20},{25,24},{29,28}} | collective-permute-start | bytes 3932168 | tf_op jit(solution)/shard_map/ppermute | solution.py:81
  593.3 57.1 %collective-permute-start.30 = (bf16[640,1024]{1,0:T(8,128)(2,1)S(1)}, bf16[640,1024]{1,0:T(8,128)(2,1)S(1)}, u32[]{:S(2)}, u32[]{:S(2)}) collective-permute-start(bf16[640,1024]{1,0:T(8,128)(2,1)S(1)} %collective-permute-done.28.refs_5_), channel_id=1, source_target_pairs={{2,3},{6,7},{10,11},{14,15},{18,19},{22,23},{26,27},{30,31}} | collective-permute-start | bytes 3932168 | tf_op jit(solution)/shard_map/ppermute | solution.py:85
  650.4 41.1 %copy-start.17 = (bf16[4096,1024]{1,0:T(8,128)(2,1)S(1)}, bf16[4096,1024]{1,0:T(8,128)(2,1)}, u32[]{:S(2)}) copy-start(bf16[4096,1024]{1,0:T(8,128)(2,1)} %copy-done.16) | copy-start | bytes 25165828
  731.6 97.6 %copy-start.14 = (bf16[1280,1024]{1,0:T(8,128)(2,1)S(1)}, bf16[1280,1024]{1,0:T(8,128)(2,1)}, u32[]{:S(2)}) copy-start(bf16[1280,1024]{1,0:T(8,128)(2,1)} %param.5) | copy-start | bytes 7864324
  (9 other events, 10.0 us)
Sparse Core Ops, SparseCore 0:
  504.5 134.4 reduce-scatter.2
  731.7 97.3 reduce-scatter.4

commit v2 on v0

--- a/solution.py
+++ b/solution.py
@@ -1,12 +1,19 @@
+import functools
+
 import jax
 import jax.numpy as jnp
 from jax import lax
+from jax.experimental import pallas as pl
+from jax.experimental.pallas import tpu as pltpu
 from jax.sharding import PartitionSpec as P
 
 LAT = 40
-
-
 eps = 1e-05
+TILE = 1024
+SUB = 512
+LANES = 128
+BLOCK = 80
+VMEM_LIMIT = 58 * 1024 * 1024
 
 
 def extended(cells, sides, width):
@@ -25,7 +32,7 @@
     return cells
 
 
-def per_device(tokens, norm_gain, w_in, conv_kernel, w_out):
+def any_mesh(tokens, norm_gain, w_in, conv_kernel, w_out):
     rows, local_cols = tokens.shape
     values = tokens.astype(jnp.float32)
     whole = lax.all_gather(tokens, "col", axis=1, tiled=True).astype(jnp.float32)
@@ -57,8 +64,402 @@
     return (values + mixed).astype(jnp.bfloat16)
 
 
+def after(value, *others):
+    return lax.optimization_barrier((value, *others))[0]
+
+
+def swap_x(v):
+    return lax.ppermute(v, "row", [(i, i ^ 2) for i in range(4)])
+
+
+def swap_core(v):
+    return lax.ppermute(v, "row", [(i, i ^ 1) for i in range(4)])
+
+
+def cores(*values):
+    out = []
+    for v in values:
+        out.append(swap_core(after(v, *out[-1:])))
+    return out
+
+
+def swap_scen(v):
+    return lax.ppermute(v, "scen", [(0, 1), (1, 0)])
+
+
+def down(v, hop):
+    return lax.ppermute(v, "col", [(i, i - 1) for i in range(1, 5 - hop)])
+
+
+def up(v, hop):
+    return lax.ppermute(v, "col", [(i, i + 1) for i in range(hop - 1, 3)])
+
+
+def gate(done, begin):
+    done, begin = lax.optimization_barrier((tuple(done), tuple(begin)))
+    return list(done), list(begin)
+
+
+def conv_gelu(hid_ref, k_ref, o_ref, col, lons):
+    for c in range(0, hid_ref.shape[1], LANES):
+        conv_gelu_lanes(hid_ref, k_ref, o_ref, c, col + c, lons)
+
+
+def conv_gelu_lanes(hid_ref, k_ref, o_ref, lane, col, lons):
+    width = LANES
+    cols, here_cols = pl.ds(col, width), pl.ds(lane, width)
+    taps = [k_ref[pl.ds(i, 1), cols] for i in range(9)]
+    at = lax.broadcasted_iota(jnp.int32, (LAT, width), 0)
+
+    def one_lon(lon):
+        left, here, right = (hid_ref[pl.ds((lon + a) * LAT, LAT), here_cols] for a in range(3))
+        s = [taps[b] * left + taps[3 + b] * here + taps[6 + b] * right for b in range(3)]
+        below = jnp.where(at == 0, 0.0, pltpu.roll(s[0], 1, 0))
+        above = jnp.where(at == LAT - 1, 0.0, pltpu.roll(s[2], LAT - 1, 0))
+        v = s[1] + below + above
+        inner = 0.7978845608028654 * (v + 0.044715 * (v * v * v))
+        return 0.5 * v * (1.0 + jnp.tanh(inner))
+
+    for lon in range(0, lons, 2):
+        both = jnp.concatenate([one_lon(lon), one_lon(lon + 1)], axis=0)
+        o_ref[pl.ds(lon * LAT, 2 * LAT), cols] = both.astype(o_ref.dtype)
+
+
+def first_kernel(has_tail, n_tok, n_w, skip, place_ref, gain_ref, *refs):
+    toks, refs = refs[:n_tok], refs[n_tok:]
+    ws, refs = refs[:n_w], refs[n_w:]
+    fresh = n_tok > 1
+    tail_ref = tail_out = normed_out = None
+    if has_tail:
+        tail_ref, refs = refs[0], refs[1:]
+    k_ref, act_ref, refs = refs[0], refs[1], refs[2:]
+    if not has_tail:
+        tail_out, refs = refs[0], refs[1:]
+    if fresh:
+        normed_out, refs = refs[0], refs[1:]
+    tok, wbuf, hid_a, hid_b, tsem, wsem, nsem = refs
+    scen, row, col = place_ref[0], place_ref[1], place_ref[2]
+    n, count = pl.program_id(0), pl.num_programs(0)
+    rows, d = tok.shape[0], gain_ref.shape[1]
+    lead = hid_a.shape[0] - rows
+    lons = act_ref.shape[0] // LAT
+
+    def w_copies(step, sub):
+        cols = pl.ds(pl.multiple_of((step + skip) * TILE + sub * SUB, SUB), SUB)
+        for ref, base, stride, flip in ws_places(ws):
+            off = base + stride * (scen if not flip else 1 - scen)
+            off = pl.multiple_of(jnp.int32(off), 16)
+            pltpu.make_async_copy(
+                ref.at[:, cols], wbuf.at[sub, pl.ds(off, ref.shape[0]), :], wsem.at[sub]
+            ).start()
+
+    @pl.when(n == 0)
+    def _():
+        def tok_copy(ref, f):
+            at = pl.multiple_of((row ^ f) * d, d)
+            pltpu.make_async_copy(ref, tok.at[:, pl.ds(at, d)], tsem).start()
+
+        if fresh:
+            tok_copy(toks[0], col)
+            for hop in (1, 2, 3):
+
+                @pl.when(col + hop <= 3)
+                def _():
+                    tok_copy(toks[hop], col + hop)
+
+                @pl.when(col - hop >= 0)
+                def _():
+                    tok_copy(toks[3 + hop], col - hop)
+
+        else:
+            pltpu.make_async_copy(toks[0], tok, tsem).start()
+        for sub in range(TILE // SUB):
+            w_copies(0, sub)
+        pltpu.make_async_copy(tok, tok, tsem).wait()
+
+        def norm(i, _):
+            part = pl.ds(pl.multiple_of(i * BLOCK, 16), BLOCK)
+            total = square = 0.0
+            for j in range(4):
+                v = tok[part, pl.ds(j * d, d)].astype(jnp.float32)
+                total += jnp.sum(v, axis=1, keepdims=True)
+                square += jnp.sum(v * v, axis=1, keepdims=True)
+            mean = total / (4 * d)
+            scale = lax.rsqrt(square / (4 * d) - mean * mean + eps)
+            for j in range(4):
+                cols = pl.ds(j * d, d)
+                v = (tok[part, cols].astype(jnp.float32) - mean) * scale * gain_ref[pl.ds(row ^ j, 1), :]
+                tok[part, cols] = v.astype(jnp.bfloat16)
+            return 0
+
+        if fresh:
+            lax.fori_loop(0, rows // BLOCK, norm, 0)
+            pltpu.make_async_copy(tok, normed_out, nsem).start()
+
+    if fresh:
+
+        @pl.when(n == count - 1)
+        def _():
+            pltpu.make_async_copy(tok, normed_out, nsem).wait()
+
+    hids = (hid_a, hid_b)
+    subs = TILE // SUB
+    for sub in range(subs):
+        pltpu.make_async_copy(wbuf.at[sub], wbuf.at[sub], wsem.at[sub]).wait()
+        hid = hids[sub % 2]
+        product = jnp.dot(tok[...], wbuf[sub], preferred_element_type=jnp.float32)
+        hidden = product.astype(jnp.bfloat16)
+        if has_tail:
+            hid[pl.ds(0, lead), :] = tail_ref[:, pl.ds(sub * SUB, SUB)].astype(jnp.float32)
+        else:
+            tail_out[:, pl.ds(sub * SUB, SUB)] = hidden[rows - 2 * LAT :]
+        hid[pl.ds(lead, rows), :] = hidden.astype(jnp.float32)
+        if sub > 0:
+            conv_gelu(hids[1 - sub % 2], k_ref, act_ref, (sub - 1) * SUB, lons)
+
+        @pl.when(n + 1 < count)
+        def _():
+            w_copies(n + 1, sub)
+
+    conv_gelu(hids[(subs - 1) % 2], k_ref, act_ref, (subs - 1) * SUB, lons)
+
+
+def ws_places(ws):
+    d = ws[0].shape[0]
+    out = [(ws[0], 0, 0, False), (ws[1], d, 0, False)]
+    for which in range(2):
+        x0, y0, x1, y1, xd = ws[2 + which * 5 : 7 + which * 5]
+        base, h = (2 + which) * d, x0.shape[0]
+        out += [(x0, base, 2 * h, False), (y0, base, 2 * h, True)]
+        out += [(x1, base + h, 2 * h, False), (y1, base + h, 2 * h, True)]
+        out += [(xd, base + 4 * h, 0, False)]
+    return out
+
+
+def first(place, gain, toks, ws, conv_kernel, tail, half, lons):
+    rows, d = toks[0].shape[0], gain.shape[1]
+    units = conv_kernel.shape[1] // 2
+    skip = half * (units // TILE)
+    has_tail, fresh = tail is not None, len(toks) > 1
+    hid_rows = rows + (2 * LAT if has_tail else 0)
+    any_spec = pl.BlockSpec(memory_space=pl.ANY)
+    wide = lambda r: pl.BlockSpec((r, TILE), lambda n: (0, n))
+    shape = lambda r, c: jax.ShapeDtypeStruct((r, c), jnp.bfloat16)
+    out_specs, out_shape = [wide(lons * LAT)], [shape(lons * LAT, units)]
+    if not has_tail:
+        out_specs.append(wide(2 * LAT))
+        out_shape.append(shape(2 * LAT, units))
+    if fresh:
+        out_specs.append(any_spec)
+        out_shape.append(shape(rows, 4 * d))
+    return pl.pallas_call(
+        functools.partial(first_kernel, has_tail, len(toks), len(ws), skip),
+        grid=(units // TILE,),
+        in_specs=[pl.BlockSpec(memory_space=pltpu.SMEM), pl.BlockSpec(gain.shape, lambda n: (0, 0))]
+        + [any_spec] * (len(toks) + len(ws))
+        + ([wide(2 * LAT)] if has_tail else [])
+        + [pl.BlockSpec((9, TILE), lambda n: (0, n + skip))],
+        out_specs=out_specs,
+        out_shape=out_shape,
+        scratch_shapes=[
+            pltpu.VMEM((rows, 4 * d), jnp.bfloat16),
+            pltpu.VMEM((TILE // SUB, 4 * d, SUB), jnp.bfloat16),
+            pltpu.VMEM((hid_rows, SUB), jnp.float32),
+            pltpu.VMEM((hid_rows, SUB), jnp.float32),
+            pltpu.SemaphoreType.DMA,
+            pltpu.SemaphoreType.DMA((TILE // SUB,)),
+            pltpu.SemaphoreType.DMA,
+        ],
+        compiler_params=pltpu.CompilerParams(vmem_limit_bytes=VMEM_LIMIT),
+        cost_estimate=pl.CostEstimate(
+            flops=2 * rows * 4 * d * units, bytes_accessed=8 * d * units, transcendentals=0
+        ),
+        name="first",
+    )(place, gain, *toks, *ws, *([tail] if has_tail else []), conv_kernel)
+
+
+def second_kernel(quarters, place_ref, act_l, act_r, own, sib, *refs):
+    pieces, refs = refs[: 4 * len(quarters)], refs[4 * len(quarters) :]
+    out_ref, wbuf, buf_l, buf_r, wsem, asem = refs
+    scen, row = place_ref[0], place_ref[1]
+    n, count = pl.program_id(0), pl.num_programs(0)
+    width = out_ref.shape[1] // 2
+    half = width // 2
+    own_at = pl.multiple_of(scen * half, half)
+    other_at = pl.multiple_of((1 - scen) * half, half)
+
+    def copies(step, slot):
+        for side in range(2):
+            copy_tile(2 * step + side, slot, side * width)
+
+    def copy_tile(tile, slot, at):
+        source = row ^ (tile // len(quarters))
+        for i, quarter in enumerate(quarters):
+            mine = lax.rem(tile, len(quarters)) == i
+
+            for j, ref in ((0, own), (1, sib)):
+
+                @pl.when(mine & (source == j))
+                def _():
+                    pltpu.make_async_copy(
+                        ref.at[:, pl.ds(quarter * width, width)],
+                        wbuf.at[slot, :, pl.ds(at, width)],
+                        wsem.at[slot],
+                    ).start()
+
+            for j in (2, 3):
+
+                @pl.when(mine & (source == j))
+                def _():
+                    for k, off in ((0, own_at), (1, other_at)):
+                        pltpu.make_async_copy(
+                            pieces[4 * i + 2 * (j - 2) + k],
+                            wbuf.at[slot, :, pl.ds(pl.multiple_of(at + off, half), half)],
+                            wsem.at[slot],
+                        ).start()
+
+    @pl.when(n == 0)
+    def _():
+        copies(0, 0)
+        loads = [
+            pltpu.make_async_copy(ref, buf, asem.at[i])
+            for i, (ref, buf) in enumerate(((act_l, buf_l), (act_r, buf_r)))
+        ]
+        for load in loads:
+            load.start()
+        copies(1, 1)
+        for load in loads:
+            load.wait()
+
+    slot = lax.rem(n, 3)
+
+    @pl.when(n + 2 < count)
+    def _():
+        copies(n + 2, lax.rem(n + 2, 3))
+
+    pltpu.make_async_copy(wbuf.at[slot], wbuf.at[slot], wsem.at[slot]).wait()
+    k = act_l.shape[1]
+    total = jnp.dot(buf_l[...], wbuf[slot, pl.ds(0, k), :], preferred_element_type=jnp.float32)
+    total += jnp.dot(buf_r[...], wbuf[slot, pl.ds(k, k), :], preferred_element_type=jnp.float32)
+    out_ref[...] = total.astype(out_ref.dtype)
+
+
+def second(place, acts, shards, pieces, quarters):
+    rows, k = acts[0].shape
+    width = shards[0].shape[1] // 4
+    count = 4 * len(quarters)
+    any_spec = pl.BlockSpec(memory_space=pl.ANY)
+    used = [p for quarter in quarters for p in pieces[quarter]]
+    return pl.pallas_call(
+        functools.partial(second_kernel, quarters),
+        grid=(count // 2,),
+        in_specs=[pl.BlockSpec(memory_space=pltpu.SMEM)] + [any_spec] * (4 + len(used)),
+        out_specs=pl.BlockSpec((rows, 2 * width), lambda n: (0, n)),
+        out_shape=jax.ShapeDtypeStruct((rows, count * width), jnp.bfloat16),
+        scratch_shapes=[
+            pltpu.VMEM((3, 2 * k, 2 * width), jnp.bfloat16),
+            pltpu.VMEM((rows, k), jnp.bfloat16),
+            pltpu.VMEM((rows, k), jnp.bfloat16),
+            pltpu.SemaphoreType.DMA((3,)),
+            pltpu.SemaphoreType.DMA((2,)),
+        ],
+        compiler_params=pltpu.CompilerParams(vmem_limit_bytes=VMEM_LIMIT),
+        cost_estimate=pl.CostEstimate(
+            flops=4 * rows * k * count * width, bytes_accessed=4 * k * count * width, transcendentals=0
+        ),
+        name="second",
+    )(place, *acts, *shards, *used)
+
+
+def scatter(v):
+    return lax.psum_scatter(v, "col", scatter_dimension=1, tiled=True)
+
+
+def per_device(tokens, norm_gain, w_in, conv_kernel, w_out):
+    rows, d = tokens.shape
+    scen, row, col = (lax.axis_index(a) for a in ("scen", "row", "col"))
+    place = jnp.stack([scen, row, col]).astype(jnp.int32)
+    lons = rows // LAT
+    la = lons // 2
+    cut = (la + 2) * LAT
+
+    h = (d * 13 // 64) // 16 * 16
+    xs_in = [lax.dynamic_slice(w_in, (scen * 2 * h + i * h, 0), (h, w_in.shape[1])) for i in range(2)]
+    xs_in.append(w_in[4 * h :])
+    q = d // 4
+    os_in = [lax.dynamic_slice(w_out, (0, i * q + scen * (q // 2)), (w_out.shape[0], q // 2)) for i in range(4)]
+    gain = norm_gain.reshape(4, d)
+    wide = extended(tokens, (("row", 0),), LAT)
+    na, nb = wide[:cut], wide[cut:]
+    (na, nb), (x0i,) = gate((na, nb), (xs_in[0],))
+    x0 = swap_x(x0i)
+    d1, u1 = down(na, 1), up(na, 1)
+    sib = swap_core(w_in)
+    (x0, sib, d1, u1), (x1i,) = gate((x0, sib, d1, u1), (xs_in[1],))
+    x1, y0 = swap_x(x1i), swap_scen(x0)
+    d2, u2 = down(d1, 2), up(u1, 2)
+    o_sib, cx0 = cores(w_out, x0)
+    (x1, y0, o_sib, cx0, d2, u2), (x2i,) = gate((x1, y0, o_sib, cx0, d2, u2), (xs_in[2],))
+    xd, y1 = swap_x(x2i), swap_scen(x1)
+    d3, u3 = down(d2, 3), up(u2, 3)
+    cy0, cx1 = cores(y0, x1)
+    (xd, y1, cy0, cx1, d3, u3), (o0i, nb) = gate((xd, y1, cy0, cx1, d3, u3), (os_in[0], nb))
+    ox0 = swap_x(o0i)
+    e1, f1 = down(nb, 1), up(nb, 1)
+    cxd, cy1 = cores(xd, y1)
+    toks_a = [na, d1, d2, d3, u1, u2, u3]
+    ws = [w_in, sib, x0, y0, x1, y1, xd, cx0, cy0, cx1, cy1, cxd]
+    act_a0, tail0, norm_a = first(place, gain, toks_a, ws, conv_kernel, None, 0, la)
+    (norm_a, ox0, e1, f1), (o1i,) = gate((norm_a, ox0, e1, f1), (os_in[1],))
+    ox1, oy0 = swap_x(o1i), swap_scen(ox0)
+    e2, f2 = down(e1, 2), up(f1, 2)
+    cox0 = swap_core(ox0)
+    act_a1, tail1 = first(place, gain, [norm_a], ws, conv_kernel, None, 1, la)
+    (act_a1, ox1, oy0, cox0, e2, f2), (o2i,) = gate((act_a1, ox1, oy0, cox0, e2, f2), (os_in[2],))
+    coy0 = swap_core(oy0)
+    ox2, oy1 = swap_x(o2i), swap_scen(ox1)
+    e3, f3 = down(e2, 3), up(f2, 3)
+    shards = (w_out, o_sib)
+    pieces = [(ox0, oy0, cox0, coy0), None, None, None]
+    p0 = second(place, (act_a0, act_a1), shards, pieces, (0,))
+    r0 = scatter(p0)
+    (p0, ox2, oy1, act_a1, e3, f3), (o3i, ox1) = gate((p0, ox2, oy1, act_a1, e3, f3), (os_in[3], ox1))
+    ox3, oy2 = swap_x(o3i), swap_scen(ox2)
+    coy1, cox1 = cores(oy1, ox1)
+    pieces[1] = (ox1, oy1, cox1, coy1)
+    p1 = second(place, (act_a0, act_a1), shards, pieces, (1,))
+    r1 = scatter(p1)
+    (p1, ox3, oy2, r0), (ox2, nb) = gate((p1, ox3, oy2, r0), (ox2, nb))
+    oy3 = swap_scen(ox3)
+    coy2, cox2 = cores(oy2, ox2)
+    toks_b = [nb, e1, e2, e3, f1, f2, f3]
+    act_b0, norm_b = first(place, gain, toks_b, ws, conv_kernel, tail0, 0, lons - la)
+    (norm_b, oy3, coy2, cox2, act_a1, r1), (ox3,) = gate((norm_b, oy3, coy2, cox2, act_a1, r1), (ox3,))
+    coy3, cox3 = cores(oy3, ox3)
+    (norm_b, coy3, cox3, act_a1), _ = gate((norm_b, coy3, cox3, act_a1), ())
+    pieces[2] = (ox2, oy2, cox2, coy2)
+    pieces[3] = (ox3, oy3, cox3, coy3)
+    p2 = second(place, (act_a0, act_a1), shards, pieces, (2, 3))
+    r2 = scatter(p2)
+    (p2, norm_b), _ = gate((p2, norm_b), ())
+    (act_b1,) = first(place, gain, [norm_b], ws, conv_kernel, tail1, 1, lons - la)
+    s0 = second(place, (act_b0, act_b1), shards, pieces, (0, 1))
+    (s0, act_b1, r2), _ = gate((s0, act_b1, r2), ())
+    s1 = second(place, (act_b0, act_b1), shards, pieces, (2, 3))
+    s0, s1 = scatter(s0), scatter(s1)
+    mixed = jnp.concatenate(
+        [jnp.concatenate([r0, r1, r2], axis=1), jnp.concatenate([s0, s1], axis=1)], axis=0
+    )
+    return (tokens.astype(jnp.float32) + mixed.astype(jnp.float32)).astype(jnp.bfloat16)
+
+
 def solution(mesh):
     placed = (P(("scen", "row"), "col"), P(), P("row", "col"), P(None, "col"), P("col", "row"))
+    sizes = tuple(mesh.shape[a] for a in ("scen", "row", "col"))
     return jax.shard_map(
-        per_device, mesh=mesh, in_specs=placed, out_specs=P(("scen", "row"), "col"), check_vma=False
+        per_device if sizes == (2, 4, 4) else any_mesh,
+        mesh=mesh,
+        in_specs=placed,
+        out_specs=P(("scen", "row"), "col"),
+        check_vma=False,
     )

time: 1020 us -> 546 us (0.54)
  waiting for transfers between devices: 814 us -> 268 us
  Pallas kernels: 0 us -> 186 us
  matrix products: 104 us -> 0 us
  other arithmetic: 85.4 us -> 8.55 us
  starting transfers between devices: 1.91 us -> 44.5 us
  local copies, waits for them, and re-layouts: 0.15 us -> 16.8 us
    all_gather x3 -> x0, waiting for transfers between devices: 450 us -> none  [the longest x1 194 us: per_device(): lax.all_gather(w_in, 'row', axis=0, tiled=True)]
    reduce_scatter x1 -> x5, waiting for transfers between devices: 347 us -> 115 us  [scatter(): return lax.psum_scatter(v, 'col', scatter_dimension=1, tiled=True)]
    pallas_call x0 -> x9, Pallas kernels: none -> 186 us  [the longest x4 106 us: first(): pl.pallas_call(functools.partial(first_kernel, has_tail, len(toks), len(w...]
    ppermute x0 -> x40, waiting for transfers between devices: none -> 147 us  [the longest x6 78.5 us: down(): return lax.ppermute(v, 'col', [(i, i - 1) for i in range(1, 5 - hop)])]
    dot_general x2 -> x0, matrix products: 104 us -> none  [the longest x1 52.9 us: per_device(): jnp.dot(act, lax.all_gather(w_out, 'row', axis=1, tiled=True), preferred_...]
    convert_element_type x3 -> x1, other arithmetic: 78.3 us -> 6.65 us  [per_device(): (tokens.astype(jnp.float32) + mixed.astype(jnp.float32)).astype(jnp.bfloa...]
    ppermute x0 -> x40, starting transfers between devices: none -> 41.3 us  [the longest x6 15.1 us: up(): return lax.ppermute(v, 'col', [(i, i + 1) for i in range(hop - 1, 3)])]
    ppermute x1, waiting for transfers between devices: 14.9 us -> 0.01 us  [extended(): lax.ppermute(tail, axis, [(i, (i + 1) % count) for i in range(count)])]
  transfers between devices with their start and end apart: 6 -> 47, of which waited for: 5 -> 23; matrix products, arithmetic and copies ran while one was open for 13% -> 2% of each run, Pallas kernels for 0% -> 31%
where the time goes in v2:
time: 546 us; the launch traced here: 538 us
  waiting for transfers between devices  268 us (49%)
  Pallas kernels  186 us (34%)
  starting transfers between devices  44.5 us (8%)
  local copies, waits for them, and re-layouts  16.8 us (3%)
  between operations  14 us (3%)
  other arithmetic  8.55 us (2%)
    reduce_scatter x5, waiting for transfers between devices, scatter(): return lax.psum_scatter(v, 'col', scatter_dimension=1, tiled=True)  115 us
    pallas_call x4, Pallas kernels, first(): pl.pallas_call(functools.partial(first_kernel, has_tail, len(toks), len(w...  106 us
    pallas_call x5, Pallas kernels, second(): pl.pallas_call(functools.partial(second_kernel, quarters), grid=(count //...  79.7 us
    ppermute x6, waiting for transfers between devices, down(): return lax.ppermute(v, 'col', [(i, i - 1) for i in range(1, 5 - hop)])  78.5 us
    ppermute x6, waiting for transfers between devices, up(): return lax.ppermute(v, 'col', [(i, i + 1) for i in range(hop - 1, 3)])  30.2 us
    ppermute x7, waiting for transfers between devices, swap_x(): return lax.ppermute(v, 'row', [(i, i ^ 2) for i in range(4)])  21.9 us
    ppermute x6, starting transfers between devices, up(): return lax.ppermute(v, 'col', [(i, i + 1) for i in range(hop - 1, 3)])  15.1 us
    ppermute x15, waiting for transfers between devices, swap_core(): return lax.ppermute(v, 'row', [(i, i ^ 1) for i in range(4)])  14.4 us
  transfers between devices with their start and end apart: 47, of which 23 were waited for; matrix products, arithmetic and copies ran while one was open for 2% of the time, Pallas kernels for 31%

profile of v2, /device:TPU:0, one launch (start us, length us, event | category | flops | bytes accessed | tf_op | source)
XLA Modules:
  0.0 537.9 jit_solution(16259585369120681755)
XLA Ops:
  8.0 2.6 collective-permute-start.1
  10.6 2.3 constant_dynamic-slice_fusion.4
  12.9 7.0 %collective-permute-done.1 = bf16[40,1024]{1,0:T(8,128)(2,1)S(1)} collective-permute-done((bf16[40,1024]{1,0:T(8,128)(2,1)S(1)}, bf16[40,1024]{1,0:T(8,128)(2,1)S(1)}, u32[]{:S(2)}, u32[]{:S(2)}) %collective-permute-start.1) | collective-permute-done | bytes 81952 | tf_op jit(solution)/shard_map/ppermute | solution.py:28
  21.2 3.0 collective-permute-start.2
  24.2 3.6 collective-permute-start.5
  27.8 1.3 collective-permute-start.4
  29.1 30.2 %collective-permute-done.5.refs_4_ = bf16[720,1024]{1,0:T(8,128)(2,1)S(1)} collective-permute-done((bf16[720,1024]{1,0:T(8,128)(2,1)S(1)}, bf16[720,1024]{1,0:T(8,128)(2,1)S(1)}, u32[]{:S(2)}, u32[]{:S(2)}) %collective-permute-start.5) | collective-permute-done | bytes 1474592 | tf_op jit(solution)/shard_map/ppermute | solution.py:95
  59.3 4.2 collective-permute-done.4.refs_1_
  64.7 1.5 collective-permute-start.7
  67.5 1.8 collective-permute-start.11
  69.3 2.7 slice.21
  72.0 29.7 %collective-permute-done.10.refs_2_ = bf16[720,1024]{1,0:T(8,128)(2,1)} collective-permute-done((bf16[720,1024]{1,0:T(8,128)(2,1)S(1)}, bf16[720,1024]{1,0:T(8,128)(2,1)}, u32[]{:S(2)}, u32[]{:S(2)}) %collective-permute-start.10) | collective-permute-done | bytes 1474592 | tf_op jit(solution)/shard_map/ppermute | solution.py:91
  101.8 1.5 collective-permute-done.6.refs_11_.refs_5_
  104.7 1.5 collective-permute-start.13
  108.4 1.5 collective-permute-start.12
  111.2 1.8 collective-permute-start.17
  113.0 4.4 constant_dynamic-slice_fusion
  117.4 30.0 %collective-permute-done.16.refs_3_ = bf16[720,1024]{1,0:T(8,128)(2,1)} collective-permute-done((bf16[720,1024]{1,0:T(8,128)(2,1)}, bf16[720,1024]{1,0:T(8,128)(2,1)}, u32[]{:S(2)}, u32[]{:S(2)}) %collective-permute-start.16) | collective-permute-done | bytes 1474592 | tf_op jit(solution)/shard_map/ppermute | solution.py:91
  147.4 3.7 collective-permute-done.18.refs_18_.refs_12_
  151.3 4.3 collective-permute-start.22
  158.1 1.5 collective-permute-start.20
  159.6 29.4 %first.4 = (bf16[640,2048]{1,0:T(8,128)(2,1)}, bf16[80,2048]{1,0:T(8,128)(2,1)}, bf16[720,4096]{1,0:T(8,128)(2,1)}) custom-call(s32[3]{0:T(128)} %pad_add_fusion.place_ref, f32[4,1024]{1,0:T(4,128)} %reshape.3.gain_ref, bf16[720,1024]{1,0:T(8,128)(2,1)} %copy-done.5, bf16[720,1024]{1,0:T(8,128)(2,1)} %copy-done.15, ...), custom_call_target="tpu_custom_call" | custom-call | flops 12079595520 | bytes 16777216 | tf_op jit(solution)/shard_map/first/pallas_call | solution.py:255
  189.0 1.3 collective-permute-start.26
  190.3 1.8 collective-permute-start.27
  193.9 25.4 %first.5 = (bf16[640,2048]{1,0:T(8,128)(2,1)}, bf16[80,2048]{1,0:T(8,128)(2,1)}) custom-call(s32[3]{0:T(128)} %pad_add_fusion.place_ref, f32[4,1024]{1,0:T(4,128)} %reshape.3.gain_ref, bf16[720,4096]{1,0:T(8,128)(2,1)} %get-tuple-element.107.refs_0_, bf16[1024,4096]{1,0:T(8,128)(2,1)} %refs_1_.3, bf16[1024,4096]{1,0:T(8,128)(2,1)} %collective-permute-done.3.refs_8_.refs_2_, ...), custom_call_target="tpu_custom_call" | custom-call | flops 12079595520 | bytes 16777216 | tf_op jit(solution)/shard_map/first/pallas_call | solution.py:255
  219.3 2.9 collective-permute-done.26.refs_2_
  223.5 1.8 collective-permute-start.32
  227.7 12.4 %second.5 = bf16[640,1024]{1,0:T(8,128)(2,1)} custom-call(s32[3]{0:T(128)} %pad_add_fusion.place_ref, bf16[640,2048]{1,0:T(8,128)(2,1)} %get-tuple-element.103.act_l, bf16[640,2048]{1,0:T(8,128)(2,1)} %get-tuple-element.144.act_r, bf16[4096,1024]{1,0:T(8,128)(2,1)} %own.9, bf16[4096,1024]{1,0:T(8,128)(2,1)} %collective-permute-done.8.sib, ...), custom_call_target="tpu_custom_call" | custom-call | flops 5368709120 | bytes 8388608 | tf_op jit(solution)/shard_map/second/pallas_call | solution.py:353
  240.2 11.0 %collective-permute-done.29.refs_0_ = bf16[4096,128]{1,0:T(8,128)(2,1)} collective-permute-done((bf16[4096,128]{1,0:T(8,128)(2,1)}, bf16[4096,128]{1,0:T(8,128)(2,1)}, u32[]{:S(2)}, u32[]{:S(2)}) %collective-permute-start.29) | collective-permute-done | bytes 1048608 | tf_op jit(solution)/shard_map/ppermute | solution.py:72
  251.9 11.7 %collective-permute-done.31.refs_3_ = bf16[640,1024]{1,0:T(8,128)(2,1)} collective-permute-done((bf16[640,1024]{1,0:T(8,128)(2,1)}, bf16[640,1024]{1,0:T(8,128)(2,1)}, u32[]{:S(2)}, u32[]{:S(2)}) %collective-permute-start.31) | collective-permute-done | bytes 1310752 | tf_op jit(solution)/shard_map/ppermute | solution.py:91
  263.6 2.9 collective-permute-done.33.refs_3_.refs_7_
  267.7 1.7 collective-permute-start.36
  270.3 12.4 %second.6 = bf16[640,1024]{1,0:T(8,128)(2,1)} custom-call(s32[3]{0:T(128)} %pad_add_fusion.place_ref, bf16[640,2048]{1,0:T(8,128)(2,1)} %get-tuple-element.103.act_l, bf16[640,2048]{1,0:T(8,128)(2,1)} %get-tuple-element.144.act_r, bf16[4096,1024]{1,0:T(8,128)(2,1)} %own.9, bf16[4096,1024]{1,0:T(8,128)(2,1)} %collective-permute-done.8.sib, ...), custom_call_target="tpu_custom_call" | custom-call | flops 5368709120 | bytes 8388608 | tf_op jit(solution)/shard_map/second/pallas_call | solution.py:353
  283.0 9.4 %collective-permute-done.35.refs_4_ = bf16[4096,128]{1,0:T(8,128)(2,1)} collective-permute-done((bf16[4096,128]{1,0:T(8,128)(2,1)}, bf16[4096,128]{1,0:T(8,128)(2,1)}, u32[]{:S(2)}, u32[]{:S(2)}) %collective-permute-start.35) | collective-permute-done | bytes 1048608 | tf_op jit(solution)/shard_map/ppermute | solution.py:72
  293.2 1.7 collective-permute-start.37
  294.8 1.3 collective-permute-done.38.refs_3_
  296.3 27.4 %first.6 = (bf16[640,2048]{1,0:T(8,128)(2,1)}, bf16[640,4096]{1,0:T(8,128)(2,1)}) custom-call(s32[3]{0:T(128)} %pad_add_fusion.place_ref, f32[4,1024]{1,0:T(4,128)} %reshape.3.gain_ref, bf16[640,1024]{1,0:T(8,128)(2,1)} %pad_maximum_fusion.1.refs_0_, bf16[640,1024]{1,0:T(8,128)(2,1)} %collective-permute-done.21.refs_1_, ...), custom_call_target="tpu_custom_call" | custom-call | flops 10737418240 | bytes 16777216 | tf_op jit(solution)/shard_map/first/pallas_call | solution.py:255
  323.8 6.0 %reduce-scatter.8.cloned.1.call-done = bf16[640,256]{1,0:T(8,128)(2,1)} async-done(((bf16[640,1024]{1,0:T(8,128)(2,1)}), bf16[640,256]{1,0:T(8,128)(2,1)}) %reduce-scatter.8.cloned.1.call-update) | async-done | bytes 327696 | tf_op jit(solution)/shard_map/reduce_scatter | solution.py:375
  329.7 2.9 collective-permute-done.40.refs_7_
  332.7 2.7 collective-permute-done.41.refs_6_
  336.4 18.3 %second.7 = bf16[640,2048]{1,0:T(8,128)(2,1)} custom-call(s32[3]{0:T(128)} %pad_add_fusion.place_ref, bf16[640,2048]{1,0:T(8,128)(2,1)} %get-tuple-element.103.act_l, bf16[640,2048]{1,0:T(8,128)(2,1)} %get-tuple-element.144.act_r, bf16[4096,1024]{1,0:T(8,128)(2,1)} %own.9, bf16[4096,1024]{1,0:T(8,128)(2,1)} %collective-permute-done.8.sib, ...), custom_call_target="tpu_custom_call" | custom-call | flops 10737418240 | bytes 16777216 | tf_op jit(solution)/shard_map/second/pallas_call | solution.py:353
  355.1 23.9 %first.7.act_r = bf16[640,2048]{1,0:T(8,128)(2,1)} custom-call(s32[3]{0:T(128)} %pad_add_fusion.place_ref, f32[4,1024]{1,0:T(4,128)} %reshape.3.gain_ref, bf16[640,4096]{1,0:T(8,128)(2,1)} %get-tuple-element.150.refs_0_, bf16[1024,4096]{1,0:T(8,128)(2,1)} %refs_1_.3, bf16[1024,4096]{1,0:T(8,128)(2,1)} %collective-permute-done.3.refs_8_.refs_2_, ...), custom_call_target="tpu_custom_call" | custom-call | flops 10737418240 | bytes 16777216 | tf_op jit(solution)/shard_map/first/pallas_call | solution.py:255
  378.9 18.4 %second.8 = bf16[640,2048]{1,0:T(8,128)(2,1)} custom-call(s32[3]{0:T(128)} %pad_add_fusion.place_ref, bf16[640,2048]{1,0:T(8,128)(2,1)} %get-tuple-element.138.act_l, bf16[640,2048]{1,0:T(8,128)(2,1)} %first.7.act_r, bf16[4096,1024]{1,0:T(8,128)(2,1)} %own.9, bf16[4096,1024]{1,0:T(8,128)(2,1)} %collective-permute-done.8.sib, bf16[4096,128]{1,0:T(8,128)(2,1)} %copy-done.6, ...), custom_call_target="tpu_custom_call" | custom-call | flops 10737418240 | bytes 16777216 | tf_op jit(solution)/shard_map/second/pallas_call | solution.py:353
  397.3 19.1 %reduce-scatter.10.cloned.1.call-done = bf16[640,512]{1,0:T(8,128)(2,1)} async-done(((bf16[640,2048]{1,0:T(8,128)(2,1)}), bf16[640,512]{1,0:T(8,128)(2,1)}) %reduce-scatter.10.cloned.1.call-update) | async-done | bytes 655376 | tf_op jit(solution)/shard_map/reduce_scatter | solution.py:375
  416.5 18.3 %second.9 = bf16[640,2048]{1,0:T(8,128)(2,1)} custom-call(s32[3]{0:T(128)} %pad_add_fusion.place_ref, bf16[640,2048]{1,0:T(8,128)(2,1)} %get-tuple-element.138.act_l, bf16[640,2048]{1,0:T(8,128)(2,1)} %first.7.act_r, bf16[4096,1024]{1,0:T(8,128)(2,1)} %own.9, bf16[4096,1024]{1,0:T(8,128)(2,1)} %collective-permute-done.8.sib, ...), custom_call_target="tpu_custom_call" | custom-call | flops 10737418240 | bytes 16777216 | tf_op jit(solution)/shard_map/second/pallas_call | solution.py:353
  434.8 35.6 %reduce-scatter.12.cloned.1.call-done = bf16[640,512]{1,0:T(8,128)(2,1)} async-done(((bf16[640,2048]{1,0:T(8,128)(2,1)}), bf16[640,512]{1,0:T(8,128)(2,1)}) %reduce-scatter.12.cloned.1.call-update) | async-done | bytes 655376 | tf_op jit(solution)/shard_map/reduce_scatter | solution.py:375
  470.4 54.0 %reduce-scatter.14.cloned.1.call-done = bf16[640,512]{1,0:T(8,128)(2,1)} async-done(((bf16[640,2048]{1,0:T(8,128)(2,1)}), bf16[640,512]{1,0:T(8,128)(2,1)}) %reduce-scatter.14.cloned.1.call-update) | async-done | bytes 655376 | tf_op jit(solution)/shard_map/reduce_scatter | solution.py:375
  524.3 6.7 %add_convert_fusion = bf16[1280,1024]{1,0:T(8,128)(2,1)} fusion(bf16[1280,1024]{1,0:T(8,128)(2,1)S(1)} %copy-done, bf16[640,512]{1,0:T(8,128)(2,1)} %reduce-scatter.14.cloned.1.call-done, bf16[640,512]{1,0:T(8,128)(2,1)} %reduce-scatter.12.cloned.1.call-done, bf16[640,512]{1,0:T(8,128)(2,1)S(1)} %copy-done.12, ...), kind=kLoop, calls=%fused_computation | loop fusion | flops 17039360 | bytes 7864320 | tf_op jit(solution)/shard_map/convert_element_type | solution.py:453
  (105 shorter events, 23.9 us)
Async XLA Ops:
  6.5 286.6 %reduce-scatter.6.cloned.1.call-start = ((), (), s32[]{:S(2)}) async-start(), calls=%async_computation.5 | async-start | bytes 1638400 | tf_op jit(solution)/shard_map/reduce_scatter | solution.py:375
  6.5 56.9 %collective-permute-start.3 = (bf16[1024,4096]{1,0:T(8,128)(2,1)}, bf16[1024,4096]{1,0:T(8,128)(2,1)}, u32[]{:S(2)}, u32[]{:S(2)}) collective-permute-start(bf16[1024,4096]{1,0:T(8,128)(2,1)} %refs_1_.3), channel_id=1, source_target_pairs={{0,4},{4,0},{8,12},{12,8},{1,5},{5,1},{9,13},{13,9},{2,6},{6,2},{1... | collective-permute-start | bytes 25165832 | tf_op jit(solution)/shard_map/ppermute | solution.py:76
  7.0 56.5 %collective-permute-start.8 = (bf16[4096,1024]{1,0:T(8,128)(2,1)}, bf16[4096,1024]{1,0:T(8,128)(2,1)}, u32[]{:S(2)}, u32[]{:S(2)}) collective-permute-start(bf16[4096,1024]{1,0:T(8,128)(2,1)} %own.9), channel_id=1, source_target_pairs={{0,4},{4,0},{8,12},{12,8},{1,5},{5,1},{9,13},{13,9},{2,6},{6,2},{1... | collective-permute-start | bytes 25165832 | tf_op jit(solution)/shard_map/ppermute | solution.py:76
  8.0 11.9 %collective-permute-start.1 = (bf16[40,1024]{1,0:T(8,128)(2,1)S(1)}, bf16[40,1024]{1,0:T(8,128)(2,1)S(1)}, u32[]{:S(2)}, u32[]{:S(2)}) collective-permute-start(bf16[40,1024]{1,0:T(8,128)(2,1)S(1)} %get-tuple-element.161), channel_id=1, source_target_pairs={{4,0},{8,4},{12,8},{0,12},{5,1},{9,5},{13,9},{1,13},{6,2},{10,6},{... | collective-permute-start | bytes 245768 | tf_op jit(solution)/shard_map/ppermute | solution.py:28
  10.6 10.5 %collective-permute-start = (bf16[40,1024]{1,0:T(8,128)(2,1)S(1)}, bf16[40,1024]{1,0:T(8,128)(2,1)S(1)}, u32[]{:S(2)}, u32[]{:S(2)}) collective-permute-start(bf16[40,1024]{1,0:T(8,128)(2,1)S(1)} %get-tuple-element.162), channel_id=1, source_target_pairs={{0,4},{4,8},{8,12},{12,0},{1,5},{5,9},{9,13},{13,1},{2,6},{6,10},{... | collective-permute-start | bytes 245768 | tf_op jit(solution)/shard_map/ppermute | solution.py:26
  21.2 42.2 %collective-permute-start.2 = (bf16[208,4096]{1,0:T(8,128)(2,1)S(1)}, bf16[208,4096]{1,0:T(8,128)(2,1)S(1)}, u32[]{:S(2)}, u32[]{:S(2)}) collective-permute-start(bf16[208,4096]{1,0:T(8,128)(2,1)S(1)} %get-tuple-element.81), channel_id=1, source_target_pairs={{0,8},{4,12},{8,0},{12,4},{1,9},{5,13},{9,1},{13,5},{2,10},{6,14},... | collective-permute-start | bytes 5111816 | tf_op jit(solution)/shard_map/ppermute | solution.py:72
  24.2 35.0 %collective-permute-start.5 = (bf16[720,1024]{1,0:T(8,128)(2,1)S(1)}, bf16[720,1024]{1,0:T(8,128)(2,1)S(1)}, u32[]{:S(2)}, u32[]{:S(2)}) collective-permute-start(bf16[720,1024]{1,0:T(8,128)(2,1)S(1)} %pad_maximum_fusion.refs_0_), channel_id=1, source_target_pairs={{0,1},{1,2},{2,3},{4,5},{5,6},{6,7},{8,9},{9,10},{10,11},{12,13},{... | collective-permute-start | bytes 4423688 | tf_op jit(solution)/shard_map/ppermute | solution.py:95
  27.8 35.7 %collective-permute-start.4 = (bf16[720,1024]{1,0:T(8,128)(2,1)S(1)}, bf16[720,1024]{1,0:T(8,128)(2,1)S(1)}, u32[]{:S(2)}, u32[]{:S(2)}) collective-permute-start(bf16[720,1024]{1,0:T(8,128)(2,1)S(1)} %pad_maximum_fusion.refs_0_), channel_id=1, source_target_pairs={{1,0},{2,1},{3,2},{5,4},{6,5},{7,6},{9,8},{10,9},{11,10},{13,12},{... | collective-permute-start | bytes 4423688 | tf_op jit(solution)/shard_map/ppermute | solution.py:91
  63.5 38.3 %collective-permute-start.9 = (bf16[208,4096]{1,0:T(8,128)(2,1)S(1)}, bf16[208,4096]{1,0:T(8,128)(2,1)S(1)}, u32[]{:S(2)}, u32[]{:S(2)}) collective-permute-start(bf16[208,4096]{1,0:T(8,128)(2,1)S(1)} %collective-permute-done.2.refs_9_.refs_3_), channel_id=1, source_target_pairs={{0,4},{4,0},{8,12},{12,8},{1,5},{5,1},{9,13},{13,9},{2,6},{6,2},{1... | collective-permute-start | bytes 5111816 | tf_op jit(solution)/shard_map/ppermute | solution.py:76
  63.6 39.7 %collective-permute-start.6 = (bf16[208,4096]{1,0:T(8,128)(2,1)S(1)}, bf16[208,4096]{1,0:T(8,128)(2,1)}, u32[]{:S(2)}, u32[]{:S(2)}) collective-permute-start(bf16[208,4096]{1,0:T(8,128)(2,1)S(1)} %get-tuple-element.83), channel_id=1, source_target_pairs={{0,8},{4,12},{8,0},{12,4},{1,9},{5,13},{9,1},{13,5},{2,10},{6,14},... | collective-permute-start | bytes 5111816 | tf_op jit(solution)/shard_map/ppermute | solution.py:72
  64.7 38.7 %collective-permute-start.7 = (bf16[208,4096]{1,0:T(8,128)(2,1)S(1)}, bf16[208,4096]{1,0:T(8,128)(2,1)S(1)}, u32[]{:S(2)}, u32[]{:S(2)}) collective-permute-start(bf16[208,4096]{1,0:T(8,128)(2,1)S(1)} %collective-permute-done.2.refs_9_.refs_3_), channel_id=1, source_target_pairs={{0,16},{16,0},{1,17},{17,1},{2,18},{18,2},{3,19},{19,3},{4,20},{20... | collective-permute-start | bytes 5111816 | tf_op jit(solution)/shard_map/ppermute | solution.py:87
  66.3 35.5 %collective-permute-start.10 = (bf16[720,1024]{1,0:T(8,128)(2,1)S(1)}, bf16[720,1024]{1,0:T(8,128)(2,1)}, u32[]{:S(2)}, u32[]{:S(2)}) collective-permute-start(bf16[720,1024]{1,0:T(8,128)(2,1)S(1)} %collective-permute-done.4.refs_1_), channel_id=1, source_target_pairs={{1,0},{2,1},{5,4},{6,5},{9,8},{10,9},{13,12},{14,13},{17,16},{18,1... | collective-permute-start | bytes 4423688 | tf_op jit(solution)/shard_map/ppermute | solution.py:91
  67.5 34.2 %collective-permute-start.11 = (bf16[720,1024]{1,0:T(8,128)(2,1)S(1)}, bf16[720,1024]{1,0:T(8,128)(2,1)}, u32[]{:S(2)}, u32[]{:S(2)}) collective-permute-start(bf16[720,1024]{1,0:T(8,128)(2,1)S(1)} %collective-permute-done.5.refs_4_), channel_id=1, source_target_pairs={{1,2},{2,3},{5,6},{6,7},{9,10},{10,11},{13,14},{14,15},{17,18},{18... | collective-permute-start | bytes 4423688 | tf_op jit(solution)/shard_map/ppermute | solution.py:95
  103.5 3.6 collective-permute-start.14
  104.7 42.6 %collective-permute-start.13 = (bf16[208,4096]{1,0:T(8,128)(2,1)}, bf16[208,4096]{1,0:T(8,128)(2,1)}, u32[]{:S(2)}, u32[]{:S(2)}) collective-permute-start(bf16[208,4096]{1,0:T(8,128)(2,1)} %collective-permute-done.6.refs_11_.refs_5_), channel_id=1, source_target_pairs={{0,16},{16,0},{1,17},{17,1},{2,18},{18,2},{3,19},{19,3},{4,20},{20... | collective-permute-start | bytes 5111816 | tf_op jit(solution)/shard_map/ppermute | solution.py:87
  108.2 39.1 %collective-permute-start.15 = (bf16[208,4096]{1,0:T(8,128)(2,1)}, bf16[208,4096]{1,0:T(8,128)(2,1)}, u32[]{:S(2)}, u32[]{:S(2)}) collective-permute-start(bf16[208,4096]{1,0:T(8,128)(2,1)} %collective-permute-done.6.refs_11_.refs_5_), channel_id=1, source_target_pairs={{0,4},{4,0},{8,12},{12,8},{1,5},{5,1},{9,13},{13,9},{2,6},{6,2},{1... | collective-permute-start | bytes 5111816 | tf_op jit(solution)/shard_map/ppermute | solution.py:76
  108.4 38.9 %collective-permute-start.12 = (bf16[192,4096]{1,0:T(8,128)(2,1)}, bf16[192,4096]{1,0:T(8,128)(2,1)}, u32[]{:S(2)}, u32[]{:S(2)}) collective-permute-start(bf16[192,4096]{1,0:T(8,128)(2,1)} %slice.21), channel_id=1, source_target_pairs={{0,8},{4,12},{8,0},{12,4},{1,9},{5,13},{9,1},{13,5},{2,10},{6,14},... | collective-permute-start | bytes 4718600 | tf_op jit(solution)/shard_map/ppermute | solution.py:72
  109.9 37.4 %collective-permute-start.16 = (bf16[720,1024]{1,0:T(8,128)(2,1)}, bf16[720,1024]{1,0:T(8,128)(2,1)}, u32[]{:S(2)}, u32[]{:S(2)}) collective-permute-start(bf16[720,1024]{1,0:T(8,128)(2,1)} %collective-permute-done.10.refs_2_), channel_id=1, source_target_pairs={{1,0},{5,4},{9,8},{13,12},{17,16},{21,20},{25,24},{29,28}} | collective-permute-start | bytes 4423688 | tf_op jit(solution)/shard_map/ppermute | solution.py:91
  111.2 36.1 %collective-permute-start.17 = (bf16[720,1024]{1,0:T(8,128)(2,1)}, bf16[720,1024]{1,0:T(8,128)(2,1)}, u32[]{:S(2)}, u32[]{:S(2)}) collective-permute-start(bf16[720,1024]{1,0:T(8,128)(2,1)} %collective-permute-done.11.refs_5_), channel_id=1, source_target_pairs={{2,3},{6,7},{10,11},{14,15},{18,19},{22,23},{26,27},{30,31}} | collective-permute-start | bytes 4423688 | tf_op jit(solution)/shard_map/ppermute | solution.py:95
  147.3 3.8 collective-permute-start.18
  151.2 8.5 %collective-permute-start.19 = (bf16[208,4096]{1,0:T(8,128)(2,1)}, bf16[208,4096]{1,0:T(8,128)(2,1)}, u32[]{:S(2)}, u32[]{:S(2)}) collective-permute-start(bf16[208,4096]{1,0:T(8,128)(2,1)} %collective-permute-done.13.refs_12_.refs_6_), channel_id=1, source_target_pairs={{0,4},{4,0},{8,12},{12,8},{1,5},{5,1},{9,13},{13,9},{2,6},{6,2},{1... | collective-permute-start | bytes 5111816 | tf_op jit(solution)/shard_map/ppermute | solution.py:76
  151.3 37.7 %collective-permute-start.22 = (bf16[640,1024]{1,0:T(8,128)(2,1)}, bf16[640,1024]{1,0:T(8,128)(2,1)}, u32[]{:S(2)}, u32[]{:S(2)}) collective-permute-start(bf16[640,1024]{1,0:T(8,128)(2,1)} %pad_maximum_fusion.1.refs_0_), channel_id=1, source_target_pairs={{0,1},{1,2},{2,3},{4,5},{5,6},{6,7},{8,9},{9,10},{10,11},{12,13},{... | collective-permute-start | bytes 3932168 | tf_op jit(solution)/shard_map/ppermute | solution.py:95
  155.6 33.4 %collective-permute-start.21 = (bf16[640,1024]{1,0:T(8,128)(2,1)}, bf16[640,1024]{1,0:T(8,128)(2,1)}, u32[]{:S(2)}, u32[]{:S(2)}) collective-permute-start(bf16[640,1024]{1,0:T(8,128)(2,1)} %pad_maximum_fusion.1.refs_0_), channel_id=1, source_target_pairs={{1,0},{2,1},{3,2},{5,4},{6,5},{7,6},{9,8},{10,9},{11,10},{13,12},{... | collective-permute-start | bytes 3932168 | tf_op jit(solution)/shard_map/ppermute | solution.py:91
  158.1 30.9 %collective-permute-start.20 = (bf16[4096,128]{1,0:T(8,128)(2,1)}, bf16[4096,128]{1,0:T(8,128)(2,1)S(1)}, u32[]{:S(2)}, u32[]{:S(2)}) collective-permute-start(bf16[4096,128]{1,0:T(8,128)(2,1)} %get-tuple-element.105), channel_id=1, source_target_pairs={{0,8},{4,12},{8,0},{12,4},{1,9},{5,13},{9,1},{13,5},{2,10},{6,14},... | collective-permute-start | bytes 3145736 | tf_op jit(solution)/shard_map/ppermute | solution.py:72
  189.0 33.2 %collective-permute-start.26 = (bf16[640,1024]{1,0:T(8,128)(2,1)}, bf16[640,1024]{1,0:T(8,128)(2,1)}, u32[]{:S(2)}, u32[]{:S(2)}) collective-permute-start(bf16[640,1024]{1,0:T(8,128)(2,1)} %collective-permute-done.21.refs_1_), channel_id=1, source_target_pairs={{1,0},{2,1},{5,4},{6,5},{9,8},{10,9},{13,12},{14,13},{17,16},{18,1... | collective-permute-start | bytes 3932168 | tf_op jit(solution)/shard_map/ppermute | solution.py:91
  190.3 31.9 %collective-permute-start.27 = (bf16[640,1024]{1,0:T(8,128)(2,1)}, bf16[640,1024]{1,0:T(8,128)(2,1)}, u32[]{:S(2)}, u32[]{:S(2)}) collective-permute-start(bf16[640,1024]{1,0:T(8,128)(2,1)} %collective-permute-done.22.refs_4_), channel_id=1, source_target_pairs={{1,2},{2,3},{5,6},{6,7},{9,10},{10,11},{13,14},{14,15},{17,18},{18... | collective-permute-start | bytes 3932168 | tf_op jit(solution)/shard_map/ppermute | solution.py:95
  192.2 27.1 %collective-permute-start.25 = (bf16[4096,128]{1,0:T(8,128)(2,1)S(1)}, bf16[4096,128]{1,0:T(8,128)(2,1)S(1)}, u32[]{:S(2)}, u32[]{:S(2)}) collective-permute-start(bf16[4096,128]{1,0:T(8,128)(2,1)S(1)} %collective-permute-done.20.refs_0_), channel_id=1, source_target_pairs={{0,4},{4,0},{8,12},{12,8},{1,5},{5,1},{9,13},{13,9},{2,6},{6,2},{1... | collective-permute-start | bytes 3145736 | tf_op jit(solution)/shard_map/ppermute | solution.py:76
  192.3 27.0 %collective-permute-start.24 = (bf16[4096,128]{1,0:T(8,128)(2,1)S(1)}, bf16[4096,128]{1,0:T(8,128)(2,1)S(1)}, u32[]{:S(2)}, u32[]{:S(2)}) collective-permute-start(bf16[4096,128]{1,0:T(8,128)(2,1)S(1)} %collective-permute-done.20.refs_0_), channel_id=1, source_target_pairs={{0,16},{16,0},{1,17},{17,1},{2,18},{18,2},{3,19},{19,3},{4,20},{20... | collective-permute-start | bytes 3145736 | tf_op jit(solution)/shard_map/ppermute | solution.py:87
  192.8 26.4 %collective-permute-start.23 = (bf16[4096,128]{1,0:T(8,128)(2,1)}, bf16[4096,128]{1,0:T(8,128)(2,1)}, u32[]{:S(2)}, u32[]{:S(2)}) collective-permute-start(bf16[4096,128]{1,0:T(8,128)(2,1)} %get-tuple-element.109), channel_id=1, source_target_pairs={{0,8},{4,12},{8,0},{12,4},{1,9},{5,13},{9,1},{13,5},{2,10},{6,14},... | collective-permute-start | bytes 3145736 | tf_op jit(solution)/shard_map/ppermute | solution.py:72
  222.2 4.6 collective-permute-start.28
  222.2 41.3 %collective-permute-start.31 = (bf16[640,1024]{1,0:T(8,128)(2,1)}, bf16[640,1024]{1,0:T(8,128)(2,1)}, u32[]{:S(2)}, u32[]{:S(2)}) collective-permute-start(bf16[640,1024]{1,0:T(8,128)(2,1)} %collective-permute-done.26.refs_2_), channel_id=1, source_target_pairs={{1,0},{5,4},{9,8},{13,12},{17,16},{21,20},{25,24},{29,28}} | collective-permute-start | bytes 3932168 | tf_op jit(solution)/shard_map/ppermute | solution.py:91
  223.5 40.1 %collective-permute-start.32 = (bf16[640,1024]{1,0:T(8,128)(2,1)}, bf16[640,1024]{1,0:T(8,128)(2,1)}, u32[]{:S(2)}, u32[]{:S(2)}) collective-permute-start(bf16[640,1024]{1,0:T(8,128)(2,1)} %collective-permute-done.27.refs_5_), channel_id=1, source_target_pairs={{2,3},{6,7},{10,11},{14,15},{18,19},{22,23},{26,27},{30,31}} | collective-permute-start | bytes 3932168 | tf_op jit(solution)/shard_map/ppermute | solution.py:95
  225.3 25.9 %collective-permute-start.29 = (bf16[4096,128]{1,0:T(8,128)(2,1)}, bf16[4096,128]{1,0:T(8,128)(2,1)}, u32[]{:S(2)}, u32[]{:S(2)}) collective-permute-start(bf16[4096,128]{1,0:T(8,128)(2,1)} %get-tuple-element.117), channel_id=1, source_target_pairs={{0,8},{4,12},{8,0},{12,4},{1,9},{5,13},{9,1},{13,5},{2,10},{6,14},... | collective-permute-start | bytes 3145736 | tf_op jit(solution)/shard_map/ppermute | solution.py:72
  226.3 25.6 %collective-permute-start.30 = (bf16[4096,128]{1,0:T(8,128)(2,1)}, bf16[4096,128]{1,0:T(8,128)(2,1)}, u32[]{:S(2)}, u32[]{:S(2)}) collective-permute-start(bf16[4096,128]{1,0:T(8,128)(2,1)} %collective-permute-done.23.refs_0_.refs_4_), channel_id=1, source_target_pairs={{0,16},{16,0},{1,17},{17,1},{2,18},{18,2},{3,19},{19,3},{4,20},{20... | collective-permute-start | bytes 3145736 | tf_op jit(solution)/shard_map/ppermute | solution.py:87
  240.2 89.5 %reduce-scatter.8.cloned.1.call-start = ((), (), s32[]{:S(2)}) async-start(), calls=%async_computation.6 | async-start | bytes 1638400 | tf_op jit(solution)/shard_map/reduce_scatter | solution.py:375
  263.6 2.9 collective-permute-start.33
  266.5 2.9 collective-permute-start.34
  266.6 25.8 %collective-permute-start.35 = (bf16[4096,128]{1,0:T(8,128)(2,1)}, bf16[4096,128]{1,0:T(8,128)(2,1)}, u32[]{:S(2)}, u32[]{:S(2)}) collective-permute-start(bf16[4096,128]{1,0:T(8,128)(2,1)} %get-tuple-element.125), channel_id=1, source_target_pairs={{0,8},{4,12},{8,0},{12,4},{1,9},{5,13},{9,1},{13,5},{2,10},{6,14},... | collective-permute-start | bytes 3145736 | tf_op jit(solution)/shard_map/ppermute | solution.py:72
  267.7 25.5 %collective-permute-start.36 = (bf16[4096,128]{1,0:T(8,128)(2,1)}, bf16[4096,128]{1,0:T(8,128)(2,1)}, u32[]{:S(2)}, u32[]{:S(2)}) collective-permute-start(bf16[4096,128]{1,0:T(8,128)(2,1)} %collective-permute-done.29.refs_0_), channel_id=1, source_target_pairs={{0,16},{16,0},{1,17},{17,1},{2,18},{18,2},{3,19},{19,3},{4,20},{20... | collective-permute-start | bytes 3145736 | tf_op jit(solution)/shard_map/ppermute | solution.py:87
  282.7 133.7 %reduce-scatter.10.cloned.1.call-start = ((), (), s32[]{:S(2)}) async-start(), calls=%async_computation.7 | async-start | bytes 3276800 | tf_op jit(solution)/shard_map/reduce_scatter | solution.py:375
  293.2 3.0 collective-permute-start.38
  293.2 30.6 %collective-permute-start.37 = (bf16[4096,128]{1,0:T(8,128)(2,1)}, bf16[4096,128]{1,0:T(8,128)(2,1)}, u32[]{:S(2)}, u32[]{:S(2)}) collective-permute-start(bf16[4096,128]{1,0:T(8,128)(2,1)} %collective-permute-done.35.refs_4_), channel_id=1, source_target_pairs={{0,16},{16,0},{1,17},{17,1},{2,18},{18,2},{3,19},{19,3},{4,20},{20... | collective-permute-start | bytes 3145736 | tf_op jit(solution)/shard_map/ppermute | solution.py:87
  296.2 27.6 %collective-permute-start.39 = (bf16[4096,128]{1,0:T(8,128)(2,1)}, bf16[4096,128]{1,0:T(8,128)(2,1)}, u32[]{:S(2)}, u32[]{:S(2)}) collective-permute-start(bf16[4096,128]{1,0:T(8,128)(2,1)} %collective-permute-done.29.refs_0_), channel_id=1, source_target_pairs={{0,4},{4,0},{8,12},{12,8},{1,5},{5,1},{9,13},{13,9},{2,6},{6,2},{1... | collective-permute-start | bytes 3145736 | tf_op jit(solution)/shard_map/ppermute | solution.py:76
  329.7 2.9 collective-permute-start.40
  332.6 2.9 collective-permute-start.41
  354.8 115.6 %reduce-scatter.12.cloned.1.call-start = ((), (), s32[]{:S(2)}) async-start(), calls=%async_computation.8 | async-start | bytes 3276800 | tf_op jit(solution)/shard_map/reduce_scatter | solution.py:375
  416.4 107.9 %reduce-scatter.14.cloned.1.call-start = ((), (), s32[]{:S(2)}) async-start(), calls=%async_computation.9 | async-start | bytes 3276800 | tf_op jit(solution)/shard_map/reduce_scatter | solution.py:375
  434.8 89.5 %copy-start.12 = (bf16[640,512]{1,0:T(8,128)(2,1)S(1)}, bf16[640,512]{1,0:T(8,128)(2,1)}, u32[]{:S(2)}) copy-start(bf16[640,512]{1,0:T(8,128)(2,1)} %reduce-scatter.10.cloned.1.call-done) | copy-start | bytes 1966084
  (17 other events, 250.3 us)
Sparse Core Ops, SparseCore 0:
  240.3 45.1 reduce-scatter.5
  287.8 41.8 reduce-scatter.7
  354.9 61.4 reduce-scatter.9
  418.6 51.7 reduce-scatter.11
  472.5 51.7 reduce-scatter.13

commit v3 on v2

--- a/solution.py
+++ b/solution.py
@@ -278,8 +278,8 @@
     )(place, gain, *toks, *ws, *([tail] if has_tail else []), conv_kernel)
 
 
-def second_kernel(quarters, place_ref, act_l, act_r, own, sib, *refs):
-    pieces, refs = refs[: 4 * len(quarters)], refs[4 * len(quarters) :]
+def second_kernel(quarters, parts, place_ref, act_l, act_r, own, sib, *refs):
+    pieces, refs = refs[: sum(parts)], refs[sum(parts) :]
     out_ref, wbuf, buf_l, buf_r, wsem, asem = refs
     scen, row = place_ref[0], place_ref[1]
     n, count = pl.program_id(0), pl.num_programs(0)
@@ -307,14 +307,17 @@
                         wsem.at[slot],
                     ).start()
 
+            part = pieces[sum(parts[:i]) : sum(parts[: i + 1])]
             for j in (2, 3):
+                share = part[len(part) // 2 * (j - 2) : len(part) // 2 * (j - 1)]
+                spots = ((own_at, half), (other_at, half)) if len(share) == 2 else ((0, width),)
 
                 @pl.when(mine & (source == j))
                 def _():
-                    for k, off in ((0, own_at), (1, other_at)):
+                    for ref, (off, wide) in zip(share, spots):
                         pltpu.make_async_copy(
-                            pieces[4 * i + 2 * (j - 2) + k],
-                            wbuf.at[slot, :, pl.ds(pl.multiple_of(at + off, half), half)],
+                            ref,
+                            wbuf.at[slot, :, pl.ds(pl.multiple_of(at + off, wide), wide)],
                             wsem.at[slot],
                         ).start()
 
@@ -351,7 +354,7 @@
     any_spec = pl.BlockSpec(memory_space=pl.ANY)
     used = [p for quarter in quarters for p in pieces[quarter]]
     return pl.pallas_call(
-        functools.partial(second_kernel, quarters),
+        functools.partial(second_kernel, quarters, tuple(len(pieces[quarter]) for quarter in quarters)),
         grid=(count // 2,),
         in_specs=[pl.BlockSpec(memory_space=pltpu.SMEM)] + [any_spec] * (4 + len(used)),
         out_specs=pl.BlockSpec((rows, 2 * width), lambda n: (0, n)),
@@ -380,14 +383,15 @@
     scen, row, col = (lax.axis_index(a) for a in ("scen", "row", "col"))
     place = jnp.stack([scen, row, col]).astype(jnp.int32)
     lons = rows // LAT
-    la = lons // 2
+    la = lons * 9 // 32 * 2
     cut = (la + 2) * LAT
 
     h = (d * 13 // 64) // 16 * 16
     xs_in = [lax.dynamic_slice(w_in, (scen * 2 * h + i * h, 0), (h, w_in.shape[1])) for i in range(2)]
     xs_in.append(w_in[4 * h :])
     q = d // 4
-    os_in = [lax.dynamic_slice(w_out, (0, i * q + scen * (q // 2)), (w_out.shape[0], q // 2)) for i in range(4)]
+    os_in = [lax.dynamic_slice(w_out, (0, i * q + scen * (q // 2)), (w_out.shape[0], q // 2)) for i in range(3)]
+    os_in.append(w_out[:, 3 * q :])
     gain = norm_gain.reshape(4, d)
     wide = extended(tokens, (("row", 0),), LAT)
     na, nb = wide[:cut], wide[cut:]
@@ -403,7 +407,7 @@
     xd, y1 = swap_x(x2i), swap_scen(x1)
     d3, u3 = down(d2, 3), up(u2, 3)
     cy0, cx1 = cores(y0, x1)
-    (xd, y1, cy0, cx1, d3, u3), (o0i, nb) = gate((xd, y1, cy0, cx1, d3, u3), (os_in[0], nb))
+    (xd, y1, cy0, cx1, d3, u3, *os_in), (o0i, nb) = gate((xd, y1, cy0, cx1, d3, u3, *os_in), (os_in[0], nb))
     ox0 = swap_x(o0i)
     e1, f1 = down(nb, 1), up(nb, 1)
     cxd, cy1 = cores(xd, y1)
@@ -429,27 +433,23 @@
     pieces[1] = (ox1, oy1, cox1, coy1)
     p1 = second(place, (act_a0, act_a1), shards, pieces, (1,))
     r1 = scatter(p1)
-    (p1, ox3, oy2, r0), (ox2, nb) = gate((p1, ox3, oy2, r0), (ox2, nb))
-    oy3 = swap_scen(ox3)
-    coy2, cox2 = cores(oy2, ox2)
+    (p1,), (ox2, nb) = gate((p1,), (ox2, nb))
+    cox2 = swap_core(ox2)
     toks_b = [nb, e1, e2, e3, f1, f2, f3]
     act_b0, norm_b = first(place, gain, toks_b, ws, conv_kernel, tail0, 0, lons - la)
-    (norm_b, oy3, coy2, cox2, act_a1, r1), (ox3,) = gate((norm_b, oy3, coy2, cox2, act_a1, r1), (ox3,))
-    coy3, cox3 = cores(oy3, ox3)
-    (norm_b, coy3, cox3, act_a1), _ = gate((norm_b, coy3, cox3, act_a1), ())
+    (norm_b, ox3, oy2, cox2, r0), (act_a1,) = gate((norm_b, ox3, oy2, cox2, r0), (act_a1,))
+    coy2, cox3 = cores(oy2, ox3)
     pieces[2] = (ox2, oy2, cox2, coy2)
-    pieces[3] = (ox3, oy3, cox3, coy3)
-    p2 = second(place, (act_a0, act_a1), shards, pieces, (2, 3))
+    p2 = second(place, (act_a0, act_a1), shards, pieces, (2,))
     r2 = scatter(p2)
-    (p2, norm_b), _ = gate((p2, norm_b), ())
+    (p2, cox3, r1), (act_a1,) = gate((p2, cox3, r1), (act_a1,))
+    pieces[3] = (ox3, cox3)
+    p3 = second(place, (act_a0, act_a1), shards, pieces, (3,))
+    r3 = scatter(p3)
+    (p3, norm_b), _ = gate((p3, norm_b), ())
     (act_b1,) = first(place, gain, [norm_b], ws, conv_kernel, tail1, 1, lons - la)
-    s0 = second(place, (act_b0, act_b1), shards, pieces, (0, 1))
-    (s0, act_b1, r2), _ = gate((s0, act_b1, r2), ())
-    s1 = second(place, (act_b0, act_b1), shards, pieces, (2, 3))
-    s0, s1 = scatter(s0), scatter(s1)
-    mixed = jnp.concatenate(
-        [jnp.concatenate([r0, r1, r2], axis=1), jnp.concatenate([s0, s1], axis=1)], axis=0
-    )
+    s = scatter(second(place, (act_b0, act_b1), shards, pieces, (0, 1, 2, 3)))
+    mixed = jnp.concatenate([jnp.concatenate([r0, r1, r2, r3], axis=1), s], axis=0)
     return (tokens.astype(jnp.float32) + mixed.astype(jnp.float32)).astype(jnp.bfloat16)
 
 

time: 546 us -> 517 us (0.947)
  waiting for transfers between devices: 268 us -> 235 us
    reduce_scatter x5, waiting for transfers between devices: 115 us -> 84 us  [scatter(): return lax.psum_scatter(v, 'col', scatter_dimension=1, tiled=True)]
    ppermute x6, waiting for transfers between devices: 78.5 us -> 50.1 us  [down(): return lax.ppermute(v, 'col', [(i, i - 1) for i in range(1, 5 - hop)])]
    ppermute x7, waiting for transfers between devices: 21.9 us -> 41.6 us  [swap_x(): return lax.ppermute(v, 'row', [(i, i ^ 2) for i in range(4)])]
    ppermute x15 -> x14, waiting for transfers between devices: 14.4 us -> 17 us  [swap_core(): return lax.ppermute(v, 'row', [(i, i ^ 1) for i in range(4)])]
  transfers between devices with their start and end apart: 47 -> 45, of which waited for: 23 -> 18; matrix products, arithmetic and copies ran while one was open for 2% -> 3% of each run, Pallas kernels for 31% -> 37%
where the time goes in v3:
time: 517 us; the launch traced here: 509 us
  waiting for transfers between devices  235 us (45%)
  Pallas kernels  187 us (36%)
  starting transfers between devices  44.6 us (9%)
  local copies, waits for them, and re-layouts  20.4 us (4%)
  between operations  14 us (3%)
  other arithmetic  7.94 us (2%)
    pallas_call x4, Pallas kernels, first(): pl.pallas_call(functools.partial(first_kernel, has_tail, len(toks), len(w...  107 us
    reduce_scatter x5, waiting for transfers between devices, scatter(): return lax.psum_scatter(v, 'col', scatter_dimension=1, tiled=True)  84 us
    pallas_call x5, Pallas kernels, second(): pl.pallas_call(functools.partial(second_kernel, quarters, tuple((len(piec...  80.6 us
    ppermute x6, waiting for transfers between devices, down(): return lax.ppermute(v, 'col', [(i, i - 1) for i in range(1, 5 - hop)])  50.1 us
    ppermute x7, waiting for transfers between devices, swap_x(): return lax.ppermute(v, 'row', [(i, i ^ 2) for i in range(4)])  41.6 us
    ppermute x6, waiting for transfers between devices, up(): return lax.ppermute(v, 'col', [(i, i + 1) for i in range(hop - 1, 3)])  33.7 us
    ppermute x14, waiting for transfers between devices, swap_core(): return lax.ppermute(v, 'row', [(i, i ^ 1) for i in range(4)])  17 us
    ppermute x6, starting transfers between devices, up(): return lax.ppermute(v, 'col', [(i, i + 1) for i in range(hop - 1, 3)])  16.3 us
  transfers between devices with their start and end apart: 45, of which 18 were waited for; matrix products, arithmetic and copies ran while one was open for 3% of the time, Pallas kernels for 37%

profile of v3, /device:TPU:0, one launch (start us, length us, event | category | flops | bytes accessed | tf_op | source)
XLA Modules:
  0.0 508.6 jit_solution(5544235223485314354)
XLA Ops:
  8.0 2.6 collective-permute-start.1
  10.6 2.3 constant_dynamic-slice_fusion.3
  12.9 7.0 %collective-permute-done.1 = bf16[40,1024]{1,0:T(8,128)(2,1)S(1)} collective-permute-done((bf16[40,1024]{1,0:T(8,128)(2,1)S(1)}, bf16[40,1024]{1,0:T(8,128)(2,1)S(1)}, u32[]{:S(2)}, u32[]{:S(2)}) %collective-permute-start.1) | collective-permute-done | bytes 81952 | tf_op jit(solution)/shard_map/ppermute | solution.py:28
  21.2 3.0 collective-permute-start.2
  24.2 3.6 collective-permute-start.5
  27.8 1.3 collective-permute-start.4
  29.1 33.7 %collective-permute-done.5.refs_4_ = bf16[800,1024]{1,0:T(8,128)(2,1)S(1)} collective-permute-done((bf16[800,1024]{1,0:T(8,128)(2,1)S(1)}, bf16[800,1024]{1,0:T(8,128)(2,1)S(1)}, u32[]{:S(2)}, u32[]{:S(2)}) %collective-permute-start.5) | collective-permute-done | bytes 1638432 | tf_op jit(solution)/shard_map/ppermute | solution.py:95
  62.7 4.2 collective-permute-done.4.refs_1_
  68.2 1.5 collective-permute-start.7
  71.0 1.8 collective-permute-start.11
  72.8 2.7 slice.24
  75.6 33.2 %collective-permute-done.10.refs_2_ = bf16[800,1024]{1,0:T(8,128)(2,1)} collective-permute-done((bf16[800,1024]{1,0:T(8,128)(2,1)S(1)}, bf16[800,1024]{1,0:T(8,128)(2,1)}, u32[]{:S(2)}, u32[]{:S(2)}) %collective-permute-start.10) | collective-permute-done | bytes 1638432 | tf_op jit(solution)/shard_map/ppermute | solution.py:91
  111.7 1.9 collective-permute-done.14.refs_15_.refs_9_
  115.0 1.3 collective-permute-start.16
  116.3 1.9 collective-permute-start.17
  118.2 1.5 collective-permute-start.12
  119.7 3.0 slice.25
  122.7 3.6 constant_dynamic-slice_fusion
  126.4 28.8 %collective-permute-done.12.refs_13_.refs_7_ = bf16[192,4096]{1,0:T(8,128)(2,1)} collective-permute-done((bf16[192,4096]{1,0:T(8,128)(2,1)}, bf16[192,4096]{1,0:T(8,128)(2,1)}, u32[]{:S(2)}, u32[]{:S(2)}) %collective-permute-start.12) | collective-permute-done | bytes 1572896 | tf_op jit(solution)/shard_map/ppermute | solution.py:72
  155.2 1.4 collective-permute-done.16.refs_3_
  156.7 3.7 collective-permute-done.18.refs_18_.refs_12_
  161.9 5.4 %collective-permute-start.22 = (bf16[560,1024]{1,0:T(8,128)(2,1)}, bf16[560,1024]{1,0:T(8,128)(2,1)S(1)}, u32[]{:S(2)}, u32[]{:S(2)}) collective-permute-start(bf16[560,1024]{1,0:T(8,128)(2,1)} %pad_maximum_fusion.1.refs_0_), channel_id=1, source_target_pairs={{0,1},{1,2},{2,3},{4,5},{5,6},{6,7},{8,9},{9,10},{10,11},{12,13},{... | collective-permute-start | bytes 3440648 | tf_op jit(solution)/shard_map/ppermute | solution.py:95
  167.3 1.3 collective-permute-start.21
  168.6 1.6 collective-permute-start.20
  170.1 32.2 %first.4 = (bf16[720,2048]{1,0:T(8,128)(2,1)}, bf16[80,2048]{1,0:T(8,128)(2,1)}, bf16[800,4096]{1,0:T(8,128)(2,1)}) custom-call(s32[3]{0:T(128)} %pad_add_fusion.place_ref, f32[4,1024]{1,0:T(4,128)} %reshape.3.gain_ref, bf16[800,1024]{1,0:T(8,128)(2,1)} %copy-done.5, bf16[800,1024]{1,0:T(8,128)(2,1)} %copy-done.17, ...), custom_call_target="tpu_custom_call" | custom-call | flops 13421772800 | bytes 16777216 | tf_op jit(solution)/shard_map/first/pallas_call | solution.py:255
  204.8 1.8 collective-permute-start.27
  206.7 27.6 %first.5 = (bf16[720,2048]{1,0:T(8,128)(2,1)}, bf16[80,2048]{1,0:T(8,128)(2,1)}) custom-call(s32[3]{0:T(128)} %pad_add_fusion.place_ref, f32[4,1024]{1,0:T(4,128)} %reshape.3.gain_ref, bf16[800,4096]{1,0:T(8,128)(2,1)} %get-tuple-element.102.refs_0_, bf16[1024,4096]{1,0:T(8,128)(2,1)} %refs_1_.3, bf16[1024,4096]{1,0:T(8,128)(2,1)} %collective-permute-done.3.refs_8_.refs_2_, ...), custom_call_target="tpu_custom_call" | custom-call | flops 13421772800 | bytes 16777216 | tf_op jit(solution)/shard_map/first/pallas_call | solution.py:255
  234.5 1.3 collective-permute-start.31
  235.8 1.7 collective-permute-start.32
  237.5 1.5 collective-permute-start.29
  239.0 1.5 collective-permute-start.30
  241.5 13.3 %second.5 = bf16[720,1024]{1,0:T(8,128)(2,1)} custom-call(s32[3]{0:T(128)} %pad_add_fusion.place_ref, bf16[720,2048]{1,0:T(8,128)(2,1)} %get-tuple-element.97.act_l, bf16[720,2048]{1,0:T(8,128)(2,1)} %get-tuple-element.137.act_r, bf16[4096,1024]{1,0:T(8,128)(2,1)} %own.9, bf16[4096,1024]{1,0:T(8,128)(2,1)} %collective-permute-done.8.sib, ...), custom_call_target="tpu_custom_call" | custom-call | flops 6039797760 | bytes 8388608 | tf_op jit(solution)/shard_map/second/pallas_call | solution.py:356
  254.9 8.5 %collective-permute-done.29.refs_0_.refs_8_ = bf16[4096,128]{1,0:T(8,128)(2,1)} collective-permute-done((bf16[4096,128]{1,0:T(8,128)(2,1)}, bf16[4096,128]{1,0:T(8,128)(2,1)}, u32[]{:S(2)}, u32[]{:S(2)}) %collective-permute-start.29) | collective-permute-done | bytes 1048608 | tf_op jit(solution)/shard_map/ppermute | solution.py:72
  264.6 11.1 %collective-permute-done.31.refs_3_ = bf16[560,1024]{1,0:T(8,128)(2,1)} collective-permute-done((bf16[560,1024]{1,0:T(8,128)(2,1)}, bf16[560,1024]{1,0:T(8,128)(2,1)}, u32[]{:S(2)}, u32[]{:S(2)}) %collective-permute-start.31) | collective-permute-done | bytes 1146912 | tf_op jit(solution)/shard_map/ppermute | solution.py:91
  275.7 2.9 collective-permute-done.33.refs_3_.refs_7_
  278.8 1.5 collective-permute-start.35
  282.5 13.4 %second.6 = bf16[720,1024]{1,0:T(8,128)(2,1)} custom-call(s32[3]{0:T(128)} %pad_add_fusion.place_ref, bf16[720,2048]{1,0:T(8,128)(2,1)} %get-tuple-element.97.act_l, bf16[720,2048]{1,0:T(8,128)(2,1)} %get-tuple-element.137.act_r, bf16[4096,1024]{1,0:T(8,128)(2,1)} %own.9, bf16[4096,1024]{1,0:T(8,128)(2,1)} %collective-permute-done.8.sib, ...), custom_call_target="tpu_custom_call" | custom-call | flops 6039797760 | bytes 8388608 | tf_op jit(solution)/shard_map/second/pallas_call | solution.py:356
  296.1 1.6 collective-permute-start.36
  297.8 25.0 %first.6 = (bf16[560,2048]{1,0:T(8,128)(2,1)}, bf16[560,4096]{1,0:T(8,128)(2,1)}) custom-call(s32[3]{0:T(128)} %pad_add_fusion.place_ref, f32[4,1024]{1,0:T(4,128)} %reshape.3.gain_ref, bf16[560,1024]{1,0:T(8,128)(2,1)} %pad_maximum_fusion.1.refs_0_, bf16[560,1024]{1,0:T(8,128)(2,1)} %copy-done.7, bf16[560,1024]{1,0:T(8,128)(2,1)} %collective-permute-done.26.refs_2_, ...), custom_call_target="tpu_custom_call" | custom-call | flops 9395240960 | bytes 16777216 | tf_op jit(solution)/shard_map/first/pallas_call | solution.py:255
  322.8 4.2 collective-permute-done.35.refs_0_.refs_12_
  327.0 2.9 collective-permute-done.38.refs_3_.refs_11_
  330.9 13.3 %second.7 = bf16[720,1024]{1,0:T(8,128)(2,1)} custom-call(s32[3]{0:T(128)} %pad_add_fusion.place_ref, bf16[720,2048]{1,0:T(8,128)(2,1)} %get-tuple-element.97.act_l, bf16[720,2048]{1,0:T(8,128)(2,1)} %get-tuple-element.137.act_r, bf16[4096,1024]{1,0:T(8,128)(2,1)} %own.9, bf16[4096,1024]{1,0:T(8,128)(2,1)} %collective-permute-done.8.sib, ...), custom_call_target="tpu_custom_call" | custom-call | flops 6039797760 | bytes 8388608 | tf_op jit(solution)/shard_map/second/pallas_call | solution.py:356
  344.4 4.4 collective-permute-done.39.refs_1_.refs_13_
  348.8 13.3 %second.8 = bf16[720,1024]{1,0:T(8,128)(2,1)} custom-call(s32[3]{0:T(128)} %pad_add_fusion.place_ref, bf16[720,2048]{1,0:T(8,128)(2,1)} %get-tuple-element.97.act_l, bf16[720,2048]{1,0:T(8,128)(2,1)} %get-tuple-element.137.act_r, bf16[4096,1024]{1,0:T(8,128)(2,1)} %own.9, bf16[4096,1024]{1,0:T(8,128)(2,1)} %collective-permute-done.8.sib, ...), custom_call_target="tpu_custom_call" | custom-call | flops 6039797760 | bytes 8388608 | tf_op jit(solution)/shard_map/second/pallas_call | solution.py:356
  362.4 21.8 %first.7.act_r = bf16[560,2048]{1,0:T(8,128)(2,1)} custom-call(s32[3]{0:T(128)} %pad_add_fusion.place_ref, f32[4,1024]{1,0:T(4,128)} %reshape.3.gain_ref, bf16[560,4096]{1,0:T(8,128)(2,1)} %get-tuple-element.141.refs_0_, bf16[1024,4096]{1,0:T(8,128)(2,1)} %refs_1_.3, bf16[1024,4096]{1,0:T(8,128)(2,1)} %collective-permute-done.3.refs_8_.refs_2_, ...), custom_call_target="tpu_custom_call" | custom-call | flops 9395240960 | bytes 16777216 | tf_op jit(solution)/shard_map/first/pallas_call | solution.py:255
  384.2 27.4 %second.9 = bf16[560,4096]{1,0:T(8,128)(2,1)} custom-call(s32[3]{0:T(128)} %pad_add_fusion.place_ref, bf16[560,2048]{1,0:T(8,128)(2,1)} %get-tuple-element.139.act_l, bf16[560,2048]{1,0:T(8,128)(2,1)} %first.7.act_r, bf16[4096,1024]{1,0:T(8,128)(2,1)} %own.9, bf16[4096,1024]{1,0:T(8,128)(2,1)} %collective-permute-done.8.sib, bf16[4096,128]{1,0:T(8,128)(2,1)} %copy-done.8, ...), custom_call_target="tpu_custom_call" | custom-call | flops 18790481920 | bytes 33554432 | tf_op jit(solution)/shard_map/second/pallas_call | solution.py:356
  411.6 83.9 %reduce-scatter.14.cloned.1.call-done = bf16[560,1024]{1,0:T(8,128)(2,1)} async-done(((bf16[560,4096]{1,0:T(8,128)(2,1)}), bf16[560,1024]{1,0:T(8,128)(2,1)}) %reduce-scatter.14.cloned.1.call-update) | async-done | bytes 1146896 | tf_op jit(solution)/shard_map/reduce_scatter | solution.py:378
  495.6 6.0 %add_convert_fusion = bf16[1280,1024]{1,0:T(8,128)(2,1)} fusion(bf16[1280,1024]{1,0:T(8,128)(2,1)S(1)} %copy-done, bf16[560,1024]{1,0:T(8,128)(2,1)} %reduce-scatter.14.cloned.1.call-done, bf16[720,256]{1,0:T(8,128)(2,1)} %reduce-scatter.12.cloned.1.call-done, bf16[720,256]{1,0:T(8,128)(2,1)} %reduce-scatter.10.cloned.1.call-done, ...), kind=kLoop, calls=%fused_computation | loop fusion | flops 17039360 | bytes 7864320 | tf_op jit(solution)/shard_map/convert_element_type | solution.py:453
  (102 shorter events, 20.0 us)
Async XLA Ops:
  6.5 320.4 %reduce-scatter.6.cloned.1.call-start = ((), (), s32[]{:S(2)}) async-start(), calls=%async_computation.5 | async-start | bytes 1843200 | tf_op jit(solution)/shard_map/reduce_scatter | solution.py:378
  6.5 60.4 %collective-permute-start.3 = (bf16[1024,4096]{1,0:T(8,128)(2,1)}, bf16[1024,4096]{1,0:T(8,128)(2,1)}, u32[]{:S(2)}, u32[]{:S(2)}) collective-permute-start(bf16[1024,4096]{1,0:T(8,128)(2,1)} %refs_1_.3), channel_id=1, source_target_pairs={{0,4},{4,0},{8,12},{12,8},{1,5},{5,1},{9,13},{13,9},{2,6},{6,2},{1... | collective-permute-start | bytes 25165832 | tf_op jit(solution)/shard_map/ppermute | solution.py:76
  7.0 60.0 %collective-permute-start.8 = (bf16[4096,1024]{1,0:T(8,128)(2,1)}, bf16[4096,1024]{1,0:T(8,128)(2,1)}, u32[]{:S(2)}, u32[]{:S(2)}) collective-permute-start(bf16[4096,1024]{1,0:T(8,128)(2,1)} %own.9), channel_id=1, source_target_pairs={{0,4},{4,0},{8,12},{12,8},{1,5},{5,1},{9,13},{13,9},{2,6},{6,2},{1... | collective-permute-start | bytes 25165832 | tf_op jit(solution)/shard_map/ppermute | solution.py:76
  8.0 11.9 %collective-permute-start.1 = (bf16[40,1024]{1,0:T(8,128)(2,1)S(1)}, bf16[40,1024]{1,0:T(8,128)(2,1)S(1)}, u32[]{:S(2)}, u32[]{:S(2)}) collective-permute-start(bf16[40,1024]{1,0:T(8,128)(2,1)S(1)} %get-tuple-element.148), channel_id=1, source_target_pairs={{4,0},{8,4},{12,8},{0,12},{5,1},{9,5},{13,9},{1,13},{6,2},{10,6},{... | collective-permute-start | bytes 245768 | tf_op jit(solution)/shard_map/ppermute | solution.py:28
  10.6 10.5 %collective-permute-start = (bf16[40,1024]{1,0:T(8,128)(2,1)S(1)}, bf16[40,1024]{1,0:T(8,128)(2,1)S(1)}, u32[]{:S(2)}, u32[]{:S(2)}) collective-permute-start(bf16[40,1024]{1,0:T(8,128)(2,1)S(1)} %get-tuple-element.149), channel_id=1, source_target_pairs={{0,4},{4,8},{8,12},{12,0},{1,5},{5,9},{9,13},{13,1},{2,6},{6,10},{... | collective-permute-start | bytes 245768 | tf_op jit(solution)/shard_map/ppermute | solution.py:26
  21.2 45.8 %collective-permute-start.2 = (bf16[208,4096]{1,0:T(8,128)(2,1)S(1)}, bf16[208,4096]{1,0:T(8,128)(2,1)S(1)}, u32[]{:S(2)}, u32[]{:S(2)}) collective-permute-start(bf16[208,4096]{1,0:T(8,128)(2,1)S(1)} %get-tuple-element.75), channel_id=1, source_target_pairs={{0,8},{4,12},{8,0},{12,4},{1,9},{5,13},{9,1},{13,5},{2,10},{6,14},... | collective-permute-start | bytes 5111816 | tf_op jit(solution)/shard_map/ppermute | solution.py:72
  24.2 38.5 %collective-permute-start.5 = (bf16[800,1024]{1,0:T(8,128)(2,1)S(1)}, bf16[800,1024]{1,0:T(8,128)(2,1)S(1)}, u32[]{:S(2)}, u32[]{:S(2)}) collective-permute-start(bf16[800,1024]{1,0:T(8,128)(2,1)S(1)} %pad_maximum_fusion.refs_0_), channel_id=1, source_target_pairs={{0,1},{1,2},{2,3},{4,5},{5,6},{6,7},{8,9},{9,10},{10,11},{12,13},{... | collective-permute-start | bytes 4915208 | tf_op jit(solution)/shard_map/ppermute | solution.py:95
  27.8 39.2 %collective-permute-start.4 = (bf16[800,1024]{1,0:T(8,128)(2,1)S(1)}, bf16[800,1024]{1,0:T(8,128)(2,1)S(1)}, u32[]{:S(2)}, u32[]{:S(2)}) collective-permute-start(bf16[800,1024]{1,0:T(8,128)(2,1)S(1)} %pad_maximum_fusion.refs_0_), channel_id=1, source_target_pairs={{1,0},{2,1},{3,2},{5,4},{6,5},{7,6},{9,8},{10,9},{11,10},{13,12},{... | collective-permute-start | bytes 4915208 | tf_op jit(solution)/shard_map/ppermute | solution.py:91
  62.7 52.3 %copy-start.16 = (bf16[800,1024]{1,0:T(8,128)(2,1)}, bf16[800,1024]{1,0:T(8,128)(2,1)S(1)}, u32[]{:S(2)}) copy-start(bf16[800,1024]{1,0:T(8,128)(2,1)S(1)} %collective-permute-done.5.refs_4_) | copy-start | bytes 4915204
  67.0 41.8 %collective-permute-start.9 = (bf16[208,4096]{1,0:T(8,128)(2,1)S(1)}, bf16[208,4096]{1,0:T(8,128)(2,1)S(1)}, u32[]{:S(2)}, u32[]{:S(2)}) collective-permute-start(bf16[208,4096]{1,0:T(8,128)(2,1)S(1)} %collective-permute-done.2.refs_9_.refs_3_), channel_id=1, source_target_pairs={{0,4},{4,0},{8,12},{12,8},{1,5},{5,1},{9,13},{13,9},{2,6},{6,2},{1... | collective-permute-start | bytes 5111816 | tf_op jit(solution)/shard_map/ppermute | solution.py:76
  67.1 41.7 %collective-permute-start.6 = (bf16[208,4096]{1,0:T(8,128)(2,1)S(1)}, bf16[208,4096]{1,0:T(8,128)(2,1)}, u32[]{:S(2)}, u32[]{:S(2)}) collective-permute-start(bf16[208,4096]{1,0:T(8,128)(2,1)S(1)} %get-tuple-element.77), channel_id=1, source_target_pairs={{0,8},{4,12},{8,0},{12,4},{1,9},{5,13},{9,1},{13,5},{2,10},{6,14},... | collective-permute-start | bytes 5111816 | tf_op jit(solution)/shard_map/ppermute | solution.py:72
  68.2 40.6 %collective-permute-start.7 = (bf16[208,4096]{1,0:T(8,128)(2,1)S(1)}, bf16[208,4096]{1,0:T(8,128)(2,1)S(1)}, u32[]{:S(2)}, u32[]{:S(2)}) collective-permute-start(bf16[208,4096]{1,0:T(8,128)(2,1)S(1)} %collective-permute-done.2.refs_9_.refs_3_), channel_id=1, source_target_pairs={{0,16},{16,0},{1,17},{17,1},{2,18},{18,2},{3,19},{19,3},{4,20},{20... | collective-permute-start | bytes 5111816 | tf_op jit(solution)/shard_map/ppermute | solution.py:87
  69.7 39.1 %collective-permute-start.10 = (bf16[800,1024]{1,0:T(8,128)(2,1)S(1)}, bf16[800,1024]{1,0:T(8,128)(2,1)}, u32[]{:S(2)}, u32[]{:S(2)}) collective-permute-start(bf16[800,1024]{1,0:T(8,128)(2,1)S(1)} %collective-permute-done.4.refs_1_), channel_id=1, source_target_pairs={{1,0},{2,1},{5,4},{6,5},{9,8},{10,9},{13,12},{14,13},{17,16},{18,1... | collective-permute-start | bytes 4915208 | tf_op jit(solution)/shard_map/ppermute | solution.py:91
  71.0 37.8 %collective-permute-start.11 = (bf16[800,1024]{1,0:T(8,128)(2,1)S(1)}, bf16[800,1024]{1,0:T(8,128)(2,1)}, u32[]{:S(2)}, u32[]{:S(2)}) collective-permute-start(bf16[800,1024]{1,0:T(8,128)(2,1)S(1)} %collective-permute-done.5.refs_4_), channel_id=1, source_target_pairs={{1,2},{2,3},{5,6},{6,7},{9,10},{10,11},{13,14},{14,15},{17,18},{18... | collective-permute-start | bytes 4915208 | tf_op jit(solution)/shard_map/ppermute | solution.py:95
  110.0 3.6 collective-permute-start.14
  111.2 45.4 %collective-permute-start.13 = (bf16[208,4096]{1,0:T(8,128)(2,1)}, bf16[208,4096]{1,0:T(8,128)(2,1)}, u32[]{:S(2)}, u32[]{:S(2)}) collective-permute-start(bf16[208,4096]{1,0:T(8,128)(2,1)} %collective-permute-done.6.refs_11_.refs_5_), channel_id=1, source_target_pairs={{0,16},{16,0},{1,17},{17,1},{2,18},{18,2},{3,19},{19,3},{4,20},{20... | collective-permute-start | bytes 5111816 | tf_op jit(solution)/shard_map/ppermute | solution.py:87
  114.9 41.8 %collective-permute-start.15 = (bf16[208,4096]{1,0:T(8,128)(2,1)}, bf16[208,4096]{1,0:T(8,128)(2,1)}, u32[]{:S(2)}, u32[]{:S(2)}) collective-permute-start(bf16[208,4096]{1,0:T(8,128)(2,1)} %collective-permute-done.6.refs_11_.refs_5_), channel_id=1, source_target_pairs={{0,4},{4,0},{8,12},{12,8},{1,5},{5,1},{9,13},{13,9},{2,6},{6,2},{1... | collective-permute-start | bytes 5111816 | tf_op jit(solution)/shard_map/ppermute | solution.py:76
  115.0 41.6 %collective-permute-start.16 = (bf16[800,1024]{1,0:T(8,128)(2,1)}, bf16[800,1024]{1,0:T(8,128)(2,1)}, u32[]{:S(2)}, u32[]{:S(2)}) collective-permute-start(bf16[800,1024]{1,0:T(8,128)(2,1)} %collective-permute-done.10.refs_2_), channel_id=1, source_target_pairs={{1,0},{5,4},{9,8},{13,12},{17,16},{21,20},{25,24},{29,28}} | collective-permute-start | bytes 4915208 | tf_op jit(solution)/shard_map/ppermute | solution.py:91
  116.3 40.3 %collective-permute-start.17 = (bf16[800,1024]{1,0:T(8,128)(2,1)}, bf16[800,1024]{1,0:T(8,128)(2,1)}, u32[]{:S(2)}, u32[]{:S(2)}) collective-permute-start(bf16[800,1024]{1,0:T(8,128)(2,1)} %collective-permute-done.11.refs_5_), channel_id=1, source_target_pairs={{2,3},{6,7},{10,11},{14,15},{18,19},{22,23},{26,27},{30,31}} | collective-permute-start | bytes 4915208 | tf_op jit(solution)/shard_map/ppermute | solution.py:95
  118.2 37.0 %collective-permute-start.12 = (bf16[192,4096]{1,0:T(8,128)(2,1)}, bf16[192,4096]{1,0:T(8,128)(2,1)}, u32[]{:S(2)}, u32[]{:S(2)}) collective-permute-start(bf16[192,4096]{1,0:T(8,128)(2,1)} %slice.24), channel_id=1, source_target_pairs={{0,8},{4,12},{8,0},{12,4},{1,9},{5,13},{9,1},{13,5},{2,10},{6,14},... | collective-permute-start | bytes 4718600 | tf_op jit(solution)/shard_map/ppermute | solution.py:72
  156.6 3.8 collective-permute-start.18
  160.5 9.7 %collective-permute-start.19 = (bf16[208,4096]{1,0:T(8,128)(2,1)}, bf16[208,4096]{1,0:T(8,128)(2,1)}, u32[]{:S(2)}, u32[]{:S(2)}) collective-permute-start(bf16[208,4096]{1,0:T(8,128)(2,1)} %collective-permute-done.13.refs_12_.refs_6_), channel_id=1, source_target_pairs={{0,4},{4,0},{8,12},{12,8},{1,5},{5,1},{9,13},{13,9},{2,6},{6,2},{1... | collective-permute-start | bytes 5111816 | tf_op jit(solution)/shard_map/ppermute | solution.py:76
  161.9 40.5 %collective-permute-start.22 = (bf16[560,1024]{1,0:T(8,128)(2,1)}, bf16[560,1024]{1,0:T(8,128)(2,1)S(1)}, u32[]{:S(2)}, u32[]{:S(2)}) collective-permute-start(bf16[560,1024]{1,0:T(8,128)(2,1)} %pad_maximum_fusion.1.refs_0_), channel_id=1, source_target_pairs={{0,1},{1,2},{2,3},{4,5},{5,6},{6,7},{8,9},{9,10},{10,11},{12,13},{... | collective-permute-start | bytes 3440648 | tf_op jit(solution)/shard_map/ppermute | solution.py:95
  167.3 35.1 %collective-permute-start.21 = (bf16[560,1024]{1,0:T(8,128)(2,1)}, bf16[560,1024]{1,0:T(8,128)(2,1)S(1)}, u32[]{:S(2)}, u32[]{:S(2)}) collective-permute-start(bf16[560,1024]{1,0:T(8,128)(2,1)} %pad_maximum_fusion.1.refs_0_), channel_id=1, source_target_pairs={{1,0},{2,1},{3,2},{5,4},{6,5},{7,6},{9,8},{10,9},{11,10},{13,12},{... | collective-permute-start | bytes 3440648 | tf_op jit(solution)/shard_map/ppermute | solution.py:91
  168.6 33.7 %collective-permute-start.20 = (bf16[4096,128]{1,0:T(8,128)(2,1)}, bf16[4096,128]{1,0:T(8,128)(2,1)S(1)}, u32[]{:S(2)}, u32[]{:S(2)}) collective-permute-start(bf16[4096,128]{1,0:T(8,128)(2,1)} %get-tuple-element.99), channel_id=1, source_target_pairs={{0,8},{4,12},{8,0},{12,4},{1,9},{5,13},{9,1},{13,5},{2,10},{6,14},... | collective-permute-start | bytes 3145736 | tf_op jit(solution)/shard_map/ppermute | solution.py:72
  202.4 32.0 %collective-permute-start.25 = (bf16[4096,128]{1,0:T(8,128)(2,1)S(1)}, bf16[4096,128]{1,0:T(8,128)(2,1)}, u32[]{:S(2)}, u32[]{:S(2)}) collective-permute-start(bf16[4096,128]{1,0:T(8,128)(2,1)S(1)} %collective-permute-done.20.refs_0_), channel_id=1, source_target_pairs={{0,4},{4,0},{8,12},{12,8},{1,5},{5,1},{9,13},{13,9},{2,6},{6,2},{1... | collective-permute-start | bytes 3145736 | tf_op jit(solution)/shard_map/ppermute | solution.py:76
  202.4 31.9 %collective-permute-start.24 = (bf16[4096,128]{1,0:T(8,128)(2,1)S(1)}, bf16[4096,128]{1,0:T(8,128)(2,1)}, u32[]{:S(2)}, u32[]{:S(2)}) collective-permute-start(bf16[4096,128]{1,0:T(8,128)(2,1)S(1)} %collective-permute-done.20.refs_0_), channel_id=1, source_target_pairs={{0,16},{16,0},{1,17},{17,1},{2,18},{18,2},{3,19},{19,3},{4,20},{20... | collective-permute-start | bytes 3145736 | tf_op jit(solution)/shard_map/ppermute | solution.py:87
  203.0 31.4 %collective-permute-start.23 = (bf16[4096,128]{1,0:T(8,128)(2,1)}, bf16[4096,128]{1,0:T(8,128)(2,1)}, u32[]{:S(2)}, u32[]{:S(2)}) collective-permute-start(bf16[4096,128]{1,0:T(8,128)(2,1)} %get-tuple-element.104), channel_id=1, source_target_pairs={{0,8},{4,12},{8,0},{12,4},{1,9},{5,13},{9,1},{13,5},{2,10},{6,14},... | collective-permute-start | bytes 3145736 | tf_op jit(solution)/shard_map/ppermute | solution.py:72
  203.6 31.0 %collective-permute-start.26 = (bf16[560,1024]{1,0:T(8,128)(2,1)S(1)}, bf16[560,1024]{1,0:T(8,128)(2,1)}, u32[]{:S(2)}, u32[]{:S(2)}) collective-permute-start(bf16[560,1024]{1,0:T(8,128)(2,1)S(1)} %collective-permute-done.21.refs_1_), channel_id=1, source_target_pairs={{1,0},{2,1},{5,4},{6,5},{9,8},{10,9},{13,12},{14,13},{17,16},{18,1... | collective-permute-start | bytes 3440648 | tf_op jit(solution)/shard_map/ppermute | solution.py:91
  204.8 29.7 %collective-permute-start.27 = (bf16[560,1024]{1,0:T(8,128)(2,1)S(1)}, bf16[560,1024]{1,0:T(8,128)(2,1)}, u32[]{:S(2)}, u32[]{:S(2)}) collective-permute-start(bf16[560,1024]{1,0:T(8,128)(2,1)S(1)} %collective-permute-done.22.refs_4_), channel_id=1, source_target_pairs={{1,2},{2,3},{5,6},{6,7},{9,10},{10,11},{13,14},{14,15},{17,18},{18... | collective-permute-start | bytes 3440648 | tf_op jit(solution)/shard_map/ppermute | solution.py:95
  234.5 6.0 %collective-permute-start.28 = (bf16[4096,128]{1,0:T(8,128)(2,1)}, bf16[4096,128]{1,0:T(8,128)(2,1)S(1)}, u32[]{:S(2)}, u32[]{:S(2)}) collective-permute-start(bf16[4096,128]{1,0:T(8,128)(2,1)} %collective-permute-done.24.refs_1_), channel_id=1, source_target_pairs={{0,4},{4,0},{8,12},{12,8},{1,5},{5,1},{9,13},{13,9},{2,6},{6,2},{1... | collective-permute-start | bytes 3145736 | tf_op jit(solution)/shard_map/ppermute | solution.py:76
  234.5 41.2 %collective-permute-start.31 = (bf16[560,1024]{1,0:T(8,128)(2,1)}, bf16[560,1024]{1,0:T(8,128)(2,1)}, u32[]{:S(2)}, u32[]{:S(2)}) collective-permute-start(bf16[560,1024]{1,0:T(8,128)(2,1)} %collective-permute-done.26.refs_2_), channel_id=1, source_target_pairs={{1,0},{5,4},{9,8},{13,12},{17,16},{21,20},{25,24},{29,28}} | collective-permute-start | bytes 3440648 | tf_op jit(solution)/shard_map/ppermute | solution.py:91
  235.8 39.9 %collective-permute-start.32 = (bf16[560,1024]{1,0:T(8,128)(2,1)}, bf16[560,1024]{1,0:T(8,128)(2,1)}, u32[]{:S(2)}, u32[]{:S(2)}) collective-permute-start(bf16[560,1024]{1,0:T(8,128)(2,1)} %collective-permute-done.27.refs_5_), channel_id=1, source_target_pairs={{2,3},{6,7},{10,11},{14,15},{18,19},{22,23},{26,27},{30,31}} | collective-permute-start | bytes 3440648 | tf_op jit(solution)/shard_map/ppermute | solution.py:95
  237.5 25.9 %collective-permute-start.29 = (bf16[4096,128]{1,0:T(8,128)(2,1)}, bf16[4096,128]{1,0:T(8,128)(2,1)}, u32[]{:S(2)}, u32[]{:S(2)}) collective-permute-start(bf16[4096,128]{1,0:T(8,128)(2,1)} %get-tuple-element.113), channel_id=1, source_target_pairs={{0,8},{4,12},{8,0},{12,4},{1,9},{5,13},{9,1},{13,5},{2,10},{6,14},... | collective-permute-start | bytes 3145736 | tf_op jit(solution)/shard_map/ppermute | solution.py:72
  239.0 25.6 %collective-permute-start.30 = (bf16[4096,128]{1,0:T(8,128)(2,1)}, bf16[4096,128]{1,0:T(8,128)(2,1)}, u32[]{:S(2)}, u32[]{:S(2)}) collective-permute-start(bf16[4096,128]{1,0:T(8,128)(2,1)} %collective-permute-done.23.refs_0_.refs_4_), channel_id=1, source_target_pairs={{0,16},{16,0},{1,17},{17,1},{2,18},{18,2},{3,19},{19,3},{4,20},{20... | collective-permute-start | bytes 3145736 | tf_op jit(solution)/shard_map/ppermute | solution.py:87
  254.8 89.6 %reduce-scatter.8.cloned.1.call-start = ((), (), s32[]{:S(2)}) async-start(), calls=%async_computation.6 | async-start | bytes 1843200 | tf_op jit(solution)/shard_map/reduce_scatter | solution.py:378
  275.7 2.9 collective-permute-start.33
  278.6 2.9 collective-permute-start.34
  278.8 48.2 %collective-permute-start.35 = (bf16[4096,256]{1,0:T(8,128)(2,1)}, bf16[4096,256]{1,0:T(8,128)(2,1)}, u32[]{:S(2)}, u32[]{:S(2)}) collective-permute-start(bf16[4096,256]{1,0:T(8,128)(2,1)} %slice.25), channel_id=1, source_target_pairs={{0,8},{4,12},{8,0},{12,4},{1,9},{5,13},{9,1},{13,5},{2,10},{6,14},... | collective-permute-start | bytes 6291464 | tf_op jit(solution)/shard_map/ppermute | solution.py:72
  295.9 115.7 %reduce-scatter.10.cloned.1.call-start = ((), (), s32[]{:S(2)}) async-start(), calls=%async_computation.7 | async-start | bytes 1843200 | tf_op jit(solution)/shard_map/reduce_scatter | solution.py:378
  296.1 26.6 %collective-permute-start.36 = (bf16[4096,128]{1,0:T(8,128)(2,1)}, bf16[4096,128]{1,0:T(8,128)(2,1)}, u32[]{:S(2)}, u32[]{:S(2)}) collective-permute-start(bf16[4096,128]{1,0:T(8,128)(2,1)} %collective-permute-done.29.refs_0_.refs_8_), channel_id=1, source_target_pairs={{0,16},{16,0},{1,17},{17,1},{2,18},{18,2},{3,19},{19,3},{4,20},{20... | collective-permute-start | bytes 3145736 | tf_op jit(solution)/shard_map/ppermute | solution.py:87
  297.8 29.2 %collective-permute-start.37 = (bf16[4096,128]{1,0:T(8,128)(2,1)}, bf16[4096,128]{1,0:T(8,128)(2,1)}, u32[]{:S(2)}, u32[]{:S(2)}) collective-permute-start(bf16[4096,128]{1,0:T(8,128)(2,1)} %collective-permute-done.29.refs_0_.refs_8_), channel_id=1, source_target_pairs={{0,4},{4,0},{8,12},{12,8},{1,5},{5,1},{9,13},{13,9},{2,6},{6,2},{1... | collective-permute-start | bytes 3145736 | tf_op jit(solution)/shard_map/ppermute | solution.py:76
  327.0 2.9 collective-permute-start.38
  344.2 67.5 %reduce-scatter.12.cloned.1.call-start = ((), (), s32[]{:S(2)}) async-start(), calls=%async_computation.8 | async-start | bytes 1843200 | tf_op jit(solution)/shard_map/reduce_scatter | solution.py:378
  344.2 4.6 collective-permute-start.39
  362.1 133.5 %reduce-scatter.14.cloned.1.call-start = ((), (), s32[]{:S(2)}) async-start(), calls=%async_computation.9 | async-start | bytes 5734400 | tf_op jit(solution)/shard_map/reduce_scatter | solution.py:378
  411.5 84.0 %copy-start.13 = (bf16[720,256]{1,0:T(8,128)(2,1)S(1)}, bf16[720,256]{1,0:T(8,128)(2,1)}, u32[]{:S(2)}) copy-start(bf16[720,256]{1,0:T(8,128)(2,1)} %reduce-scatter.6.cloned.1.call-done) | copy-start | bytes 1105924
  411.5 84.0 %copy-start.14 = (bf16[720,256]{1,0:T(8,128)(2,1)S(1)}, bf16[720,256]{1,0:T(8,128)(2,1)}, u32[]{:S(2)}) copy-start(bf16[720,256]{1,0:T(8,128)(2,1)} %reduce-scatter.8.cloned.1.call-done) | copy-start | bytes 1105924
  (15 other events, 249.1 us)
Sparse Core Ops, SparseCore 0:
  255.0 40.1 reduce-scatter.5
  297.5 33.0 reduce-scatter.7
  344.3 32.0 reduce-scatter.9
  378.7 32.6 reduce-scatter.11
  413.5 82.0 reduce-scatter.13

commit v4 on v3

--- a/solution.py
+++ b/solution.py
@@ -410,7 +410,7 @@
     (xd, y1, cy0, cx1, d3, u3, *os_in), (o0i, nb) = gate((xd, y1, cy0, cx1, d3, u3, *os_in), (os_in[0], nb))
     ox0 = swap_x(o0i)
     e1, f1 = down(nb, 1), up(nb, 1)
-    cxd, cy1 = cores(xd, y1)
+    cxd, cy1 = swap_core(xd), swap_core(y1)
     toks_a = [na, d1, d2, d3, u1, u2, u3]
     ws = [w_in, sib, x0, y0, x1, y1, xd, cx0, cy0, cx1, cy1, cxd]
     act_a0, tail0, norm_a = first(place, gain, toks_a, ws, conv_kernel, None, 0, la)
@@ -449,8 +449,9 @@
     (p3, norm_b), _ = gate((p3, norm_b), ())
     (act_b1,) = first(place, gain, [norm_b], ws, conv_kernel, tail1, 1, lons - la)
     s = scatter(second(place, (act_b0, act_b1), shards, pieces, (0, 1, 2, 3)))
-    mixed = jnp.concatenate([jnp.concatenate([r0, r1, r2, r3], axis=1), s], axis=0)
-    return (tokens.astype(jnp.float32) + mixed.astype(jnp.float32)).astype(jnp.bfloat16)
+    top = tokens[: la * LAT].astype(jnp.float32) + jnp.concatenate([r0, r1, r2, r3], axis=1).astype(jnp.float32)
+    low = tokens[la * LAT :].astype(jnp.float32) + s.astype(jnp.float32)
+    return jnp.concatenate([top.astype(jnp.bfloat16), low.astype(jnp.bfloat16)], axis=0)
 
 
 def solution(mesh):

time: 517 us -> 511 us (0.988)
  waiting for transfers between devices: 235 us -> 227 us
  transfers between devices with their start and end apart: 45 -> 45, of which waited for: 18 -> 17; matrix products, arithmetic and copies ran while one was open for 3% -> 4% of each run, Pallas kernels for 37% -> 37%
where the time goes in v4:
time: 511 us; the launch traced here: 503 us
  waiting for transfers between devices  227 us (44%)
  Pallas kernels  187 us (37%)
  starting transfers between devices  44.9 us (9%)
  local copies, waits for them, and re-layouts  21.4 us (4%)
  between operations  14 us (3%)
  other arithmetic  8.1 us (2%)
    pallas_call x4, Pallas kernels, first(): pl.pallas_call(functools.partial(first_kernel, has_tail, len(toks), len(w...  107 us
    pallas_call x5, Pallas kernels, second(): pl.pallas_call(functools.partial(second_kernel, quarters, tuple((len(piec...  80.6 us
    reduce_scatter x5, waiting for transfers between devices, scatter(): return lax.psum_scatter(v, 'col', scatter_dimension=1, tiled=True)  80.2 us
    ppermute x6, waiting for transfers between devices, down(): return lax.ppermute(v, 'col', [(i, i - 1) for i in range(1, 5 - hop)])  50.1 us
    ppermute x7, waiting for transfers between devices, swap_x(): return lax.ppermute(v, 'row', [(i, i ^ 2) for i in range(4)])  41.6 us
    ppermute x6, waiting for transfers between devices, up(): return lax.ppermute(v, 'col', [(i, i + 1) for i in range(hop - 1, 3)])  33.7 us
    ppermute x6, starting transfers between devices, up(): return lax.ppermute(v, 'col', [(i, i + 1) for i in range(hop - 1, 3)])  16.2 us
    ppermute x14, waiting for transfers between devices, swap_core(): return lax.ppermute(v, 'row', [(i, i ^ 1) for i in range(4)])  13.3 us
  transfers between devices with their start and end apart: 45, of which 17 were waited for; matrix products, arithmetic and copies ran while one was open for 4% of the time, Pallas kernels for 37%

profile of v4, /device:TPU:0, one launch (start us, length us, event | category | flops | bytes accessed | tf_op | source)
XLA Modules:
  0.0 502.7 jit_solution(16662900287786043971)
XLA Ops:
  8.0 2.6 collective-permute-start.1
  10.6 2.3 constant_dynamic-slice_fusion.3
  12.9 7.0 %collective-permute-done.1 = bf16[40,1024]{1,0:T(8,128)(2,1)S(1)} collective-permute-done((bf16[40,1024]{1,0:T(8,128)(2,1)S(1)}, bf16[40,1024]{1,0:T(8,128)(2,1)S(1)}, u32[]{:S(2)}, u32[]{:S(2)}) %collective-permute-start.1) | collective-permute-done | bytes 81952 | tf_op jit(solution)/shard_map/ppermute | solution.py:28
  21.2 3.0 collective-permute-start.2
  24.2 3.6 collective-permute-start.5
  27.8 1.3 collective-permute-start.4
  29.1 33.7 %collective-permute-done.5.refs_4_ = bf16[800,1024]{1,0:T(8,128)(2,1)S(1)} collective-permute-done((bf16[800,1024]{1,0:T(8,128)(2,1)S(1)}, bf16[800,1024]{1,0:T(8,128)(2,1)S(1)}, u32[]{:S(2)}, u32[]{:S(2)}) %collective-permute-start.5) | collective-permute-done | bytes 1638432 | tf_op jit(solution)/shard_map/ppermute | solution.py:95
  62.8 4.2 collective-permute-done.4.refs_1_
  68.2 1.5 collective-permute-start.7
  71.0 1.8 collective-permute-start.11
  72.8 2.7 slice.31
  75.6 33.2 %collective-permute-done.10.refs_2_ = bf16[800,1024]{1,0:T(8,128)(2,1)} collective-permute-done((bf16[800,1024]{1,0:T(8,128)(2,1)S(1)}, bf16[800,1024]{1,0:T(8,128)(2,1)}, u32[]{:S(2)}, u32[]{:S(2)}) %collective-permute-start.10) | collective-permute-done | bytes 1638432 | tf_op jit(solution)/shard_map/ppermute | solution.py:91
  111.7 1.9 collective-permute-done.14.refs_15_.refs_9_
  116.3 1.9 collective-permute-start.17
  118.2 1.5 collective-permute-start.12
  119.7 3.0 slice.32
  122.7 3.6 constant_dynamic-slice_fusion
  126.3 28.8 %collective-permute-done.12.refs_13_.refs_7_ = bf16[192,4096]{1,0:T(8,128)(2,1)} collective-permute-done((bf16[192,4096]{1,0:T(8,128)(2,1)}, bf16[192,4096]{1,0:T(8,128)(2,1)}, u32[]{:S(2)}, u32[]{:S(2)}) %collective-permute-start.12) | collective-permute-done | bytes 1572896 | tf_op jit(solution)/shard_map/ppermute | solution.py:72
  155.2 1.4 collective-permute-done.16.refs_3_
  158.4 5.4 %collective-permute-start.22 = (bf16[560,1024]{1,0:T(8,128)(2,1)}, bf16[560,1024]{1,0:T(8,128)(2,1)S(1)}, u32[]{:S(2)}, u32[]{:S(2)}) collective-permute-start(bf16[560,1024]{1,0:T(8,128)(2,1)} %pad_maximum_fusion.2.refs_0_), channel_id=1, source_target_pairs={{0,1},{1,2},{2,3},{4,5},{5,6},{6,7},{8,9},{9,10},{10,11},{12,13},{... | collective-permute-start | bytes 3440648 | tf_op jit(solution)/shard_map/ppermute | solution.py:95
  163.8 1.3 collective-permute-start.21
  165.1 1.6 collective-permute-start.20
  166.7 32.2 %first.4 = (bf16[720,2048]{1,0:T(8,128)(2,1)}, bf16[80,2048]{1,0:T(8,128)(2,1)}, bf16[800,4096]{1,0:T(8,128)(2,1)}) custom-call(s32[3]{0:T(128)} %pad_add_fusion.place_ref, f32[4,1024]{1,0:T(4,128)} %reshape.3.gain_ref, bf16[800,1024]{1,0:T(8,128)(2,1)} %copy-done.6, bf16[800,1024]{1,0:T(8,128)(2,1)} %copy-done.18, ...), custom_call_target="tpu_custom_call" | custom-call | flops 13421772800 | bytes 16777216 | tf_op jit(solution)/shard_map/first/pallas_call | solution.py:255
  201.4 1.9 collective-permute-start.27
  203.3 27.6 %first.5 = (bf16[720,2048]{1,0:T(8,128)(2,1)}, bf16[80,2048]{1,0:T(8,128)(2,1)}) custom-call(s32[3]{0:T(128)} %pad_add_fusion.place_ref, f32[4,1024]{1,0:T(4,128)} %reshape.3.gain_ref, bf16[800,4096]{1,0:T(8,128)(2,1)} %get-tuple-element.100.refs_0_, bf16[1024,4096]{1,0:T(8,128)(2,1)} %refs_1_.3, bf16[1024,4096]{1,0:T(8,128)(2,1)} %collective-permute-done.3.refs_8_.refs_2_, ...), custom_call_target="tpu_custom_call" | custom-call | flops 13421772800 | bytes 16777216 | tf_op jit(solution)/shard_map/first/pallas_call | solution.py:255
  231.1 1.3 collective-permute-start.31
  232.4 1.7 collective-permute-start.32
  234.1 1.5 collective-permute-start.29
  235.6 1.5 collective-permute-start.30
  238.1 13.3 %second.5 = bf16[720,1024]{1,0:T(8,128)(2,1)} custom-call(s32[3]{0:T(128)} %pad_add_fusion.place_ref, bf16[720,2048]{1,0:T(8,128)(2,1)} %get-tuple-element.95.act_l, bf16[720,2048]{1,0:T(8,128)(2,1)} %get-tuple-element.135.act_r, bf16[4096,1024]{1,0:T(8,128)(2,1)} %own.9, bf16[4096,1024]{1,0:T(8,128)(2,1)} %collective-permute-done.8.sib, ...), custom_call_target="tpu_custom_call" | custom-call | flops 6039797760 | bytes 8388608 | tf_op jit(solution)/shard_map/second/pallas_call | solution.py:356
  251.5 8.5 %collective-permute-done.29.refs_0_.refs_8_ = bf16[4096,128]{1,0:T(8,128)(2,1)} collective-permute-done((bf16[4096,128]{1,0:T(8,128)(2,1)}, bf16[4096,128]{1,0:T(8,128)(2,1)}, u32[]{:S(2)}, u32[]{:S(2)}) %collective-permute-start.29) | collective-permute-done | bytes 1048608 | tf_op jit(solution)/shard_map/ppermute | solution.py:72
  261.2 11.1 %collective-permute-done.31.refs_3_ = bf16[560,1024]{1,0:T(8,128)(2,1)} collective-permute-done((bf16[560,1024]{1,0:T(8,128)(2,1)}, bf16[560,1024]{1,0:T(8,128)(2,1)}, u32[]{:S(2)}, u32[]{:S(2)}) %collective-permute-start.31) | collective-permute-done | bytes 1146912 | tf_op jit(solution)/shard_map/ppermute | solution.py:91
  272.3 2.9 collective-permute-done.33.refs_3_.refs_7_
  275.3 1.5 collective-permute-start.35
  279.0 13.4 %second.6 = bf16[720,1024]{1,0:T(8,128)(2,1)} custom-call(s32[3]{0:T(128)} %pad_add_fusion.place_ref, bf16[720,2048]{1,0:T(8,128)(2,1)} %get-tuple-element.95.act_l, bf16[720,2048]{1,0:T(8,128)(2,1)} %get-tuple-element.135.act_r, bf16[4096,1024]{1,0:T(8,128)(2,1)} %own.9, bf16[4096,1024]{1,0:T(8,128)(2,1)} %collective-permute-done.8.sib, ...), custom_call_target="tpu_custom_call" | custom-call | flops 6039797760 | bytes 8388608 | tf_op jit(solution)/shard_map/second/pallas_call | solution.py:356
  292.7 1.6 collective-permute-start.36
  294.3 25.0 %first.6 = (bf16[560,2048]{1,0:T(8,128)(2,1)}, bf16[560,4096]{1,0:T(8,128)(2,1)}) custom-call(s32[3]{0:T(128)} %pad_add_fusion.place_ref, f32[4,1024]{1,0:T(4,128)} %reshape.3.gain_ref, bf16[560,1024]{1,0:T(8,128)(2,1)} %pad_maximum_fusion.2.refs_0_, bf16[560,1024]{1,0:T(8,128)(2,1)} %copy-done.8, bf16[560,1024]{1,0:T(8,128)(2,1)} %collective-permute-done.26.refs_2_, ...), custom_call_target="tpu_custom_call" | custom-call | flops 9395240960 | bytes 16777216 | tf_op jit(solution)/shard_map/first/pallas_call | solution.py:255
  319.3 4.2 collective-permute-done.35.refs_0_.refs_12_
  323.6 2.9 collective-permute-done.38.refs_3_.refs_11_
  327.4 13.3 %second.7 = bf16[720,1024]{1,0:T(8,128)(2,1)} custom-call(s32[3]{0:T(128)} %pad_add_fusion.place_ref, bf16[720,2048]{1,0:T(8,128)(2,1)} %get-tuple-element.95.act_l, bf16[720,2048]{1,0:T(8,128)(2,1)} %get-tuple-element.135.act_r, bf16[4096,1024]{1,0:T(8,128)(2,1)} %own.9, bf16[4096,1024]{1,0:T(8,128)(2,1)} %collective-permute-done.8.sib, ...), custom_call_target="tpu_custom_call" | custom-call | flops 6039797760 | bytes 8388608 | tf_op jit(solution)/shard_map/second/pallas_call | solution.py:356
  341.0 4.4 collective-permute-done.39.refs_1_.refs_13_
  345.4 13.3 %second.8 = bf16[720,1024]{1,0:T(8,128)(2,1)} custom-call(s32[3]{0:T(128)} %pad_add_fusion.place_ref, bf16[720,2048]{1,0:T(8,128)(2,1)} %get-tuple-element.95.act_l, bf16[720,2048]{1,0:T(8,128)(2,1)} %get-tuple-element.135.act_r, bf16[4096,1024]{1,0:T(8,128)(2,1)} %own.9, bf16[4096,1024]{1,0:T(8,128)(2,1)} %collective-permute-done.8.sib, ...), custom_call_target="tpu_custom_call" | custom-call | flops 6039797760 | bytes 8388608 | tf_op jit(solution)/shard_map/second/pallas_call | solution.py:356
  359.0 21.8 %first.7.act_r = bf16[560,2048]{1,0:T(8,128)(2,1)} custom-call(s32[3]{0:T(128)} %pad_add_fusion.place_ref, f32[4,1024]{1,0:T(4,128)} %reshape.3.gain_ref, bf16[560,4096]{1,0:T(8,128)(2,1)} %get-tuple-element.139.refs_0_, bf16[1024,4096]{1,0:T(8,128)(2,1)} %refs_1_.3, bf16[1024,4096]{1,0:T(8,128)(2,1)} %collective-permute-done.3.refs_8_.refs_2_, ...), custom_call_target="tpu_custom_call" | custom-call | flops 9395240960 | bytes 16777216 | tf_op jit(solution)/shard_map/first/pallas_call | solution.py:255
  380.8 27.4 %second.9 = bf16[560,4096]{1,0:T(8,128)(2,1)} custom-call(s32[3]{0:T(128)} %pad_add_fusion.place_ref, bf16[560,2048]{1,0:T(8,128)(2,1)} %get-tuple-element.137.act_l, bf16[560,2048]{1,0:T(8,128)(2,1)} %first.7.act_r, bf16[4096,1024]{1,0:T(8,128)(2,1)} %own.9, bf16[4096,1024]{1,0:T(8,128)(2,1)} %collective-permute-done.8.sib, bf16[4096,128]{1,0:T(8,128)(2,1)} %copy-done.9, ...), custom_call_target="tpu_custom_call" | custom-call | flops 18790481920 | bytes 33554432 | tf_op jit(solution)/shard_map/second/pallas_call | solution.py:356
  409.2 2.7 add_convert_fusion
  411.9 80.2 %reduce-scatter.14.cloned.1.call-done = bf16[560,1024]{1,0:T(8,128)(2,1)} async-done(((bf16[560,4096]{1,0:T(8,128)(2,1)}), bf16[560,1024]{1,0:T(8,128)(2,1)}) %reduce-scatter.14.cloned.1.call-update) | async-done | bytes 1146896 | tf_op jit(solution)/shard_map/reduce_scatter | solution.py:378
  492.1 1.8 add_convert_fusion.1
  494.0 1.7 pad_maximum_fusion
  (106 shorter events, 22.6 us)
Async XLA Ops:
  6.5 317.0 %reduce-scatter.6.cloned.1.call-start = ((), (), s32[]{:S(2)}) async-start(), calls=%async_computation.5 | async-start | bytes 1843200 | tf_op jit(solution)/shard_map/reduce_scatter | solution.py:378
  6.5 60.4 %collective-permute-start.3 = (bf16[1024,4096]{1,0:T(8,128)(2,1)}, bf16[1024,4096]{1,0:T(8,128)(2,1)}, u32[]{:S(2)}, u32[]{:S(2)}) collective-permute-start(bf16[1024,4096]{1,0:T(8,128)(2,1)} %refs_1_.3), channel_id=1, source_target_pairs={{0,4},{4,0},{8,12},{12,8},{1,5},{5,1},{9,13},{13,9},{2,6},{6,2},{1... | collective-permute-start | bytes 25165832 | tf_op jit(solution)/shard_map/ppermute | solution.py:76
  7.0 60.0 %collective-permute-start.8 = (bf16[4096,1024]{1,0:T(8,128)(2,1)}, bf16[4096,1024]{1,0:T(8,128)(2,1)}, u32[]{:S(2)}, u32[]{:S(2)}) collective-permute-start(bf16[4096,1024]{1,0:T(8,128)(2,1)} %own.9), channel_id=1, source_target_pairs={{0,4},{4,0},{8,12},{12,8},{1,5},{5,1},{9,13},{13,9},{2,6},{6,2},{1... | collective-permute-start | bytes 25165832 | tf_op jit(solution)/shard_map/ppermute | solution.py:76
  8.0 11.9 %collective-permute-start.1 = (bf16[40,1024]{1,0:T(8,128)(2,1)S(1)}, bf16[40,1024]{1,0:T(8,128)(2,1)S(1)}, u32[]{:S(2)}, u32[]{:S(2)}) collective-permute-start(bf16[40,1024]{1,0:T(8,128)(2,1)S(1)} %get-tuple-element.146), channel_id=1, source_target_pairs={{4,0},{8,4},{12,8},{0,12},{5,1},{9,5},{13,9},{1,13},{6,2},{10,6},{... | collective-permute-start | bytes 245768 | tf_op jit(solution)/shard_map/ppermute | solution.py:28
  10.6 10.5 %collective-permute-start = (bf16[40,1024]{1,0:T(8,128)(2,1)S(1)}, bf16[40,1024]{1,0:T(8,128)(2,1)S(1)}, u32[]{:S(2)}, u32[]{:S(2)}) collective-permute-start(bf16[40,1024]{1,0:T(8,128)(2,1)S(1)} %get-tuple-element.147), channel_id=1, source_target_pairs={{0,4},{4,8},{8,12},{12,0},{1,5},{5,9},{9,13},{13,1},{2,6},{6,10},{... | collective-permute-start | bytes 245768 | tf_op jit(solution)/shard_map/ppermute | solution.py:26
  21.2 45.8 %copy-start.6 = (bf16[800,1024]{1,0:T(8,128)(2,1)}, bf16[800,1024]{1,0:T(8,128)(2,1)S(1)}, u32[]{:S(2)}) copy-start(bf16[800,1024]{1,0:T(8,128)(2,1)S(1)} %pad_maximum_fusion.1.refs_0_) | copy-start | bytes 4915204
  21.2 45.8 %collective-permute-start.2 = (bf16[208,4096]{1,0:T(8,128)(2,1)S(1)}, bf16[208,4096]{1,0:T(8,128)(2,1)S(1)}, u32[]{:S(2)}, u32[]{:S(2)}) collective-permute-start(bf16[208,4096]{1,0:T(8,128)(2,1)S(1)} %get-tuple-element.74), channel_id=1, source_target_pairs={{0,8},{4,12},{8,0},{12,4},{1,9},{5,13},{9,1},{13,5},{2,10},{6,14},... | collective-permute-start | bytes 5111816 | tf_op jit(solution)/shard_map/ppermute | solution.py:72
  24.2 38.5 %collective-permute-start.5 = (bf16[800,1024]{1,0:T(8,128)(2,1)S(1)}, bf16[800,1024]{1,0:T(8,128)(2,1)S(1)}, u32[]{:S(2)}, u32[]{:S(2)}) collective-permute-start(bf16[800,1024]{1,0:T(8,128)(2,1)S(1)} %pad_maximum_fusion.1.refs_0_), channel_id=1, source_target_pairs={{0,1},{1,2},{2,3},{4,5},{5,6},{6,7},{8,9},{9,10},{10,11},{12,13},{... | collective-permute-start | bytes 4915208 | tf_op jit(solution)/shard_map/ppermute | solution.py:95
  27.8 39.2 %collective-permute-start.4 = (bf16[800,1024]{1,0:T(8,128)(2,1)S(1)}, bf16[800,1024]{1,0:T(8,128)(2,1)S(1)}, u32[]{:S(2)}, u32[]{:S(2)}) collective-permute-start(bf16[800,1024]{1,0:T(8,128)(2,1)S(1)} %pad_maximum_fusion.1.refs_0_), channel_id=1, source_target_pairs={{1,0},{2,1},{3,2},{5,4},{6,5},{7,6},{9,8},{10,9},{11,10},{13,12},{... | collective-permute-start | bytes 4915208 | tf_op jit(solution)/shard_map/ppermute | solution.py:91
  62.8 52.2 %copy-start.17 = (bf16[800,1024]{1,0:T(8,128)(2,1)}, bf16[800,1024]{1,0:T(8,128)(2,1)S(1)}, u32[]{:S(2)}) copy-start(bf16[800,1024]{1,0:T(8,128)(2,1)S(1)} %collective-permute-done.5.refs_4_) | copy-start | bytes 4915204
  67.0 49.3 %copy-start.18 = (bf16[800,1024]{1,0:T(8,128)(2,1)}, bf16[800,1024]{1,0:T(8,128)(2,1)S(1)}, u32[]{:S(2)}) copy-start(bf16[800,1024]{1,0:T(8,128)(2,1)S(1)} %collective-permute-done.4.refs_1_) | copy-start | bytes 4915204
  67.0 41.8 %collective-permute-start.9 = (bf16[208,4096]{1,0:T(8,128)(2,1)S(1)}, bf16[208,4096]{1,0:T(8,128)(2,1)S(1)}, u32[]{:S(2)}, u32[]{:S(2)}) collective-permute-start(bf16[208,4096]{1,0:T(8,128)(2,1)S(1)} %collective-permute-done.2.refs_9_.refs_3_), channel_id=1, source_target_pairs={{0,4},{4,0},{8,12},{12,8},{1,5},{5,1},{9,13},{13,9},{2,6},{6,2},{1... | collective-permute-start | bytes 5111816 | tf_op jit(solution)/shard_map/ppermute | solution.py:76
  67.1 41.7 %collective-permute-start.6 = (bf16[208,4096]{1,0:T(8,128)(2,1)S(1)}, bf16[208,4096]{1,0:T(8,128)(2,1)}, u32[]{:S(2)}, u32[]{:S(2)}) collective-permute-start(bf16[208,4096]{1,0:T(8,128)(2,1)S(1)} %get-tuple-element.76), channel_id=1, source_target_pairs={{0,8},{4,12},{8,0},{12,4},{1,9},{5,13},{9,1},{13,5},{2,10},{6,14},... | collective-permute-start | bytes 5111816 | tf_op jit(solution)/shard_map/ppermute | solution.py:72
  68.2 40.6 %collective-permute-start.7 = (bf16[208,4096]{1,0:T(8,128)(2,1)S(1)}, bf16[208,4096]{1,0:T(8,128)(2,1)S(1)}, u32[]{:S(2)}, u32[]{:S(2)}) collective-permute-start(bf16[208,4096]{1,0:T(8,128)(2,1)S(1)} %collective-permute-done.2.refs_9_.refs_3_), channel_id=1, source_target_pairs={{0,16},{16,0},{1,17},{17,1},{2,18},{18,2},{3,19},{19,3},{4,20},{20... | collective-permute-start | bytes 5111816 | tf_op jit(solution)/shard_map/ppermute | solution.py:87
  69.7 39.1 %collective-permute-start.10 = (bf16[800,1024]{1,0:T(8,128)(2,1)S(1)}, bf16[800,1024]{1,0:T(8,128)(2,1)}, u32[]{:S(2)}, u32[]{:S(2)}) collective-permute-start(bf16[800,1024]{1,0:T(8,128)(2,1)S(1)} %collective-permute-done.4.refs_1_), channel_id=1, source_target_pairs={{1,0},{2,1},{5,4},{6,5},{9,8},{10,9},{13,12},{14,13},{17,16},{18,1... | collective-permute-start | bytes 4915208 | tf_op jit(solution)/shard_map/ppermute | solution.py:91
  71.0 37.8 %collective-permute-start.11 = (bf16[800,1024]{1,0:T(8,128)(2,1)S(1)}, bf16[800,1024]{1,0:T(8,128)(2,1)}, u32[]{:S(2)}, u32[]{:S(2)}) collective-permute-start(bf16[800,1024]{1,0:T(8,128)(2,1)S(1)} %collective-permute-done.5.refs_4_), channel_id=1, source_target_pairs={{1,2},{2,3},{5,6},{6,7},{9,10},{10,11},{13,14},{14,15},{17,18},{18... | collective-permute-start | bytes 4915208 | tf_op jit(solution)/shard_map/ppermute | solution.py:95
  110.0 3.6 collective-permute-start.14
  111.2 45.4 %collective-permute-start.13 = (bf16[208,4096]{1,0:T(8,128)(2,1)}, bf16[208,4096]{1,0:T(8,128)(2,1)}, u32[]{:S(2)}, u32[]{:S(2)}) collective-permute-start(bf16[208,4096]{1,0:T(8,128)(2,1)} %collective-permute-done.6.refs_11_.refs_5_), channel_id=1, source_target_pairs={{0,16},{16,0},{1,17},{17,1},{2,18},{18,2},{3,19},{19,3},{4,20},{20... | collective-permute-start | bytes 5111816 | tf_op jit(solution)/shard_map/ppermute | solution.py:87
  114.9 41.8 %collective-permute-start.15 = (bf16[208,4096]{1,0:T(8,128)(2,1)}, bf16[208,4096]{1,0:T(8,128)(2,1)}, u32[]{:S(2)}, u32[]{:S(2)}) collective-permute-start(bf16[208,4096]{1,0:T(8,128)(2,1)} %collective-permute-done.6.refs_11_.refs_5_), channel_id=1, source_target_pairs={{0,4},{4,0},{8,12},{12,8},{1,5},{5,1},{9,13},{13,9},{2,6},{6,2},{1... | collective-permute-start | bytes 5111816 | tf_op jit(solution)/shard_map/ppermute | solution.py:76
  115.0 41.6 %collective-permute-start.16 = (bf16[800,1024]{1,0:T(8,128)(2,1)}, bf16[800,1024]{1,0:T(8,128)(2,1)}, u32[]{:S(2)}, u32[]{:S(2)}) collective-permute-start(bf16[800,1024]{1,0:T(8,128)(2,1)} %collective-permute-done.10.refs_2_), channel_id=1, source_target_pairs={{1,0},{5,4},{9,8},{13,12},{17,16},{21,20},{25,24},{29,28}} | collective-permute-start | bytes 4915208 | tf_op jit(solution)/shard_map/ppermute | solution.py:91
  116.3 40.3 %collective-permute-start.17 = (bf16[800,1024]{1,0:T(8,128)(2,1)}, bf16[800,1024]{1,0:T(8,128)(2,1)}, u32[]{:S(2)}, u32[]{:S(2)}) collective-permute-start(bf16[800,1024]{1,0:T(8,128)(2,1)} %collective-permute-done.11.refs_5_), channel_id=1, source_target_pairs={{2,3},{6,7},{10,11},{14,15},{18,19},{22,23},{26,27},{30,31}} | collective-permute-start | bytes 4915208 | tf_op jit(solution)/shard_map/ppermute | solution.py:95
  118.2 37.0 %collective-permute-start.12 = (bf16[192,4096]{1,0:T(8,128)(2,1)}, bf16[192,4096]{1,0:T(8,128)(2,1)}, u32[]{:S(2)}, u32[]{:S(2)}) collective-permute-start(bf16[192,4096]{1,0:T(8,128)(2,1)} %slice.31), channel_id=1, source_target_pairs={{0,8},{4,12},{8,0},{12,4},{1,9},{5,13},{9,1},{13,5},{2,10},{6,14},... | collective-permute-start | bytes 4718600 | tf_op jit(solution)/shard_map/ppermute | solution.py:72
  156.6 10.0 %collective-permute-start.18 = (bf16[208,4096]{1,0:T(8,128)(2,1)}, bf16[208,4096]{1,0:T(8,128)(2,1)}, u32[]{:S(2)}, u32[]{:S(2)}) collective-permute-start(bf16[208,4096]{1,0:T(8,128)(2,1)} %collective-permute-done.13.refs_12_.refs_6_), channel_id=1, source_target_pairs={{0,4},{4,0},{8,12},{12,8},{1,5},{5,1},{9,13},{13,9},{2,6},{6,2},{1... | collective-permute-start | bytes 5111816 | tf_op jit(solution)/shard_map/ppermute | solution.py:76
  156.7 9.9 %collective-permute-start.19 = (bf16[192,4096]{1,0:T(8,128)(2,1)}, bf16[192,4096]{1,0:T(8,128)(2,1)}, u32[]{:S(2)}, u32[]{:S(2)}) collective-permute-start(bf16[192,4096]{1,0:T(8,128)(2,1)} %collective-permute-done.12.refs_13_.refs_7_), channel_id=1, source_target_pairs={{0,4},{4,0},{8,12},{12,8},{1,5},{5,1},{9,13},{13,9},{2,6},{6,2},{1... | collective-permute-start | bytes 4718600 | tf_op jit(solution)/shard_map/ppermute | solution.py:76
  158.4 40.5 %collective-permute-start.22 = (bf16[560,1024]{1,0:T(8,128)(2,1)}, bf16[560,1024]{1,0:T(8,128)(2,1)S(1)}, u32[]{:S(2)}, u32[]{:S(2)}) collective-permute-start(bf16[560,1024]{1,0:T(8,128)(2,1)} %pad_maximum_fusion.2.refs_0_), channel_id=1, source_target_pairs={{0,1},{1,2},{2,3},{4,5},{5,6},{6,7},{8,9},{9,10},{10,11},{12,13},{... | collective-permute-start | bytes 3440648 | tf_op jit(solution)/shard_map/ppermute | solution.py:95
  163.8 35.1 %collective-permute-start.21 = (bf16[560,1024]{1,0:T(8,128)(2,1)}, bf16[560,1024]{1,0:T(8,128)(2,1)S(1)}, u32[]{:S(2)}, u32[]{:S(2)}) collective-permute-start(bf16[560,1024]{1,0:T(8,128)(2,1)} %pad_maximum_fusion.2.refs_0_), channel_id=1, source_target_pairs={{1,0},{2,1},{3,2},{5,4},{6,5},{7,6},{9,8},{10,9},{11,10},{13,12},{... | collective-permute-start | bytes 3440648 | tf_op jit(solution)/shard_map/ppermute | solution.py:91
  165.1 33.8 %collective-permute-start.20 = (bf16[4096,128]{1,0:T(8,128)(2,1)}, bf16[4096,128]{1,0:T(8,128)(2,1)S(1)}, u32[]{:S(2)}, u32[]{:S(2)}) collective-permute-start(bf16[4096,128]{1,0:T(8,128)(2,1)} %get-tuple-element.97), channel_id=1, source_target_pairs={{0,8},{4,12},{8,0},{12,4},{1,9},{5,13},{9,1},{13,5},{2,10},{6,14},... | collective-permute-start | bytes 3145736 | tf_op jit(solution)/shard_map/ppermute | solution.py:72
  198.9 32.0 %collective-permute-start.25 = (bf16[4096,128]{1,0:T(8,128)(2,1)S(1)}, bf16[4096,128]{1,0:T(8,128)(2,1)}, u32[]{:S(2)}, u32[]{:S(2)}) collective-permute-start(bf16[4096,128]{1,0:T(8,128)(2,1)S(1)} %collective-permute-done.20.refs_0_), channel_id=1, source_target_pairs={{0,4},{4,0},{8,12},{12,8},{1,5},{5,1},{9,13},{13,9},{2,6},{6,2},{1... | collective-permute-start | bytes 3145736 | tf_op jit(solution)/shard_map/ppermute | solution.py:76
  199.0 32.0 %collective-permute-start.24 = (bf16[4096,128]{1,0:T(8,128)(2,1)S(1)}, bf16[4096,128]{1,0:T(8,128)(2,1)}, u32[]{:S(2)}, u32[]{:S(2)}) collective-permute-start(bf16[4096,128]{1,0:T(8,128)(2,1)S(1)} %collective-permute-done.20.refs_0_), channel_id=1, source_target_pairs={{0,16},{16,0},{1,17},{17,1},{2,18},{18,2},{3,19},{19,3},{4,20},{20... | collective-permute-start | bytes 3145736 | tf_op jit(solution)/shard_map/ppermute | solution.py:87
  199.6 31.4 %collective-permute-start.23 = (bf16[4096,128]{1,0:T(8,128)(2,1)}, bf16[4096,128]{1,0:T(8,128)(2,1)}, u32[]{:S(2)}, u32[]{:S(2)}) collective-permute-start(bf16[4096,128]{1,0:T(8,128)(2,1)} %get-tuple-element.102), channel_id=1, source_target_pairs={{0,8},{4,12},{8,0},{12,4},{1,9},{5,13},{9,1},{13,5},{2,10},{6,14},... | collective-permute-start | bytes 3145736 | tf_op jit(solution)/shard_map/ppermute | solution.py:72
  200.1 31.0 %collective-permute-start.26 = (bf16[560,1024]{1,0:T(8,128)(2,1)S(1)}, bf16[560,1024]{1,0:T(8,128)(2,1)}, u32[]{:S(2)}, u32[]{:S(2)}) collective-permute-start(bf16[560,1024]{1,0:T(8,128)(2,1)S(1)} %collective-permute-done.21.refs_1_), channel_id=1, source_target_pairs={{1,0},{2,1},{5,4},{6,5},{9,8},{10,9},{13,12},{14,13},{17,16},{18,1... | collective-permute-start | bytes 3440648 | tf_op jit(solution)/shard_map/ppermute | solution.py:91
  201.4 29.7 %collective-permute-start.27 = (bf16[560,1024]{1,0:T(8,128)(2,1)S(1)}, bf16[560,1024]{1,0:T(8,128)(2,1)}, u32[]{:S(2)}, u32[]{:S(2)}) collective-permute-start(bf16[560,1024]{1,0:T(8,128)(2,1)S(1)} %collective-permute-done.22.refs_4_), channel_id=1, source_target_pairs={{1,2},{2,3},{5,6},{6,7},{9,10},{10,11},{13,14},{14,15},{17,18},{18... | collective-permute-start | bytes 3440648 | tf_op jit(solution)/shard_map/ppermute | solution.py:95
  231.1 6.0 %collective-permute-start.28 = (bf16[4096,128]{1,0:T(8,128)(2,1)}, bf16[4096,128]{1,0:T(8,128)(2,1)S(1)}, u32[]{:S(2)}, u32[]{:S(2)}) collective-permute-start(bf16[4096,128]{1,0:T(8,128)(2,1)} %collective-permute-done.24.refs_1_), channel_id=1, source_target_pairs={{0,4},{4,0},{8,12},{12,8},{1,5},{5,1},{9,13},{13,9},{2,6},{6,2},{1... | collective-permute-start | bytes 3145736 | tf_op jit(solution)/shard_map/ppermute | solution.py:76
  231.1 41.2 %collective-permute-start.31 = (bf16[560,1024]{1,0:T(8,128)(2,1)}, bf16[560,1024]{1,0:T(8,128)(2,1)}, u32[]{:S(2)}, u32[]{:S(2)}) collective-permute-start(bf16[560,1024]{1,0:T(8,128)(2,1)} %collective-permute-done.26.refs_2_), channel_id=1, source_target_pairs={{1,0},{5,4},{9,8},{13,12},{17,16},{21,20},{25,24},{29,28}} | collective-permute-start | bytes 3440648 | tf_op jit(solution)/shard_map/ppermute | solution.py:91
  232.4 39.9 %collective-permute-start.32 = (bf16[560,1024]{1,0:T(8,128)(2,1)}, bf16[560,1024]{1,0:T(8,128)(2,1)}, u32[]{:S(2)}, u32[]{:S(2)}) collective-permute-start(bf16[560,1024]{1,0:T(8,128)(2,1)} %collective-permute-done.27.refs_5_), channel_id=1, source_target_pairs={{2,3},{6,7},{10,11},{14,15},{18,19},{22,23},{26,27},{30,31}} | collective-permute-start | bytes 3440648 | tf_op jit(solution)/shard_map/ppermute | solution.py:95
  234.1 25.9 %collective-permute-start.29 = (bf16[4096,128]{1,0:T(8,128)(2,1)}, bf16[4096,128]{1,0:T(8,128)(2,1)}, u32[]{:S(2)}, u32[]{:S(2)}) collective-permute-start(bf16[4096,128]{1,0:T(8,128)(2,1)} %get-tuple-element.111), channel_id=1, source_target_pairs={{0,8},{4,12},{8,0},{12,4},{1,9},{5,13},{9,1},{13,5},{2,10},{6,14},... | collective-permute-start | bytes 3145736 | tf_op jit(solution)/shard_map/ppermute | solution.py:72
  235.6 25.6 %collective-permute-start.30 = (bf16[4096,128]{1,0:T(8,128)(2,1)}, bf16[4096,128]{1,0:T(8,128)(2,1)}, u32[]{:S(2)}, u32[]{:S(2)}) collective-permute-start(bf16[4096,128]{1,0:T(8,128)(2,1)} %collective-permute-done.23.refs_0_.refs_4_), channel_id=1, source_target_pairs={{0,16},{16,0},{1,17},{17,1},{2,18},{18,2},{3,19},{19,3},{4,20},{20... | collective-permute-start | bytes 3145736 | tf_op jit(solution)/shard_map/ppermute | solution.py:87
  251.4 89.6 %reduce-scatter.8.cloned.1.call-start = ((), (), s32[]{:S(2)}) async-start(), calls=%async_computation.6 | async-start | bytes 1843200 | tf_op jit(solution)/shard_map/reduce_scatter | solution.py:378
  272.3 2.9 collective-permute-start.33
  275.2 2.9 collective-permute-start.34
  275.3 48.2 %collective-permute-start.35 = (bf16[4096,256]{1,0:T(8,128)(2,1)}, bf16[4096,256]{1,0:T(8,128)(2,1)}, u32[]{:S(2)}, u32[]{:S(2)}) collective-permute-start(bf16[4096,256]{1,0:T(8,128)(2,1)} %slice.32), channel_id=1, source_target_pairs={{0,8},{4,12},{8,0},{12,4},{1,9},{5,13},{9,1},{13,5},{2,10},{6,14},... | collective-permute-start | bytes 6291464 | tf_op jit(solution)/shard_map/ppermute | solution.py:72
  292.5 115.8 %reduce-scatter.10.cloned.1.call-start = ((), (), s32[]{:S(2)}) async-start(), calls=%async_computation.7 | async-start | bytes 1843200 | tf_op jit(solution)/shard_map/reduce_scatter | solution.py:378
  292.7 26.6 %collective-permute-start.36 = (bf16[4096,128]{1,0:T(8,128)(2,1)}, bf16[4096,128]{1,0:T(8,128)(2,1)}, u32[]{:S(2)}, u32[]{:S(2)}) collective-permute-start(bf16[4096,128]{1,0:T(8,128)(2,1)} %collective-permute-done.29.refs_0_.refs_8_), channel_id=1, source_target_pairs={{0,16},{16,0},{1,17},{17,1},{2,18},{18,2},{3,19},{19,3},{4,20},{20... | collective-permute-start | bytes 3145736 | tf_op jit(solution)/shard_map/ppermute | solution.py:87
  294.3 29.2 %collective-permute-start.37 = (bf16[4096,128]{1,0:T(8,128)(2,1)}, bf16[4096,128]{1,0:T(8,128)(2,1)}, u32[]{:S(2)}, u32[]{:S(2)}) collective-permute-start(bf16[4096,128]{1,0:T(8,128)(2,1)} %collective-permute-done.29.refs_0_.refs_8_), channel_id=1, source_target_pairs={{0,4},{4,0},{8,12},{12,8},{1,5},{5,1},{9,13},{13,9},{2,6},{6,2},{1... | collective-permute-start | bytes 3145736 | tf_op jit(solution)/shard_map/ppermute | solution.py:76
  323.6 2.9 collective-permute-start.38
  340.7 67.5 %reduce-scatter.12.cloned.1.call-start = ((), (), s32[]{:S(2)}) async-start(), calls=%async_computation.8 | async-start | bytes 1843200 | tf_op jit(solution)/shard_map/reduce_scatter | solution.py:378
  340.8 4.6 collective-permute-start.39
  358.7 133.4 %reduce-scatter.14.cloned.1.call-start = ((), (), s32[]{:S(2)}) async-start(), calls=%async_computation.9 | async-start | bytes 5734400 | tf_op jit(solution)/shard_map/reduce_scatter | solution.py:378
  (16 other events, 154.4 us)
Sparse Core Ops, SparseCore 0:
  251.5 40.1 reduce-scatter.5
  294.1 32.9 reduce-scatter.7
  340.9 32.0 reduce-scatter.9
  375.2 32.6 reduce-scatter.11
  410.1 82.0 reduce-scatter.13

commit v5 on v4

--- a/solution.py
+++ b/solution.py
@@ -11,7 +11,7 @@
 eps = 1e-05
 TILE = 1024
 SUB = 512
-LANES = 128
+LANES = 256
 BLOCK = 80
 VMEM_LIMIT = 58 * 1024 * 1024
 

time: 511 us -> 511 us (level)
  no operation moved by 1% of the time
where the time goes in v5:
time: 511 us; the launch traced here: 503 us
  waiting for transfers between devices  227 us (44%)
  Pallas kernels  187 us (37%)
  starting transfers between devices  44.9 us (9%)
  local copies, waits for them, and re-layouts  21.4 us (4%)
  between operations  14 us (3%)
  other arithmetic  8.1 us (2%)
    pallas_call x4, Pallas kernels, first(): pl.pallas_call(functools.partial(first_kernel, has_tail, len(toks), len(w...  107 us
    pallas_call x5, Pallas kernels, second(): pl.pallas_call(functools.partial(second_kernel, quarters, tuple((len(piec...  80.6 us
    reduce_scatter x5, waiting for transfers between devices, scatter(): return lax.psum_scatter(v, 'col', scatter_dimension=1, tiled=True)  80.2 us
    ppermute x6, waiting for transfers between devices, down(): return lax.ppermute(v, 'col', [(i, i - 1) for i in range(1, 5 - hop)])  50.1 us
    ppermute x7, waiting for transfers between devices, swap_x(): return lax.ppermute(v, 'row', [(i, i ^ 2) for i in range(4)])  41.6 us
    ppermute x6, waiting for transfers between devices, up(): return lax.ppermute(v, 'col', [(i, i + 1) for i in range(hop - 1, 3)])  33.7 us
    ppermute x6, starting transfers between devices, up(): return lax.ppermute(v, 'col', [(i, i + 1) for i in range(hop - 1, 3)])  16.2 us
    ppermute x14, waiting for transfers between devices, swap_core(): return lax.ppermute(v, 'row', [(i, i ^ 1) for i in range(4)])  13.2 us
  transfers between devices with their start and end apart: 45, of which 17 were waited for; matrix products, arithmetic and copies ran while one was open for 4% of the time, Pallas kernels for 37%

profile of v5, /device:TPU:0, one launch (start us, length us, event | category | flops | bytes accessed | tf_op | source)
XLA Modules:
  0.0 502.6 jit_solution(16473104882880476355)
XLA Ops:
  8.0 2.6 collective-permute-start.1
  10.6 2.3 constant_dynamic-slice_fusion.3
  12.9 7.0 %collective-permute-done.1 = bf16[40,1024]{1,0:T(8,128)(2,1)S(1)} collective-permute-done((bf16[40,1024]{1,0:T(8,128)(2,1)S(1)}, bf16[40,1024]{1,0:T(8,128)(2,1)S(1)}, u32[]{:S(2)}, u32[]{:S(2)}) %collective-permute-start.1) | collective-permute-done | bytes 81952 | tf_op jit(solution)/shard_map/ppermute | solution.py:28
  21.2 3.0 collective-permute-start.2
  24.2 3.6 collective-permute-start.5
  27.8 1.3 collective-permute-start.4
  29.1 33.7 %collective-permute-done.5.refs_4_ = bf16[800,1024]{1,0:T(8,128)(2,1)S(1)} collective-permute-done((bf16[800,1024]{1,0:T(8,128)(2,1)S(1)}, bf16[800,1024]{1,0:T(8,128)(2,1)S(1)}, u32[]{:S(2)}, u32[]{:S(2)}) %collective-permute-start.5) | collective-permute-done | bytes 1638432 | tf_op jit(solution)/shard_map/ppermute | solution.py:95
  62.8 4.2 collective-permute-done.4.refs_1_
  68.2 1.5 collective-permute-start.7
  71.0 1.8 collective-permute-start.11
  72.8 2.7 slice.31
  75.6 33.2 %collective-permute-done.10.refs_2_ = bf16[800,1024]{1,0:T(8,128)(2,1)} collective-permute-done((bf16[800,1024]{1,0:T(8,128)(2,1)S(1)}, bf16[800,1024]{1,0:T(8,128)(2,1)}, u32[]{:S(2)}, u32[]{:S(2)}) %collective-permute-start.10) | collective-permute-done | bytes 1638432 | tf_op jit(solution)/shard_map/ppermute | solution.py:91
  111.7 1.9 collective-permute-done.14.refs_15_.refs_9_
  116.3 1.9 collective-permute-start.17
  118.2 1.5 collective-permute-start.12
  119.7 3.0 slice.32
  122.7 3.6 constant_dynamic-slice_fusion
  126.3 28.8 %collective-permute-done.12.refs_13_.refs_7_ = bf16[192,4096]{1,0:T(8,128)(2,1)} collective-permute-done((bf16[192,4096]{1,0:T(8,128)(2,1)}, bf16[192,4096]{1,0:T(8,128)(2,1)}, u32[]{:S(2)}, u32[]{:S(2)}) %collective-permute-start.12) | collective-permute-done | bytes 1572896 | tf_op jit(solution)/shard_map/ppermute | solution.py:72
  155.2 1.4 collective-permute-done.16.refs_3_
  158.4 5.4 %collective-permute-start.22 = (bf16[560,1024]{1,0:T(8,128)(2,1)}, bf16[560,1024]{1,0:T(8,128)(2,1)S(1)}, u32[]{:S(2)}, u32[]{:S(2)}) collective-permute-start(bf16[560,1024]{1,0:T(8,128)(2,1)} %pad_maximum_fusion.2.refs_0_), channel_id=1, source_target_pairs={{0,1},{1,2},{2,3},{4,5},{5,6},{6,7},{8,9},{9,10},{10,11},{12,13},{... | collective-permute-start | bytes 3440648 | tf_op jit(solution)/shard_map/ppermute | solution.py:95
  163.8 1.3 collective-permute-start.21
  165.1 1.6 collective-permute-start.20
  166.7 32.2 %first.4 = (bf16[720,2048]{1,0:T(8,128)(2,1)}, bf16[80,2048]{1,0:T(8,128)(2,1)}, bf16[800,4096]{1,0:T(8,128)(2,1)}) custom-call(s32[3]{0:T(128)} %pad_add_fusion.place_ref, f32[4,1024]{1,0:T(4,128)} %reshape.3.gain_ref, bf16[800,1024]{1,0:T(8,128)(2,1)} %copy-done.6, bf16[800,1024]{1,0:T(8,128)(2,1)} %copy-done.18, ...), custom_call_target="tpu_custom_call" | custom-call | flops 13421772800 | bytes 16777216 | tf_op jit(solution)/shard_map/first/pallas_call | solution.py:255
  201.4 1.9 collective-permute-start.27
  203.3 27.6 %first.5 = (bf16[720,2048]{1,0:T(8,128)(2,1)}, bf16[80,2048]{1,0:T(8,128)(2,1)}) custom-call(s32[3]{0:T(128)} %pad_add_fusion.place_ref, f32[4,1024]{1,0:T(4,128)} %reshape.3.gain_ref, bf16[800,4096]{1,0:T(8,128)(2,1)} %get-tuple-element.100.refs_0_, bf16[1024,4096]{1,0:T(8,128)(2,1)} %refs_1_.3, bf16[1024,4096]{1,0:T(8,128)(2,1)} %collective-permute-done.3.refs_8_.refs_2_, ...), custom_call_target="tpu_custom_call" | custom-call | flops 13421772800 | bytes 16777216 | tf_op jit(solution)/shard_map/first/pallas_call | solution.py:255
  231.1 1.3 collective-permute-start.31
  232.4 1.7 collective-permute-start.32
  234.1 1.5 collective-permute-start.29
  235.6 1.5 collective-permute-start.30
  238.1 13.3 %second.5 = bf16[720,1024]{1,0:T(8,128)(2,1)} custom-call(s32[3]{0:T(128)} %pad_add_fusion.place_ref, bf16[720,2048]{1,0:T(8,128)(2,1)} %get-tuple-element.95.act_l, bf16[720,2048]{1,0:T(8,128)(2,1)} %get-tuple-element.135.act_r, bf16[4096,1024]{1,0:T(8,128)(2,1)} %own.9, bf16[4096,1024]{1,0:T(8,128)(2,1)} %collective-permute-done.8.sib, ...), custom_call_target="tpu_custom_call" | custom-call | flops 6039797760 | bytes 8388608 | tf_op jit(solution)/shard_map/second/pallas_call | solution.py:356
  251.4 8.5 %collective-permute-done.29.refs_0_.refs_8_ = bf16[4096,128]{1,0:T(8,128)(2,1)} collective-permute-done((bf16[4096,128]{1,0:T(8,128)(2,1)}, bf16[4096,128]{1,0:T(8,128)(2,1)}, u32[]{:S(2)}, u32[]{:S(2)}) %collective-permute-start.29) | collective-permute-done | bytes 1048608 | tf_op jit(solution)/shard_map/ppermute | solution.py:72
  261.2 11.1 %collective-permute-done.31.refs_3_ = bf16[560,1024]{1,0:T(8,128)(2,1)} collective-permute-done((bf16[560,1024]{1,0:T(8,128)(2,1)}, bf16[560,1024]{1,0:T(8,128)(2,1)}, u32[]{:S(2)}, u32[]{:S(2)}) %collective-permute-start.31) | collective-permute-done | bytes 1146912 | tf_op jit(solution)/shard_map/ppermute | solution.py:91
  272.3 2.9 collective-permute-done.33.refs_3_.refs_7_
  275.3 1.5 collective-permute-start.35
  279.0 13.4 %second.6 = bf16[720,1024]{1,0:T(8,128)(2,1)} custom-call(s32[3]{0:T(128)} %pad_add_fusion.place_ref, bf16[720,2048]{1,0:T(8,128)(2,1)} %get-tuple-element.95.act_l, bf16[720,2048]{1,0:T(8,128)(2,1)} %get-tuple-element.135.act_r, bf16[4096,1024]{1,0:T(8,128)(2,1)} %own.9, bf16[4096,1024]{1,0:T(8,128)(2,1)} %collective-permute-done.8.sib, ...), custom_call_target="tpu_custom_call" | custom-call | flops 6039797760 | bytes 8388608 | tf_op jit(solution)/shard_map/second/pallas_call | solution.py:356
  292.7 1.6 collective-permute-start.36
  294.3 25.0 %first.6 = (bf16[560,2048]{1,0:T(8,128)(2,1)}, bf16[560,4096]{1,0:T(8,128)(2,1)}) custom-call(s32[3]{0:T(128)} %pad_add_fusion.place_ref, f32[4,1024]{1,0:T(4,128)} %reshape.3.gain_ref, bf16[560,1024]{1,0:T(8,128)(2,1)} %pad_maximum_fusion.2.refs_0_, bf16[560,1024]{1,0:T(8,128)(2,1)} %copy-done.8, bf16[560,1024]{1,0:T(8,128)(2,1)} %collective-permute-done.26.refs_2_, ...), custom_call_target="tpu_custom_call" | custom-call | flops 9395240960 | bytes 16777216 | tf_op jit(solution)/shard_map/first/pallas_call | solution.py:255
  319.3 4.2 collective-permute-done.35.refs_0_.refs_12_
  323.5 2.9 collective-permute-done.38.refs_3_.refs_11_
  327.4 13.3 %second.7 = bf16[720,1024]{1,0:T(8,128)(2,1)} custom-call(s32[3]{0:T(128)} %pad_add_fusion.place_ref, bf16[720,2048]{1,0:T(8,128)(2,1)} %get-tuple-element.95.act_l, bf16[720,2048]{1,0:T(8,128)(2,1)} %get-tuple-element.135.act_r, bf16[4096,1024]{1,0:T(8,128)(2,1)} %own.9, bf16[4096,1024]{1,0:T(8,128)(2,1)} %collective-permute-done.8.sib, ...), custom_call_target="tpu_custom_call" | custom-call | flops 6039797760 | bytes 8388608 | tf_op jit(solution)/shard_map/second/pallas_call | solution.py:356
  341.0 4.4 collective-permute-done.39.refs_1_.refs_13_
  345.3 13.3 %second.8 = bf16[720,1024]{1,0:T(8,128)(2,1)} custom-call(s32[3]{0:T(128)} %pad_add_fusion.place_ref, bf16[720,2048]{1,0:T(8,128)(2,1)} %get-tuple-element.95.act_l, bf16[720,2048]{1,0:T(8,128)(2,1)} %get-tuple-element.135.act_r, bf16[4096,1024]{1,0:T(8,128)(2,1)} %own.9, bf16[4096,1024]{1,0:T(8,128)(2,1)} %collective-permute-done.8.sib, ...), custom_call_target="tpu_custom_call" | custom-call | flops 6039797760 | bytes 8388608 | tf_op jit(solution)/shard_map/second/pallas_call | solution.py:356
  359.0 21.8 %first.7.act_r = bf16[560,2048]{1,0:T(8,128)(2,1)} custom-call(s32[3]{0:T(128)} %pad_add_fusion.place_ref, f32[4,1024]{1,0:T(4,128)} %reshape.3.gain_ref, bf16[560,4096]{1,0:T(8,128)(2,1)} %get-tuple-element.139.refs_0_, bf16[1024,4096]{1,0:T(8,128)(2,1)} %refs_1_.3, bf16[1024,4096]{1,0:T(8,128)(2,1)} %collective-permute-done.3.refs_8_.refs_2_, ...), custom_call_target="tpu_custom_call" | custom-call | flops 9395240960 | bytes 16777216 | tf_op jit(solution)/shard_map/first/pallas_call | solution.py:255
  380.7 27.4 %second.9 = bf16[560,4096]{1,0:T(8,128)(2,1)} custom-call(s32[3]{0:T(128)} %pad_add_fusion.place_ref, bf16[560,2048]{1,0:T(8,128)(2,1)} %get-tuple-element.137.act_l, bf16[560,2048]{1,0:T(8,128)(2,1)} %first.7.act_r, bf16[4096,1024]{1,0:T(8,128)(2,1)} %own.9, bf16[4096,1024]{1,0:T(8,128)(2,1)} %collective-permute-done.8.sib, bf16[4096,128]{1,0:T(8,128)(2,1)} %copy-done.9, ...), custom_call_target="tpu_custom_call" | custom-call | flops 18790481920 | bytes 33554432 | tf_op jit(solution)/shard_map/second/pallas_call | solution.py:356
  409.2 2.7 add_convert_fusion
  411.9 80.2 %reduce-scatter.14.cloned.1.call-done = bf16[560,1024]{1,0:T(8,128)(2,1)} async-done(((bf16[560,4096]{1,0:T(8,128)(2,1)}), bf16[560,1024]{1,0:T(8,128)(2,1)}) %reduce-scatter.14.cloned.1.call-update) | async-done | bytes 1146896 | tf_op jit(solution)/shard_map/reduce_scatter | solution.py:378
  492.1 1.8 add_convert_fusion.1
  493.9 1.7 pad_maximum_fusion
  (106 shorter events, 22.6 us)
Async XLA Ops:
  6.5 317.0 %reduce-scatter.6.cloned.1.call-start = ((), (), s32[]{:S(2)}) async-start(), calls=%async_computation.5 | async-start | bytes 1843200 | tf_op jit(solution)/shard_map/reduce_scatter | solution.py:378
  6.5 60.4 %collective-permute-start.3 = (bf16[1024,4096]{1,0:T(8,128)(2,1)}, bf16[1024,4096]{1,0:T(8,128)(2,1)}, u32[]{:S(2)}, u32[]{:S(2)}) collective-permute-start(bf16[1024,4096]{1,0:T(8,128)(2,1)} %refs_1_.3), channel_id=1, source_target_pairs={{0,4},{4,0},{8,12},{12,8},{1,5},{5,1},{9,13},{13,9},{2,6},{6,2},{1... | collective-permute-start | bytes 25165832 | tf_op jit(solution)/shard_map/ppermute | solution.py:76
  7.0 60.0 %collective-permute-start.8 = (bf16[4096,1024]{1,0:T(8,128)(2,1)}, bf16[4096,1024]{1,0:T(8,128)(2,1)}, u32[]{:S(2)}, u32[]{:S(2)}) collective-permute-start(bf16[4096,1024]{1,0:T(8,128)(2,1)} %own.9), channel_id=1, source_target_pairs={{0,4},{4,0},{8,12},{12,8},{1,5},{5,1},{9,13},{13,9},{2,6},{6,2},{1... | collective-permute-start | bytes 25165832 | tf_op jit(solution)/shard_map/ppermute | solution.py:76
  8.0 11.9 %collective-permute-start.1 = (bf16[40,1024]{1,0:T(8,128)(2,1)S(1)}, bf16[40,1024]{1,0:T(8,128)(2,1)S(1)}, u32[]{:S(2)}, u32[]{:S(2)}) collective-permute-start(bf16[40,1024]{1,0:T(8,128)(2,1)S(1)} %get-tuple-element.146), channel_id=1, source_target_pairs={{4,0},{8,4},{12,8},{0,12},{5,1},{9,5},{13,9},{1,13},{6,2},{10,6},{... | collective-permute-start | bytes 245768 | tf_op jit(solution)/shard_map/ppermute | solution.py:28
  10.6 10.5 %collective-permute-start = (bf16[40,1024]{1,0:T(8,128)(2,1)S(1)}, bf16[40,1024]{1,0:T(8,128)(2,1)S(1)}, u32[]{:S(2)}, u32[]{:S(2)}) collective-permute-start(bf16[40,1024]{1,0:T(8,128)(2,1)S(1)} %get-tuple-element.147), channel_id=1, source_target_pairs={{0,4},{4,8},{8,12},{12,0},{1,5},{5,9},{9,13},{13,1},{2,6},{6,10},{... | collective-permute-start | bytes 245768 | tf_op jit(solution)/shard_map/ppermute | solution.py:26
  21.2 45.8 %copy-start.6 = (bf16[800,1024]{1,0:T(8,128)(2,1)}, bf16[800,1024]{1,0:T(8,128)(2,1)S(1)}, u32[]{:S(2)}) copy-start(bf16[800,1024]{1,0:T(8,128)(2,1)S(1)} %pad_maximum_fusion.1.refs_0_) | copy-start | bytes 4915204
  21.2 45.8 %collective-permute-start.2 = (bf16[208,4096]{1,0:T(8,128)(2,1)S(1)}, bf16[208,4096]{1,0:T(8,128)(2,1)S(1)}, u32[]{:S(2)}, u32[]{:S(2)}) collective-permute-start(bf16[208,4096]{1,0:T(8,128)(2,1)S(1)} %get-tuple-element.74), channel_id=1, source_target_pairs={{0,8},{4,12},{8,0},{12,4},{1,9},{5,13},{9,1},{13,5},{2,10},{6,14},... | collective-permute-start | bytes 5111816 | tf_op jit(solution)/shard_map/ppermute | solution.py:72
  24.2 38.5 %collective-permute-start.5 = (bf16[800,1024]{1,0:T(8,128)(2,1)S(1)}, bf16[800,1024]{1,0:T(8,128)(2,1)S(1)}, u32[]{:S(2)}, u32[]{:S(2)}) collective-permute-start(bf16[800,1024]{1,0:T(8,128)(2,1)S(1)} %pad_maximum_fusion.1.refs_0_), channel_id=1, source_target_pairs={{0,1},{1,2},{2,3},{4,5},{5,6},{6,7},{8,9},{9,10},{10,11},{12,13},{... | collective-permute-start | bytes 4915208 | tf_op jit(solution)/shard_map/ppermute | solution.py:95
  27.8 39.2 %collective-permute-start.4 = (bf16[800,1024]{1,0:T(8,128)(2,1)S(1)}, bf16[800,1024]{1,0:T(8,128)(2,1)S(1)}, u32[]{:S(2)}, u32[]{:S(2)}) collective-permute-start(bf16[800,1024]{1,0:T(8,128)(2,1)S(1)} %pad_maximum_fusion.1.refs_0_), channel_id=1, source_target_pairs={{1,0},{2,1},{3,2},{5,4},{6,5},{7,6},{9,8},{10,9},{11,10},{13,12},{... | collective-permute-start | bytes 4915208 | tf_op jit(solution)/shard_map/ppermute | solution.py:91
  62.8 52.2 %copy-start.17 = (bf16[800,1024]{1,0:T(8,128)(2,1)}, bf16[800,1024]{1,0:T(8,128)(2,1)S(1)}, u32[]{:S(2)}) copy-start(bf16[800,1024]{1,0:T(8,128)(2,1)S(1)} %collective-permute-done.5.refs_4_) | copy-start | bytes 4915204
  67.0 49.3 %copy-start.18 = (bf16[800,1024]{1,0:T(8,128)(2,1)}, bf16[800,1024]{1,0:T(8,128)(2,1)S(1)}, u32[]{:S(2)}) copy-start(bf16[800,1024]{1,0:T(8,128)(2,1)S(1)} %collective-permute-done.4.refs_1_) | copy-start | bytes 4915204
  67.0 41.8 %collective-permute-start.9 = (bf16[208,4096]{1,0:T(8,128)(2,1)S(1)}, bf16[208,4096]{1,0:T(8,128)(2,1)S(1)}, u32[]{:S(2)}, u32[]{:S(2)}) collective-permute-start(bf16[208,4096]{1,0:T(8,128)(2,1)S(1)} %collective-permute-done.2.refs_9_.refs_3_), channel_id=1, source_target_pairs={{0,4},{4,0},{8,12},{12,8},{1,5},{5,1},{9,13},{13,9},{2,6},{6,2},{1... | collective-permute-start | bytes 5111816 | tf_op jit(solution)/shard_map/ppermute | solution.py:76
  67.1 41.7 %collective-permute-start.6 = (bf16[208,4096]{1,0:T(8,128)(2,1)S(1)}, bf16[208,4096]{1,0:T(8,128)(2,1)}, u32[]{:S(2)}, u32[]{:S(2)}) collective-permute-start(bf16[208,4096]{1,0:T(8,128)(2,1)S(1)} %get-tuple-element.76), channel_id=1, source_target_pairs={{0,8},{4,12},{8,0},{12,4},{1,9},{5,13},{9,1},{13,5},{2,10},{6,14},... | collective-permute-start | bytes 5111816 | tf_op jit(solution)/shard_map/ppermute | solution.py:72
  68.2 40.6 %collective-permute-start.7 = (bf16[208,4096]{1,0:T(8,128)(2,1)S(1)}, bf16[208,4096]{1,0:T(8,128)(2,1)S(1)}, u32[]{:S(2)}, u32[]{:S(2)}) collective-permute-start(bf16[208,4096]{1,0:T(8,128)(2,1)S(1)} %collective-permute-done.2.refs_9_.refs_3_), channel_id=1, source_target_pairs={{0,16},{16,0},{1,17},{17,1},{2,18},{18,2},{3,19},{19,3},{4,20},{20... | collective-permute-start | bytes 5111816 | tf_op jit(solution)/shard_map/ppermute | solution.py:87
  69.7 39.1 %collective-permute-start.10 = (bf16[800,1024]{1,0:T(8,128)(2,1)S(1)}, bf16[800,1024]{1,0:T(8,128)(2,1)}, u32[]{:S(2)}, u32[]{:S(2)}) collective-permute-start(bf16[800,1024]{1,0:T(8,128)(2,1)S(1)} %collective-permute-done.4.refs_1_), channel_id=1, source_target_pairs={{1,0},{2,1},{5,4},{6,5},{9,8},{10,9},{13,12},{14,13},{17,16},{18,1... | collective-permute-start | bytes 4915208 | tf_op jit(solution)/shard_map/ppermute | solution.py:91
  71.0 37.8 %collective-permute-start.11 = (bf16[800,1024]{1,0:T(8,128)(2,1)S(1)}, bf16[800,1024]{1,0:T(8,128)(2,1)}, u32[]{:S(2)}, u32[]{:S(2)}) collective-permute-start(bf16[800,1024]{1,0:T(8,128)(2,1)S(1)} %collective-permute-done.5.refs_4_), channel_id=1, source_target_pairs={{1,2},{2,3},{5,6},{6,7},{9,10},{10,11},{13,14},{14,15},{17,18},{18... | collective-permute-start | bytes 4915208 | tf_op jit(solution)/shard_map/ppermute | solution.py:95
  110.0 3.6 collective-permute-start.14
  111.2 45.4 %collective-permute-start.13 = (bf16[208,4096]{1,0:T(8,128)(2,1)}, bf16[208,4096]{1,0:T(8,128)(2,1)}, u32[]{:S(2)}, u32[]{:S(2)}) collective-permute-start(bf16[208,4096]{1,0:T(8,128)(2,1)} %collective-permute-done.6.refs_11_.refs_5_), channel_id=1, source_target_pairs={{0,16},{16,0},{1,17},{17,1},{2,18},{18,2},{3,19},{19,3},{4,20},{20... | collective-permute-start | bytes 5111816 | tf_op jit(solution)/shard_map/ppermute | solution.py:87
  114.9 41.8 %collective-permute-start.15 = (bf16[208,4096]{1,0:T(8,128)(2,1)}, bf16[208,4096]{1,0:T(8,128)(2,1)}, u32[]{:S(2)}, u32[]{:S(2)}) collective-permute-start(bf16[208,4096]{1,0:T(8,128)(2,1)} %collective-permute-done.6.refs_11_.refs_5_), channel_id=1, source_target_pairs={{0,4},{4,0},{8,12},{12,8},{1,5},{5,1},{9,13},{13,9},{2,6},{6,2},{1... | collective-permute-start | bytes 5111816 | tf_op jit(solution)/shard_map/ppermute | solution.py:76
  115.0 41.6 %collective-permute-start.16 = (bf16[800,1024]{1,0:T(8,128)(2,1)}, bf16[800,1024]{1,0:T(8,128)(2,1)}, u32[]{:S(2)}, u32[]{:S(2)}) collective-permute-start(bf16[800,1024]{1,0:T(8,128)(2,1)} %collective-permute-done.10.refs_2_), channel_id=1, source_target_pairs={{1,0},{5,4},{9,8},{13,12},{17,16},{21,20},{25,24},{29,28}} | collective-permute-start | bytes 4915208 | tf_op jit(solution)/shard_map/ppermute | solution.py:91
  116.3 40.3 %collective-permute-start.17 = (bf16[800,1024]{1,0:T(8,128)(2,1)}, bf16[800,1024]{1,0:T(8,128)(2,1)}, u32[]{:S(2)}, u32[]{:S(2)}) collective-permute-start(bf16[800,1024]{1,0:T(8,128)(2,1)} %collective-permute-done.11.refs_5_), channel_id=1, source_target_pairs={{2,3},{6,7},{10,11},{14,15},{18,19},{22,23},{26,27},{30,31}} | collective-permute-start | bytes 4915208 | tf_op jit(solution)/shard_map/ppermute | solution.py:95
  118.2 37.0 %collective-permute-start.12 = (bf16[192,4096]{1,0:T(8,128)(2,1)}, bf16[192,4096]{1,0:T(8,128)(2,1)}, u32[]{:S(2)}, u32[]{:S(2)}) collective-permute-start(bf16[192,4096]{1,0:T(8,128)(2,1)} %slice.31), channel_id=1, source_target_pairs={{0,8},{4,12},{8,0},{12,4},{1,9},{5,13},{9,1},{13,5},{2,10},{6,14},... | collective-permute-start | bytes 4718600 | tf_op jit(solution)/shard_map/ppermute | solution.py:72
  156.6 10.0 %collective-permute-start.18 = (bf16[208,4096]{1,0:T(8,128)(2,1)}, bf16[208,4096]{1,0:T(8,128)(2,1)}, u32[]{:S(2)}, u32[]{:S(2)}) collective-permute-start(bf16[208,4096]{1,0:T(8,128)(2,1)} %collective-permute-done.13.refs_12_.refs_6_), channel_id=1, source_target_pairs={{0,4},{4,0},{8,12},{12,8},{1,5},{5,1},{9,13},{13,9},{2,6},{6,2},{1... | collective-permute-start | bytes 5111816 | tf_op jit(solution)/shard_map/ppermute | solution.py:76
  156.7 9.9 %collective-permute-start.19 = (bf16[192,4096]{1,0:T(8,128)(2,1)}, bf16[192,4096]{1,0:T(8,128)(2,1)}, u32[]{:S(2)}, u32[]{:S(2)}) collective-permute-start(bf16[192,4096]{1,0:T(8,128)(2,1)} %collective-permute-done.12.refs_13_.refs_7_), channel_id=1, source_target_pairs={{0,4},{4,0},{8,12},{12,8},{1,5},{5,1},{9,13},{13,9},{2,6},{6,2},{1... | collective-permute-start | bytes 4718600 | tf_op jit(solution)/shard_map/ppermute | solution.py:76
  158.4 40.5 %collective-permute-start.22 = (bf16[560,1024]{1,0:T(8,128)(2,1)}, bf16[560,1024]{1,0:T(8,128)(2,1)S(1)}, u32[]{:S(2)}, u32[]{:S(2)}) collective-permute-start(bf16[560,1024]{1,0:T(8,128)(2,1)} %pad_maximum_fusion.2.refs_0_), channel_id=1, source_target_pairs={{0,1},{1,2},{2,3},{4,5},{5,6},{6,7},{8,9},{9,10},{10,11},{12,13},{... | collective-permute-start | bytes 3440648 | tf_op jit(solution)/shard_map/ppermute | solution.py:95
  163.8 35.1 %collective-permute-start.21 = (bf16[560,1024]{1,0:T(8,128)(2,1)}, bf16[560,1024]{1,0:T(8,128)(2,1)S(1)}, u32[]{:S(2)}, u32[]{:S(2)}) collective-permute-start(bf16[560,1024]{1,0:T(8,128)(2,1)} %pad_maximum_fusion.2.refs_0_), channel_id=1, source_target_pairs={{1,0},{2,1},{3,2},{5,4},{6,5},{7,6},{9,8},{10,9},{11,10},{13,12},{... | collective-permute-start | bytes 3440648 | tf_op jit(solution)/shard_map/ppermute | solution.py:91
  165.1 33.8 %collective-permute-start.20 = (bf16[4096,128]{1,0:T(8,128)(2,1)}, bf16[4096,128]{1,0:T(8,128)(2,1)S(1)}, u32[]{:S(2)}, u32[]{:S(2)}) collective-permute-start(bf16[4096,128]{1,0:T(8,128)(2,1)} %get-tuple-element.97), channel_id=1, source_target_pairs={{0,8},{4,12},{8,0},{12,4},{1,9},{5,13},{9,1},{13,5},{2,10},{6,14},... | collective-permute-start | bytes 3145736 | tf_op jit(solution)/shard_map/ppermute | solution.py:72
  198.9 32.0 %collective-permute-start.25 = (bf16[4096,128]{1,0:T(8,128)(2,1)S(1)}, bf16[4096,128]{1,0:T(8,128)(2,1)}, u32[]{:S(2)}, u32[]{:S(2)}) collective-permute-start(bf16[4096,128]{1,0:T(8,128)(2,1)S(1)} %collective-permute-done.20.refs_0_), channel_id=1, source_target_pairs={{0,4},{4,0},{8,12},{12,8},{1,5},{5,1},{9,13},{13,9},{2,6},{6,2},{1... | collective-permute-start | bytes 3145736 | tf_op jit(solution)/shard_map/ppermute | solution.py:76
  199.0 31.9 %collective-permute-start.24 = (bf16[4096,128]{1,0:T(8,128)(2,1)S(1)}, bf16[4096,128]{1,0:T(8,128)(2,1)}, u32[]{:S(2)}, u32[]{:S(2)}) collective-permute-start(bf16[4096,128]{1,0:T(8,128)(2,1)S(1)} %collective-permute-done.20.refs_0_), channel_id=1, source_target_pairs={{0,16},{16,0},{1,17},{17,1},{2,18},{18,2},{3,19},{19,3},{4,20},{20... | collective-permute-start | bytes 3145736 | tf_op jit(solution)/shard_map/ppermute | solution.py:87
  199.6 31.3 %collective-permute-start.23 = (bf16[4096,128]{1,0:T(8,128)(2,1)}, bf16[4096,128]{1,0:T(8,128)(2,1)}, u32[]{:S(2)}, u32[]{:S(2)}) collective-permute-start(bf16[4096,128]{1,0:T(8,128)(2,1)} %get-tuple-element.102), channel_id=1, source_target_pairs={{0,8},{4,12},{8,0},{12,4},{1,9},{5,13},{9,1},{13,5},{2,10},{6,14},... | collective-permute-start | bytes 3145736 | tf_op jit(solution)/shard_map/ppermute | solution.py:72
  200.1 31.0 %collective-permute-start.26 = (bf16[560,1024]{1,0:T(8,128)(2,1)S(1)}, bf16[560,1024]{1,0:T(8,128)(2,1)}, u32[]{:S(2)}, u32[]{:S(2)}) collective-permute-start(bf16[560,1024]{1,0:T(8,128)(2,1)S(1)} %collective-permute-done.21.refs_1_), channel_id=1, source_target_pairs={{1,0},{2,1},{5,4},{6,5},{9,8},{10,9},{13,12},{14,13},{17,16},{18,1... | collective-permute-start | bytes 3440648 | tf_op jit(solution)/shard_map/ppermute | solution.py:91
  201.4 29.7 %collective-permute-start.27 = (bf16[560,1024]{1,0:T(8,128)(2,1)S(1)}, bf16[560,1024]{1,0:T(8,128)(2,1)}, u32[]{:S(2)}, u32[]{:S(2)}) collective-permute-start(bf16[560,1024]{1,0:T(8,128)(2,1)S(1)} %collective-permute-done.22.refs_4_), channel_id=1, source_target_pairs={{1,2},{2,3},{5,6},{6,7},{9,10},{10,11},{13,14},{14,15},{17,18},{18... | collective-permute-start | bytes 3440648 | tf_op jit(solution)/shard_map/ppermute | solution.py:95
  231.1 6.0 %collective-permute-start.28 = (bf16[4096,128]{1,0:T(8,128)(2,1)}, bf16[4096,128]{1,0:T(8,128)(2,1)S(1)}, u32[]{:S(2)}, u32[]{:S(2)}) collective-permute-start(bf16[4096,128]{1,0:T(8,128)(2,1)} %collective-permute-done.24.refs_1_), channel_id=1, source_target_pairs={{0,4},{4,0},{8,12},{12,8},{1,5},{5,1},{9,13},{13,9},{2,6},{6,2},{1... | collective-permute-start | bytes 3145736 | tf_op jit(solution)/shard_map/ppermute | solution.py:76
  231.1 41.2 %collective-permute-start.31 = (bf16[560,1024]{1,0:T(8,128)(2,1)}, bf16[560,1024]{1,0:T(8,128)(2,1)}, u32[]{:S(2)}, u32[]{:S(2)}) collective-permute-start(bf16[560,1024]{1,0:T(8,128)(2,1)} %collective-permute-done.26.refs_2_), channel_id=1, source_target_pairs={{1,0},{5,4},{9,8},{13,12},{17,16},{21,20},{25,24},{29,28}} | collective-permute-start | bytes 3440648 | tf_op jit(solution)/shard_map/ppermute | solution.py:91
  232.4 39.9 %collective-permute-start.32 = (bf16[560,1024]{1,0:T(8,128)(2,1)}, bf16[560,1024]{1,0:T(8,128)(2,1)}, u32[]{:S(2)}, u32[]{:S(2)}) collective-permute-start(bf16[560,1024]{1,0:T(8,128)(2,1)} %collective-permute-done.27.refs_5_), channel_id=1, source_target_pairs={{2,3},{6,7},{10,11},{14,15},{18,19},{22,23},{26,27},{30,31}} | collective-permute-start | bytes 3440648 | tf_op jit(solution)/shard_map/ppermute | solution.py:95
  234.1 25.9 %collective-permute-start.29 = (bf16[4096,128]{1,0:T(8,128)(2,1)}, bf16[4096,128]{1,0:T(8,128)(2,1)}, u32[]{:S(2)}, u32[]{:S(2)}) collective-permute-start(bf16[4096,128]{1,0:T(8,128)(2,1)} %get-tuple-element.111), channel_id=1, source_target_pairs={{0,8},{4,12},{8,0},{12,4},{1,9},{5,13},{9,1},{13,5},{2,10},{6,14},... | collective-permute-start | bytes 3145736 | tf_op jit(solution)/shard_map/ppermute | solution.py:72
  235.6 25.6 %collective-permute-start.30 = (bf16[4096,128]{1,0:T(8,128)(2,1)}, bf16[4096,128]{1,0:T(8,128)(2,1)}, u32[]{:S(2)}, u32[]{:S(2)}) collective-permute-start(bf16[4096,128]{1,0:T(8,128)(2,1)} %collective-permute-done.23.refs_0_.refs_4_), channel_id=1, source_target_pairs={{0,16},{16,0},{1,17},{17,1},{2,18},{18,2},{3,19},{19,3},{4,20},{20... | collective-permute-start | bytes 3145736 | tf_op jit(solution)/shard_map/ppermute | solution.py:87
  251.4 89.6 %reduce-scatter.8.cloned.1.call-start = ((), (), s32[]{:S(2)}) async-start(), calls=%async_computation.6 | async-start | bytes 1843200 | tf_op jit(solution)/shard_map/reduce_scatter | solution.py:378
  272.3 2.9 collective-permute-start.33
  275.2 2.9 collective-permute-start.34
  275.3 48.2 %collective-permute-start.35 = (bf16[4096,256]{1,0:T(8,128)(2,1)}, bf16[4096,256]{1,0:T(8,128)(2,1)}, u32[]{:S(2)}, u32[]{:S(2)}) collective-permute-start(bf16[4096,256]{1,0:T(8,128)(2,1)} %slice.32), channel_id=1, source_target_pairs={{0,8},{4,12},{8,0},{12,4},{1,9},{5,13},{9,1},{13,5},{2,10},{6,14},... | collective-permute-start | bytes 6291464 | tf_op jit(solution)/shard_map/ppermute | solution.py:72
  292.4 115.7 %reduce-scatter.10.cloned.1.call-start = ((), (), s32[]{:S(2)}) async-start(), calls=%async_computation.7 | async-start | bytes 1843200 | tf_op jit(solution)/shard_map/reduce_scatter | solution.py:378
  292.7 26.6 %collective-permute-start.36 = (bf16[4096,128]{1,0:T(8,128)(2,1)}, bf16[4096,128]{1,0:T(8,128)(2,1)}, u32[]{:S(2)}, u32[]{:S(2)}) collective-permute-start(bf16[4096,128]{1,0:T(8,128)(2,1)} %collective-permute-done.29.refs_0_.refs_8_), channel_id=1, source_target_pairs={{0,16},{16,0},{1,17},{17,1},{2,18},{18,2},{3,19},{19,3},{4,20},{20... | collective-permute-start | bytes 3145736 | tf_op jit(solution)/shard_map/ppermute | solution.py:87
  294.3 29.2 %collective-permute-start.37 = (bf16[4096,128]{1,0:T(8,128)(2,1)}, bf16[4096,128]{1,0:T(8,128)(2,1)}, u32[]{:S(2)}, u32[]{:S(2)}) collective-permute-start(bf16[4096,128]{1,0:T(8,128)(2,1)} %collective-permute-done.29.refs_0_.refs_8_), channel_id=1, source_target_pairs={{0,4},{4,0},{8,12},{12,8},{1,5},{5,1},{9,13},{13,9},{2,6},{6,2},{1... | collective-permute-start | bytes 3145736 | tf_op jit(solution)/shard_map/ppermute | solution.py:76
  323.5 2.9 collective-permute-start.38
  340.7 67.5 %reduce-scatter.12.cloned.1.call-start = ((), (), s32[]{:S(2)}) async-start(), calls=%async_computation.8 | async-start | bytes 1843200 | tf_op jit(solution)/shard_map/reduce_scatter | solution.py:378
  340.8 4.6 collective-permute-start.39
  358.7 133.4 %reduce-scatter.14.cloned.1.call-start = ((), (), s32[]{:S(2)}) async-start(), calls=%async_computation.9 | async-start | bytes 5734400 | tf_op jit(solution)/shard_map/reduce_scatter | solution.py:378
  (16 other events, 154.4 us)
Sparse Core Ops, SparseCore 0:
  251.5 40.1 reduce-scatter.5
  294.1 32.9 reduce-scatter.7
  340.8 32.0 reduce-scatter.9
  375.2 32.6 reduce-scatter.11
  410.1 81.9 reduce-scatter.13
